TPU v7x, 768 devices: a whole 4x8x12 slice. The times are simulated.
768 devices in a mesh: pair: 48 (over x, z), orb: 16 (over y, core).
Axes of the slice: x: 4, y: 8, z: 12, core: 2. Of those that a mesh axis runs over, the one named last changes fastest.
Arguments:
- amplitudes: float32 [144, 64, 64, 640], P('pair', None, 'orb'), may hold values from -3 to 3
- integrals: float32 [640, 64, 768], P('orb', None, 'pair'), may hold values from -0.03125 to 0.03125
- a_irrep: int32 [144], P('pair'), may hold values from 0 to 7
- b_irrep: int32 [12], replicated, may hold values from 0 to 7
- occ_irrep: int32 [64], replicated, may hold values from 0 to 7
Outputs:
- cycle_residual: float32 [144, 64, 768], P('pair', 'orb')
All inputs are finite; a program needn't handle non-finite values.
Results may differ from a plain program's by a relative error of at most 0.000082.
Values sent between devices are 32-bit elements; how exact they have to be, the bound alone decides.
No kernel may reach another device: no remote copies, remote signals or barrier semaphores. Data moves between devices by JAX's collectives and lax.ppermute only.
A program may use at most 64 MiB of HBM per device.

v0:
```python
import jax
import jax.numpy as jnp
from jax import lax
from jax.sharding import PartitionSpec as P


def spin_rows(cycle_block):
    mixed = 2.0 * cycle_block - jnp.transpose(cycle_block, (0, 2, 1, 3))
    return mixed.reshape(mixed.shape[0] * mixed.shape[1], mixed.shape[2] * mixed.shape[3])


def ordered_columns(portion):
    swapped = jnp.transpose(portion, (1, 0, 2))
    return swapped.reshape(-1, swapped.shape[2])


def body(amplitudes, integrals, a_irrep, b_irrep, occ_irrep):
    occupied = amplitudes.shape[1]
    cycle_block = lax.all_to_all(amplitudes, "orb", split_axis=3, concat_axis=2, tiled=True)
    spin = spin_rows(cycle_block)
    partial_sum = jnp.dot(
        spin,
        ordered_columns(lax.all_gather(integrals, "pair", axis=2, tiled=True)),
        precision=lax.Precision.HIGHEST,
        preferred_element_type=jnp.float32,
    )
    partial_sum = partial_sum.reshape(cycle_block.shape[0], occupied, -1)
    shares = lax.psum_scatter(partial_sum, "orb", scatter_dimension=1, tiled=True)
    local_rows = shares.shape[1]
    row_offset = lax.axis_index("orb") * local_rows
    local_occ = lax.dynamic_slice_in_dim(occ_irrep, row_offset, local_rows)
    col_sym = jnp.bitwise_xor(b_irrep[:, None], occ_irrep[None, :]).reshape(-1)
    symmetry = jnp.bitwise_xor(
        jnp.bitwise_xor(a_irrep[:, None, None], local_occ[None, :, None]), col_sym[None, None, :]
    )
    return jnp.where(symmetry == 0, shares, jnp.float32(0.0))


def solution(mesh):
    placed = (P("pair", None, "orb", None), P("orb", None, "pair"), P("pair"), P(), P())
    return jax.shard_map(
        body, mesh=mesh, in_specs=placed, out_specs=P("pair", "orb", None), check_vma=False
    )
```

profile of v0, /device:TPU:1, one launch (start us, length us, event | category | flops | bytes accessed | tf_op | source)
XLA Modules:
  0.0 343.5 jit_solution(8693554411935379522)
XLA Ops:
  6.5 0.0 all-gather.2.cloned.1.call-start
  6.5 1.8 copy.21
  8.4 0.0 all-gather.2.cloned.1.call-update
  8.4 0.0 all-reduce.3.cloned.1.call-start
  8.4 5.3 %copy.17 = f32[3,64,4,640]{1,2,0,3:T(4,128)} copy(f32[3,64,4,640]{3,2,1,0:T(4,128)} %param.5) | data formatting | bytes 3932160 | tf_op args[0]
  13.8 6.0 %reshape.58 = f32[16,1,30720]{2,1,0:T(1,128)} reshape(f32[640,3,4,64]{3,2,1,0:T(4,128)} %bitcast.25) | data formatting | bytes 3932160
  19.7 62.4 %all_to_all.18 = f32[16,1,30720]{2,1,0:T(1,128)S(1)} all-to-all(f32[16,1,30720]{2,1,0:T(1,128)} %reshape.58), channel_id=1, replica_groups=mesh['pair'=48,'orb'=16] {'orb'}, dimensions={0} | all-to-all | bytes 3932160 | tf_op jit(solution)/shard_map/all_to_all | solution.py:19
  82.1 0.5 broadcast.29
  82.6 7.2 %reduce = f32[16,30720]{1,0:T(8,128)} reduce(f32[16,1,30720]{2,1,0:T(1,128)S(1)} %all_to_all.18, f32[]{:T(128)} %broadcast.29), dimensions={1}, to_apply=%all_to_all.13.reduce_sub_computation | reduce | bytes 3932164 | tf_op jit(solution)/shard_map/all_to_all | solution.py:19
  89.8 5.2 %reshape.59 = f32[640,3,4,64]{3,2,1,0:T(4,128)} reshape(f32[16,30720]{1,0:T(8,128)} %reduce) | data formatting | bytes 3932160
  95.0 3.0 copy.18
  98.0 2.4 copy.19
  100.4 5.6 %copy.20 = f32[3,64,64,40]{2,3,1,0:T(8,128)} copy(f32[3,64,64,40]{1,3,2,0:T(8,128)} %bitcast.21) | data formatting | bytes 3932160 | tf_op jit(solution)/shard_map/all_to_all | solution.py:19
  106.0 5.7 %multiply_subtract_fusion = f32[3,64,64,40]{2,3,1,0:T(8,128)} fusion(f32[3,64,64,40]{2,3,1,0:T(8,128)} %bitcast.22, f32[3,64,64,40]{2,3,1,0:T(8,128)} %copy.20), kind=kLoop, calls=%fused_computation.3 | loop fusion | flops 983040 | bytes 5898240 | tf_op jit(solution)/shard_map/sub | solution.py:8
  111.7 78.0 %all-gather.2.cloned.1.call-done = f32[40,64,768]{1,0,2:T(8,128)} async-done(((f32[40,64,16]{1,0,2:T(8,128)}), f32[40,64,768]{1,0,2:T(8,128)}) %all-gather.2.cloned.1.call-update) | async-done | bytes 7864336 | tf_op jit(solution)/shard_map/all_gather | solution.py:23
  189.7 14.8 %copy.22 = f32[40,64,768]{2,1,0:T(8,128)} copy(f32[40,64,768]{1,0,2:T(8,128)} %all-gather.2.cloned.1.call-done) | data formatting | bytes 15728640 | tf_op jit(solution)/shard_map/all_gather | solution.py:23
  204.5 0.0 copy-start
  204.5 0.0 copy-start.1
  204.5 0.0 copy-start.2
  204.5 13.4 %fusion.3 = f32[3,64,768]{2,1,0:T(8,128)} fusion(f32[40,64,768]{2,1,0:T(8,128)} %copy.22, f32[3,64,64,40]{2,3,1,0:T(8,128)} %multiply_subtract_fusion), kind=kOutput, calls=%fused_computation.4 | convolution fusion | flops 4529848320 | bytes 10420224 | tf_op jit(solution)/shard_map/dot_general | solution.py:21
  217.9 0.0 all-reduce.3.cloned.1.call-update
  217.9 0.0 copy-done
  217.9 0.0 copy-done.1
  217.9 0.1 broadcast_xor_fusion
  218.0 0.1 xor.58
  218.1 0.1 dynamic_slice.3
  218.1 1.3 dynamic-slice
  220.1 0.0 copy-done.2
  220.1 0.1 broadcast_xor_fusion.1
  220.1 114.9 %all-reduce.3.cloned.1.call-done = f32[3,64,768]{2,1,0:T(8,128)} async-done(((f32[3,64,768]{2,1,0:T(8,128)}), f32[3,64,768]{2,1,0:T(8,128)}) %all-reduce.3.cloned.1.call-update) | async-done | bytes 589840
  335.0 1.6 dynamic-slice_select_fusion
Async XLA Ops:
  6.5 183.2 %all-gather.2.cloned.1.call-start = ((), (), s32[]{:S(2)}) async-start(), calls=%async_computation.1 | async-start | bytes 16056320 | tf_op jit(solution)/shard_map/all_gather | solution.py:23
  8.4 326.7 %all-reduce.3.cloned.1.call-start = ((), (), s32[]{:S(2)}) async-start(), calls=%async_computation.2 | async-start | bytes 1179648
  204.5 13.4 %copy-start = (s32[12]{0:T(128)S(1)}, s32[12]{0:T(128)}, u32[]{:S(2)}) copy-start(s32[12]{0:T(128)} %param.8) | copy-start | bytes 148
  204.5 13.4 %copy-start.1 = (s32[64]{0:T(128)S(1)}, s32[64]{0:T(128)}, u32[]{:S(2)}) copy-start(s32[64]{0:T(128)} %param.9) | copy-start | bytes 772
  204.5 15.6 %copy-start.2 = (s32[3]{0:T(128)S(1)}, s32[3]{0:T(128)}, u32[]{:S(2)}) copy-start(s32[3]{0:T(128)} %param.7) | copy-start | bytes 40
Sparse Core Ops, SparseCore 0:
  11.0 178.6 all-gather.1
  218.0 116.9 all-reduce.2
where the time goes:
time: 344 us; the launch traced here: 343 us
  waiting for transfers between devices  193 us (56%)
  blocking collectives  62.4 us (18%)
  local copies, waits for them, and re-layouts  46 us (13%)
  other arithmetic  14.6 us (4%)
  between operations  14.1 us (4%)
  matrix products  13.4 us (4%)
    unnamed x3, waiting for transfers between devices  115 us
    all_gather x1, waiting for transfers between devices, body(): lax.all_gather(integrals, 'pair', axis=2, tiled=True)  78 us
    all_to_all x1, blocking collectives, body(): lax.all_to_all(amplitudes, 'orb', split_axis=3, concat_axis=2, tiled=True)  62.4 us
    unnamed x11, local copies, waits for them, and re-layouts  19.6 us
    all_gather x1, local copies, waits for them, and re-layouts, body(): lax.all_gather(integrals, 'pair', axis=2, tiled=True)  14.8 us
    dot_general x1, matrix products, body(): jnp.dot(spin, ordered_columns(lax.all_gather(integrals, 'pair', axis=2, t...  13.4 us
    all_to_all x4, local copies, waits for them, and re-layouts, body(): lax.all_to_all(amplitudes, 'orb', split_axis=3, concat_axis=2, tiled=True)  11.5 us
    all_to_all x1, other arithmetic, body(): lax.all_to_all(amplitudes, 'orb', split_axis=3, concat_axis=2, tiled=True)  7.19 us
  transfers between devices with their start and end apart: 2, of which 2 were waited for; matrix products, arithmetic and copies ran while one was open for 12% of the time, Pallas kernels for 0%

commit v1 on v0

v1 whole, which is shorter than its diff:
```python
import jax
import jax.numpy as jnp
from jax import lax
from jax.experimental import pallas as pl
from jax.experimental.pallas import tpu as pltpu
from jax.sharding import Mesh, PartitionSpec as P

MIB = 1 << 20


def spin_kernel(xl_ref, own_ref, other_ref, swapped_ref, high_ref, low_ref, rows):
    xl = xl_ref[0]
    _, window, occupied, virtual = own_ref.shape
    for rel, direct in enumerate((own_ref, other_ref)):
        source = xl if rel == 0 else 1 - xl
        for j in range(2):
            for a in range(window):
                for orb in range(occupied // 4):
                    rows[pl.ds(4 * orb, 4), :] = swapped_ref[2 * orb + source, j, a]
                spin = 2.0 * direct[j, a] - rows[...]
                high = spin.astype(jnp.bfloat16)
                low = (spin - high.astype(jnp.float32)).astype(jnp.bfloat16)
                at = (pl.ds((rel * window + a) * occupied, occupied), pl.ds(j * virtual, virtual))
                high_ref[at] = high
                low_ref[at] = low


def spin_rows(xl, own, other, swapped):
    _, window, occupied, virtual = own.shape
    shape = jax.ShapeDtypeStruct((2 * window * occupied, 2 * virtual), jnp.bfloat16)
    vmem = pl.BlockSpec(memory_space=pltpu.VMEM)
    return pl.pallas_call(
        spin_kernel,
        out_shape=(shape, shape),
        in_specs=[pl.BlockSpec(memory_space=pltpu.SMEM), vmem, vmem, vmem],
        out_specs=(vmem, vmem),
        scratch_shapes=[pltpu.VMEM((occupied, virtual), jnp.float32)],
        compiler_params=pltpu.CompilerParams(vmem_limit_bytes=40 * MIB),
    )(xl, own, other, swapped)


def product_kernel(xl_ref, high_ref, low_ref, columns_ref, out_ref):
    xl = xl_ref[0]
    blocks, virtual, lanes = columns_ref.shape
    half = lanes // 2
    total = None
    for j in range(2):
        block = jnp.concatenate(
            [columns_ref[z, :, j * half:(j + 1) * half] for z in range(blocks)], axis=1
        )
        high = block.astype(jnp.bfloat16)
        low = (block - high.astype(jnp.float32)).astype(jnp.bfloat16)
        left_high = high_ref[:, j * virtual:(j + 1) * virtual]
        left_low = low_ref[:, j * virtual:(j + 1) * virtual]
        for left, right in ((left_high, low), (left_low, high), (left_high, high)):
            part = jnp.dot(left, right, preferred_element_type=jnp.float32)
            total = part if total is None else total + part
    cores, _, ys, window, local = out_ref.shape[:5]
    for rel in range(2):
        target = xl if rel == 0 else 1 - xl
        for a in range(window):
            for y in range(ys):
                for core in range(cores):
                    start = ((rel * window + a) * ys * cores + y * cores + core) * local
                    out_ref[core, target, y, a] = total[start:start + local]


def product(xl, high, low, columns, ys, window, local):
    steps = 3
    zs, virtual, lanes = columns.shape
    blocks = zs // steps
    width = blocks * lanes // 2
    rows, depth = high.shape
    out = jax.ShapeDtypeStruct((2, 2, ys, window, local, steps * width), jnp.float32)
    return pl.pallas_call(
        product_kernel,
        grid=(steps,),
        out_shape=out,
        in_specs=[
            pl.BlockSpec(memory_space=pltpu.SMEM),
            pl.BlockSpec((rows, depth), lambda n: (0, 0)),
            pl.BlockSpec((rows, depth), lambda n: (0, 0)),
            pl.BlockSpec((blocks, virtual, lanes), lambda n: (n, 0, 0)),
        ],
        out_specs=pl.BlockSpec((2, 2, ys, window, local, width), lambda n: (0, 0, 0, 0, 0, n)),
        compiler_params=pltpu.CompilerParams(vmem_limit_bytes=40 * MIB),
    )(xl, high, low, columns)


def body(amplitudes, integrals, a_irrep, b_irrep, occ_irrep):
    window, occupied, local, virtual = amplitudes.shape
    share, _, width = integrals.shape
    ys = lax.axis_size("y")
    xl = lax.axis_index("xl")
    orb = lax.axis_index("y") * 2 + lax.axis_index("core")
    orbs = 2 * ys

    sent = integrals.reshape(share, orbs, 2, 2, width).transpose(2, 1, 3, 0, 4)
    sent = jnp.broadcast_to(sent[None], (2,) + sent.shape).reshape(4 * orbs, -1)
    got = lax.all_to_all(sent, ("xh", "xl", "y", "core"), 0, 0, tiled=True)
    got = got.reshape(4, orbs, 2, share, width).transpose(1, 3, 2, 0, 4).reshape(virtual, 8 * width)
    columns = lax.all_gather(got, "z", axis=0)

    direct = amplitudes.transpose(2, 0, 1, 3)
    own = lax.dynamic_slice_in_dim(direct, 2 * xl, 2)
    given = lax.dynamic_slice_in_dim(direct, 2 * (1 - xl), 2)
    other = lax.ppermute(given, "xl", [(0, 1), (1, 0)])
    swapped = amplitudes.transpose(1, 0, 2, 3).reshape(2 * orbs, 2, window, local, virtual)
    swapped, _ = lax.optimization_barrier((swapped, got))
    swapped = lax.all_to_all(swapped, ("y", "core", "xl"), 0, 0, tiled=True)

    xl_ref = xl.astype(jnp.int32).reshape(1)
    high, low = spin_rows(xl_ref, own, other, swapped)
    partial = product(xl_ref, high, low, columns, ys, window, local)

    partial = lax.all_to_all(partial, "core", 0, 0, tiled=True)
    partial = (partial[0] + partial[1]).reshape(2 * ys, window, local, -1)
    partial = lax.all_to_all(partial, ("xl", "y"), 0, 0, tiled=True)
    shares = jnp.sum(partial, axis=0)
    zs = columns.shape[0]
    shares = shares.reshape(window, local, zs, 4, width).transpose(0, 1, 3, 2, 4).reshape(window, local, -1)

    local_occ = lax.dynamic_slice_in_dim(occ_irrep, orb * local, local)
    col_sym = jnp.bitwise_xor(b_irrep[:, None], occ_irrep[None, :]).reshape(-1)
    symmetry = jnp.bitwise_xor(
        jnp.bitwise_xor(a_irrep[:, None, None], local_occ[None, :, None]), col_sym[None, None, :]
    )
    return jnp.where(symmetry == 0, shares, jnp.float32(0.0))


def solution(mesh):
    split = Mesh(mesh.devices.reshape(2, 2, 12, 8, 2), ("xh", "xl", "z", "y", "core"))
    pair, orb = ("xh", "xl", "z"), ("y", "core")
    placed = (P(pair, None, orb, None), P(orb, None, pair), P(pair), P(), P())
    return jax.shard_map(
        body, mesh=split, in_specs=placed, out_specs=P(pair, orb, None), check_vma=False
    )
```

time: 344 us -> 158 us (0.46)
  waiting for transfers between devices: 193 us -> 58.9 us
  blocking collectives: 62.4 us -> 36.5 us
  local copies, waits for them, and re-layouts: 46 us -> 24.7 us
  starting transfers between devices: 0.04 us -> 15.5 us
  matrix products: 13.4 us -> 0 us
  other arithmetic: 14.6 us -> 2.67 us
  Pallas kernels: 0 us -> 4.73 us
    unnamed x3 -> x1, waiting for transfers between devices: 115 us -> 0.02 us
    all_gather x1, waiting for transfers between devices: 78 us -> 3.67 us  [body(): columns = lax.all_gather(got, 'z', axis=0)]
    ppermute x0 -> x1, waiting for transfers between devices: none -> 38.5 us  [body(): other = lax.ppermute(given, 'xl', [(0, 1), (1, 0)])]
    all_to_all x1 -> x2, blocking collectives: 62.4 us -> 36.5 us  [the longest x1 27.1 us: body(): got = lax.all_to_all(sent, ('xh', 'xl', 'y', 'core'), 0, 0, tiled=True)]
    all_to_all x0 -> x2, waiting for transfers between devices: none -> 16.7 us  [the longest x1 15.4 us: body(): partial = lax.all_to_all(partial, ('xl', 'y'), 0, 0, tiled=True)]
    all_gather x1 -> x0, local copies, waits for them, and re-layouts: 14.8 us -> none  [body(): lax.all_gather(integrals, 'pair', axis=2, tiled=True)]
    dot_general x1 -> x0, matrix products: 13.4 us -> none  [body(): jnp.dot(spin, ordered_columns(lax.all_gather(integrals, 'pair', axis=2, t...]
    all_to_all x0 -> x2, starting transfers between devices: none -> 12.2 us  [the longest x1 7.45 us: body(): partial = lax.all_to_all(partial, ('xl', 'y'), 0, 0, tiled=True)]
  transfers between devices with their start and end apart: 2 -> 4, of which waited for: 2 -> 4; matrix products, arithmetic and copies ran while one was open for 12% -> 3% of each run, Pallas kernels for 0% -> 1%
where the time goes in v1:
time: 158 us; the launch traced here: 157 us
  waiting for transfers between devices  58.9 us (37%)
  blocking collectives  36.5 us (23%)
  local copies, waits for them, and re-layouts  24.7 us (16%)
  starting transfers between devices  15.5 us (10%)
  between operations  13.6 us (9%)
  Pallas kernels  4.73 us (3%)
  other arithmetic  2.67 us (2%)
    ppermute x1, waiting for transfers between devices, body(): other = lax.ppermute(given, 'xl', [(0, 1), (1, 0)])  38.5 us
    all_to_all x1, blocking collectives, body(): got = lax.all_to_all(sent, ('xh', 'xl', 'y', 'core'), 0, 0, tiled=True)  27.1 us
    all_to_all x1, waiting for transfers between devices, body(): partial = lax.all_to_all(partial, ('xl', 'y'), 0, 0, tiled=True)  15.4 us
    unnamed x25, local copies, waits for them, and re-layouts  9.99 us
    all_to_all x1, blocking collectives, body(): partial = lax.all_to_all(partial, 'core', 0, 0, tiled=True)  9.42 us
    all_to_all x1, starting transfers between devices, body(): partial = lax.all_to_all(partial, ('xl', 'y'), 0, 0, tiled=True)  7.45 us
    all_to_all x1, starting transfers between devices, body(): swapped = lax.all_to_all(swapped, ('y', 'core', 'xl'), 0, 0, tiled=True)  4.77 us
    pallas_call x1, Pallas kernels, product(): pl.pallas_call(product_kernel, grid=(steps,), out_shape=out, in_specs=[pl...  3.86 us
  transfers between devices with their start and end apart: 4, of which 4 were waited for; matrix products, arithmetic and copies ran while one was open for 3% of the time, Pallas kernels for 1%

profile of v1, /device:TPU:1, one launch (start us, length us, event | category | flops | bytes accessed | tf_op | source)
XLA Modules:
  0.0 156.6 jit_solution(12154058926039670388)
XLA Ops:
  6.5 0.0 all-gather.2.cloned.1.call-start
  6.5 1.3 copy.21
  7.8 1.5 copy.22
  9.3 1.5 broadcast_in_dim.5
  10.8 0.9 all_to_all.20
  11.8 27.1 %all_to_all.25 = f32[64,1,1280]{2,1,0:T(1,128)S(1)} all-to-all(f32[64,1,1280]{2,1,0:T(1,128)S(1)} %all_to_all.20), channel_id=1, replica_groups=mesh['xh'=2,'xl'=2,'z'=12,'y'=8,'core'=2] {'xh','xl','y','core'}, dimensions={0} | all-to-all | bytes 655360 | tf_op jit(solution)/shard_map/all_to_all | solution.py:100
  38.9 0.8 reduce
  39.7 0.9 reshape.80
  40.6 1.8 %copy.24 = f32[16,40,2,4,16]{1,0,4,3,2:T(8,128)} copy(f32[16,40,2,4,16]{4,1,2,0,3:T(8,128)S(1)} %bitcast.22) | data formatting | bytes 655360 | tf_op jit(solution)/shard_map/transpose | solution.py:101
  42.4 0.0 copy-start.7
  42.4 1.8 %all_gather_reshape.3 = f32[1,640,128]{1,2,0:T(8,128)S(1)} reshape(f32[16,40,2,4,16]{1,0,4,3,2:T(8,128)} %copy.24) | data formatting | bytes 655360 | tf_op jit(solution)/shard_map/all_gather;reshape | solution.py:102
  44.2 0.9 copy.25
  45.1 0.0 all-gather.2.cloned.1.call-update
  45.1 0.0 copy-done.7
  45.1 1.6 %copy.20 = f32[64,3,4,640]{3,2,1,0:T(4,128)} copy(f32[64,3,4,640]{3,2,0,1:T(4,128)S(1)} %bitcast.23) | data formatting | bytes 3932160 | tf_op jit(solution)/shard_map/transpose | solution.py:108
  46.7 4.8 %all-to-all-start = ((f32[32,2,3,4,640]{4,3,2,1,0:T(4,128)}), f32[32,2,3,4,640]{4,3,2,1,0:T(4,128)S(1)}, u32[]{:S(2)}, u32[]{:S(2)}) async-start(f32[32,2,3,4,640]{4,3,2,1,0:T(4,128)} %bitcast.24), calls=%async_computation | async-start | bytes 3932160 | tf_op jit(solution)/shard_map/all_to_all | solution.py:110
  51.5 3.2 %constant_dynamic-slice_fusion = (f32[3,64,2,640]{3,2,1,0:T(2,128)S(1)}, f32[3,64,2,640]{3,2,1,0:T(2,128)S(1)}) fusion(f32[3,64,4,640]{3,2,1,0:T(4,128)} %param.5, s32[]{:T(128)S(6)} %select_n.15, s32[]{:T(128)S(6)} %select_n.14), kind=kLoop, calls=%fused_computation.7 | loop fusion | bytes 3932168 | tf_op jit(solution)/shard_map/dynamic-slice.1
  54.7 0.1 copy.31
  54.8 3.3 %collective-permute-start = (f32[2,3,64,640]{3,2,1,0:T(8,128)S(1)}, f32[2,3,64,640]{3,2,1,0:T(8,128)S(1)}, u32[]{:S(2)}, u32[]{:S(2)}) collective-permute-start(f32[2,3,64,640]{3,2,1,0:T(8,128)S(1)} %bitcast.27), channel_id=1, source_target_pairs={{0,192},{192,0},{1,193},{193,1},{2,194},{194,2},{3,195},{195,3},{4... | collective-permute-start | bytes 2949128 | tf_op jit(solution)/shard_map/ppermute | solution.py:107
  58.1 0.1 copy.32
  58.1 38.5 %collective-permute-done.other_ref = f32[2,3,64,640]{3,2,1,0:T(8,128)S(1)} collective-permute-done((f32[2,3,64,640]{3,2,1,0:T(8,128)S(1)}, f32[2,3,64,640]{3,2,1,0:T(8,128)S(1)}, u32[]{:S(2)}, u32[]{:S(2)}) %collective-permute-start) | collective-permute-done | bytes 983072 | tf_op jit(solution)/shard_map/ppermute | solution.py:107
  96.7 0.9 copy-done.5
  97.6 1.3 all-to-all-done.swapped_ref
  98.9 1.2 copy-done.6
  100.1 0.9 shard_map.55
  101.0 0.0 copy-start.1
  101.0 0.9 copy-done.1
  101.9 1.0 copy-done.3
  102.9 3.7 %all-gather.2.cloned.1.call-done.columns_ref = f32[12,640,128]{2,1,0:T(8,128)} async-done(((f32[1,640,128]{2,1,0:T(8,128)}), f32[12,640,128]{2,1,0:T(8,128)}) %all-gather.2.cloned.1.call-update) | async-done | bytes 3932176 | tf_op jit(solution)/shard_map/all_gather | solution.py:102
  106.5 2.1 %copy-done = f32[12,640,128]{2,1,0:T(8,128)S(1)} copy-done((f32[12,640,128]{2,1,0:T(8,128)S(1)}, f32[12,640,128]{2,1,0:T(8,128)}, u32[]{:S(2)}) %copy-start) | copy-done | bytes 3932184
  108.7 1.2 copy-done.2
  109.9 1.2 copy-done.4
  111.1 3.9 %shard_map.56 = f32[2,2,8,3,4,768]{5,4,3,2,1,0:T(4,128)S(1)} custom-call(s32[1]{0:T(128)} %bitcast.xl_ref, bf16[384,1280]{1,0:T(8,128)(2,1)S(1)} %copy-done.2, bf16[384,1280]{1,0:T(8,128)(2,1)S(1)} %copy-done.4, f32[12,640,128]{2,1,0:T(8,128)S(1)} %copy-done), custom_call_target="tpu_custom_call" | custom-call | tf_op jit(solution)/shard_map/pallas_call | solution.py:75
  114.9 9.4 %all_to_all.26 = f32[2,2,8,3,4,768]{5,4,3,2,1,0:T(4,128)S(1)} all-to-all(f32[2,2,8,3,4,768]{5,4,3,2,1,0:T(4,128)S(1)} %shard_map.56), channel_id=1, replica_groups=mesh['xh'=2,'xl'=2,'z'=12,'y'=8,'core'=2] {'core'}, dimensions={0} | all-to-all | bytes 2359296 | tf_op jit(solution)/shard_map/all_to_all | solution.py:116
  124.4 1.0 slice_add_fusion
  125.3 7.4 %all-to-all-start.3 = ((f32[16,3,4,768]{3,2,1,0:T(4,128)}), f32[16,3,4,768]{3,2,1,0:T(4,128)S(1)}, u32[]{:S(2)}, u32[]{:S(2)}) async-start(f32[16,3,4,768]{3,2,1,0:T(4,128)} %bitcast.8), calls=%async_computation.3 | async-start | bytes 1179648 | tf_op jit(solution)/shard_map/all_to_all | solution.py:118
  132.8 0.0 copy-done.8
  132.8 0.1 dynamic_slice.9
  132.9 0.0 copy-done.9
  132.9 0.1 broadcast_xor_fusion
  132.9 0.1 xor.58
  133.0 0.0 copy-done.10
  133.0 0.1 broadcast_xor_fusion.1
  133.1 15.4 %all-to-all-done.3 = f32[16,3,4,768]{3,2,1,0:T(4,128)S(1)} async-done(((f32[16,3,4,768]{3,2,1,0:T(4,128)}), f32[16,3,4,768]{3,2,1,0:T(4,128)S(1)}, u32[]{:S(2)}, u32[]{:S(2)}) %all-to-all-start.3) | async-done | bytes 589856 | tf_op jit(solution)/shard_map/all_to_all | solution.py:118
  148.5 0.1 reduce_sum.9
  148.6 0.2 reshape.81
  148.9 0.2 reshape.82
  149.1 0.7 fusion
  (10 shorter events, 0.1 us)
Async XLA Ops:
  6.5 100.0 %all-gather.2.cloned.1.call-start = ((), (), s32[]{:S(2)}) async-start(), calls=%async_computation.4 | async-start | bytes 4259840 | tf_op jit(solution)/shard_map/all_gather | solution.py:102
  42.4 2.7 %copy-start.7 = (f32[3,64,4,640]{3,2,1,0:T(4,128)S(1)}, f32[3,64,4,640]{3,2,1,0:T(4,128)}, u32[]{:S(2)}) copy-start(f32[3,64,4,640]{3,2,1,0:T(4,128)} %param.5) | copy-start | bytes 5898244
  46.7 52.1 %all-to-all-start = ((f32[32,2,3,4,640]{4,3,2,1,0:T(4,128)}), f32[32,2,3,4,640]{4,3,2,1,0:T(4,128)S(1)}, u32[]{:S(2)}, u32[]{:S(2)}) async-start(f32[32,2,3,4,640]{4,3,2,1,0:T(4,128)} %bitcast.24), calls=%async_computation | async-start | bytes 3932160 | tf_op jit(solution)/shard_map/all_to_all | solution.py:110
  54.8 41.9 %collective-permute-start = (f32[2,3,64,640]{3,2,1,0:T(8,128)S(1)}, f32[2,3,64,640]{3,2,1,0:T(8,128)S(1)}, u32[]{:S(2)}, u32[]{:S(2)}) collective-permute-start(f32[2,3,64,640]{3,2,1,0:T(8,128)S(1)} %bitcast.27), channel_id=1, source_target_pairs={{0,192},{192,0},{1,193},{193,1},{2,194},{194,2},{3,195},{195,3},{4... | collective-permute-start | bytes 2949128 | tf_op jit(solution)/shard_map/ppermute | solution.py:107
  96.7 0.9 copy-start.5
  98.9 1.2 copy-start.6
  101.0 0.9 copy-start.1
  101.9 1.0 copy-start.3
  106.5 2.1 %copy-start = (f32[12,640,128]{2,1,0:T(8,128)S(1)}, f32[12,640,128]{2,1,0:T(8,128)}, u32[]{:S(2)}) copy-start(f32[12,640,128]{2,1,0:T(8,128)} %all-gather.2.cloned.1.call-done.columns_ref) | copy-start | bytes 11796484
  108.6 1.2 copy-start.2
  109.9 1.2 copy-start.4
  124.3 8.4 %copy-start.8 = (s32[64]{0:T(128)S(1)}, s32[64]{0:T(128)}, u32[]{:S(2)}) copy-start(s32[64]{0:T(128)} %param.9) | copy-start | bytes 772
  124.3 8.5 %copy-start.9 = (s32[12]{0:T(128)S(1)}, s32[12]{0:T(128)}, u32[]{:S(2)}) copy-start(s32[12]{0:T(128)} %param.8) | copy-start | bytes 148
  124.4 8.7 %copy-start.10 = (s32[3]{0:T(128)S(1)}, s32[3]{0:T(128)}, u32[]{:S(2)}) copy-start(s32[3]{0:T(128)} %param.7) | copy-start | bytes 40
  125.3 23.2 %all-to-all-start.3 = ((f32[16,3,4,768]{3,2,1,0:T(4,128)}), f32[16,3,4,768]{3,2,1,0:T(4,128)S(1)}, u32[]{:S(2)}, u32[]{:S(2)}) async-start(f32[16,3,4,768]{3,2,1,0:T(4,128)} %bitcast.8), calls=%async_computation.3 | async-start | bytes 1179648 | tf_op jit(solution)/shard_map/all_to_all | solution.py:118
Sparse Core Ops, SparseCore 0:
  45.2 61.2 all-gather.1

commit v2 on v0

v2 whole, which is shorter than its diff:
```python
import jax
import jax.numpy as jnp
from jax import lax
from jax.experimental import pallas as pl
from jax.experimental.pallas import tpu as pltpu
from jax.sharding import Mesh, PartitionSpec as P

MIB = 1 << 20
VMEM = pl.BlockSpec(memory_space=pltpu.VMEM)


def pack_integrals_kernel(in_ref, out_ref):
    share, _, occupied = in_ref.shape
    half = share // 2
    for xl in range(2):
        for c in range(0, half, 2):
            first = xl * half + c
            pair = jnp.concatenate([in_ref[first], in_ref[first + 1]], axis=1)
            for xh in range(2):
                out_ref[2 * xh + xl, :, c * occupied:(c + 2) * occupied] = pair


def pack_integrals(integrals):
    share, occupied, width = integrals.shape
    return pl.pallas_call(
        pack_integrals_kernel,
        out_shape=jax.ShapeDtypeStruct((4, width, share // 2 * occupied), jnp.float32),
        in_specs=[VMEM],
        out_specs=VMEM,
    )(integrals.transpose(0, 2, 1))


def pack_amplitudes_kernel(in_ref, out_ref, rows, turned, mixed):
    _, occupied, local, virtual = in_ref.shape
    targets, _, depth, lanes = out_ref.shape
    tiles = range(virtual // lanes)
    for d1 in range(occupied):
        for t in tiles:
            rows[t, pl.ds(local * d1, local), :] = in_ref[0, d1, :, t * lanes:(t + 1) * lanes]
    for d2 in range(0, local, 2):
        for t in tiles:
            both = [rows[t, pl.ds(d2 + s, occupied, stride=local), :] for s in range(2)]
            turned[pl.ds(t * lanes, lanes), :] = jnp.concatenate(both, axis=0).T
        even = turned[pl.ds(0, virtual // 2, stride=2), :]
        odd = turned[pl.ds(1, virtual // 2, stride=2), :]
        for s in range(2):
            at = slice(s * occupied, (s + 1) * occupied)
            mixed[pl.ds(d2 + s, virtual // 2, stride=local), :] = jnp.concatenate(
                [even[:, at], odd[:, at]], axis=1
            )
    for target in range(targets):
        out_ref[target, 0] = mixed[pl.ds(depth * target, depth), :]


def pack_amplitudes(amplitudes, targets):
    window, occupied, local, virtual = amplitudes.shape
    depth = virtual // targets // 2 * local
    return pl.pallas_call(
        pack_amplitudes_kernel,
        grid=(window,),
        out_shape=jax.ShapeDtypeStruct((targets, window, depth, 2 * occupied), jnp.float32),
        in_specs=[pl.BlockSpec((1, occupied, local, virtual), lambda a: (a, 0, 0, 0))],
        out_specs=pl.BlockSpec((targets, 1, depth, 2 * occupied), lambda a: (0, a, 0, 0)),
        scratch_shapes=[
            pltpu.VMEM((virtual // (2 * occupied), occupied * local, 2 * occupied), jnp.float32),
            pltpu.VMEM((virtual, 2 * occupied), jnp.float32),
            pltpu.VMEM((virtual // 2 * local, 2 * occupied), jnp.float32),
        ],
        compiler_params=pltpu.CompilerParams(vmem_limit_bytes=16 * MIB),
        cost_estimate=pl.CostEstimate(
            flops=0, bytes_accessed=8 * amplitudes.size, transcendentals=0
        ),
    )(amplitudes)


def spin_kernel(in_ref, high_ref, low_ref, block):
    sources, window, depth, lanes = in_ref.shape
    occupied = lanes // 2
    local = 2 * occupied // sources
    for xl in range(2):
        for a in range(window):
            row = (xl * window + a) * occupied
            for c in range(depth // local):
                for orb in range(sources // 2):
                    block[c % 2, pl.ds(local * orb, local), :] = in_ref[
                        2 * orb + xl, a, c * local:(c + 1) * local
                    ]
                swapped = block[c % 2]
                turned = swapped.T
                direct = jnp.concatenate([turned[:occupied], turned[occupied:]], axis=1)
                spin = 2.0 * direct - swapped
                high = spin.astype(jnp.bfloat16)
                at = (slice(row, row + occupied), slice(c * lanes, (c + 1) * lanes))
                high_ref[at] = high
                low_ref[at] = (spin - high.astype(jnp.float32)).astype(jnp.bfloat16)


def spin_rows(got):
    sources, window, depth, lanes = got.shape
    occupied = lanes // 2
    local = 2 * occupied // sources
    shape = jax.ShapeDtypeStruct((2 * window * occupied, depth // local * lanes), jnp.bfloat16)
    return pl.pallas_call(
        spin_kernel,
        out_shape=(shape, shape),
        in_specs=[VMEM],
        out_specs=(VMEM, VMEM),
        scratch_shapes=[pltpu.VMEM((2, occupied, lanes), jnp.float32)],
        compiler_params=pltpu.CompilerParams(vmem_limit_bytes=16 * MIB),
        cost_estimate=pl.CostEstimate(flops=0, bytes_accessed=8 * got.size, transcendentals=0),
    )(got)


def product_kernel(high_ref, low_ref, columns_ref, out_ref, right_high, right_low):
    zs, _, xls, width, _ = columns_ref.shape
    for xl in range(xls):
        for z in range(zs):
            at = pl.ds((xl * zs + z) * width, width)
            block = columns_ref[z, 0, xl]
            high = block.astype(jnp.bfloat16)
            right_high[at] = high
            right_low[at] = (block - high.astype(jnp.float32)).astype(jnp.bfloat16)

    def dot(left, right):
        return lax.dot_general(
            left[...], right[...], (((1,), (1,)), ((), ())), preferred_element_type=jnp.float32
        )

    total = dot(high_ref, right_low) + dot(low_ref, right_high) + dot(high_ref, right_high)
    cores, _, ys, window, local = out_ref.shape[:5]
    for xl in range(xls):
        for a in range(window):
            for y in range(ys):
                for core in range(cores):
                    start = (((xl * window + a) * ys + y) * cores + core) * local
                    out_ref[core, xl, y, a] = total[start:start + local]


def product(high, low, columns, ys, window, local):
    zs, xhs, xls, width, depth = columns.shape
    rows = high.shape[0]
    block = xls * zs * width
    return pl.pallas_call(
        product_kernel,
        grid=(xhs,),
        out_shape=jax.ShapeDtypeStruct((2, xls, ys, window, local, xhs * block), jnp.float32),
        in_specs=[
            pl.BlockSpec((rows, depth), lambda n: (0, 0)),
            pl.BlockSpec((rows, depth), lambda n: (0, 0)),
            pl.BlockSpec((zs, 1, xls, width, depth), lambda n: (0, n, 0, 0, 0)),
        ],
        out_specs=pl.BlockSpec((2, xls, ys, window, local, block), lambda n: (0, 0, 0, 0, 0, n)),
        scratch_shapes=[pltpu.VMEM((block, depth), jnp.bfloat16)] * 2,
        compiler_params=pltpu.CompilerParams(vmem_limit_bytes=60 * MIB),
        cost_estimate=pl.CostEstimate(
            flops=6 * rows * depth * xhs * block, bytes_accessed=8 << 20, transcendentals=0
        ),
    )(high, low, columns)


def body(amplitudes, integrals, a_irrep, b_irrep, occ_irrep):
    window, occupied, local, virtual = amplitudes.shape
    ys = lax.axis_size("y")
    orb = lax.axis_index("y") * 2 + lax.axis_index("core")

    sent = pack_integrals(integrals)
    got = lax.all_to_all(sent, ("xh", "xl"), 0, 0, tiled=True)
    columns = lax.all_gather(got.reshape((2, 2) + got.shape[1:]), "z", axis=0)

    packed = pack_amplitudes(amplitudes, 4 * ys)
    packed, _ = lax.optimization_barrier((packed, got))
    packed = lax.all_to_all(packed, ("y", "core", "xl"), 0, 0, tiled=True)

    high, low = spin_rows(packed)
    partial = product(high, low, columns, ys, window, local)

    partial = lax.all_to_all(partial, "core", 0, 0, tiled=True)
    partial = (partial[0] + partial[1]).reshape(2 * ys, window, local, -1)
    partial = lax.all_to_all(partial, ("xl", "y"), 0, 0, tiled=True)
    shares = jnp.sum(partial, axis=0)

    local_occ = lax.dynamic_slice_in_dim(occ_irrep, orb * local, local)
    col_sym = jnp.bitwise_xor(b_irrep[:, None], occ_irrep[None, :]).reshape(-1)
    symmetry = jnp.bitwise_xor(
        jnp.bitwise_xor(a_irrep[:, None, None], local_occ[None, :, None]), col_sym[None, None, :]
    )
    return jnp.where(symmetry == 0, shares, jnp.float32(0.0))


def solution(mesh):
    split = Mesh(mesh.devices.reshape(2, 2, 12, 8, 2), ("xh", "xl", "z", "y", "core"))
    pair, orb = ("xh", "xl", "z"), ("y", "core")
    placed = (P(pair, None, orb, None), P(orb, None, pair), P(pair), P(), P())
    return jax.shard_map(
        body, mesh=split, in_specs=placed, out_specs=P(pair, orb, None), check_vma=False
    )
```

time: 344 us -> 138 us (0.40)
  waiting for transfers between devices: 193 us -> 15.4 us
  local copies, waits for them, and re-layouts: 46 us -> 3.64 us
  blocking collectives: 62.4 us -> 82.9 us
  matrix products: 13.4 us -> 0 us
  other arithmetic: 14.6 us -> 1.9 us
  Pallas kernels: 0 us -> 11.6 us
  starting transfers between devices: 0.04 us -> 7.45 us
    unnamed x3 -> x1, waiting for transfers between devices: 115 us -> 0.02 us
    all_gather x1, waiting for transfers between devices: 78 us -> 0.01 us  [body(): columns = lax.all_gather(got.reshape((2, 2) + got.shape[1:]), 'z', axis=0)]
    all_to_all x1 -> x3, blocking collectives: 62.4 us -> 82.9 us  [the longest x1 61.8 us: body(): packed = lax.all_to_all(packed, ('y', 'core', 'xl'), 0, 0, tiled=True)]
    unnamed x11 -> x12, local copies, waits for them, and re-layouts: 19.6 us -> 3.49 us
    all_to_all x0 -> x1, waiting for transfers between devices: none -> 15.4 us  [body(): partial = lax.all_to_all(partial, ('xl', 'y'), 0, 0, tiled=True)]
    all_gather x1 -> x0, local copies, waits for them, and re-layouts: 14.8 us -> none  [body(): lax.all_gather(integrals, 'pair', axis=2, tiled=True)]
    dot_general x1 -> x0, matrix products: 13.4 us -> none  [body(): jnp.dot(spin, ordered_columns(lax.all_gather(integrals, 'pair', axis=2, t...]
    pallas_call x0 -> x4, Pallas kernels: none -> 11.6 us  [the longest x1 6.41 us: product(): pl.pallas_call(product_kernel, grid=(xhs,), out_shape=jax.ShapeDtypeStruc...]
  transfers between devices with their start and end apart: 2 -> 2, of which waited for: 2 -> 1; matrix products, arithmetic and copies ran while one was open for 12% -> 0% of each run, Pallas kernels for 0% -> 2%
where the time goes in v2:
time: 138 us; the launch traced here: 136 us
  blocking collectives  82.9 us (60%)
  waiting for transfers between devices  15.4 us (11%)
  between operations  13.5 us (10%)
  Pallas kernels  11.6 us (8%)
  starting transfers between devices  7.45 us (5%)
  local copies, waits for them, and re-layouts  3.64 us (3%)
  other arithmetic  1.9 us (1%)
    all_to_all x1, blocking collectives, body(): packed = lax.all_to_all(packed, ('y', 'core', 'xl'), 0, 0, tiled=True)  61.8 us
    all_to_all x1, waiting for transfers between devices, body(): partial = lax.all_to_all(partial, ('xl', 'y'), 0, 0, tiled=True)  15.4 us
    all_to_all x1, blocking collectives, body(): got = lax.all_to_all(sent, ('xh', 'xl'), 0, 0, tiled=True)  10.8 us
    all_to_all x1, blocking collectives, body(): partial = lax.all_to_all(partial, 'core', 0, 0, tiled=True)  10.3 us
    all_to_all x1, starting transfers between devices, body(): partial = lax.all_to_all(partial, ('xl', 'y'), 0, 0, tiled=True)  7.45 us
    pallas_call x1, Pallas kernels, product(): pl.pallas_call(product_kernel, grid=(xhs,), out_shape=jax.ShapeDtypeStruc...  6.41 us
    unnamed x12, local copies, waits for them, and re-layouts  3.49 us
  transfers between devices with their start and end apart: 2, of which 1 were waited for; matrix products, arithmetic and copies ran while one was open for 0% of the time, Pallas kernels for 2%

profile of v2, /device:TPU:1, one launch (start us, length us, event | category | flops | bytes accessed | tf_op | source)
XLA Modules:
  0.0 136.4 jit_solution(3248357112653615318)
XLA Ops:
  6.5 0.0 all-gather.2.cloned.1.call-start
  6.5 1.8 %shard_map.56 = f32[4,16,1280]{2,1,0:T(8,128)} custom-call(f32[40,16,64]{2,1,0:T(8,128)} %bitcast.4), custom_call_target="tpu_custom_call" | custom-call | tf_op jit(solution)/shard_map/pallas_call | solution.py:25
  8.3 10.8 %all_to_all.20 = f32[4,16,1280]{2,1,0:T(8,128)} all-to-all(f32[4,16,1280]{2,1,0:T(8,128)} %shard_map.56), channel_id=1, replica_groups=mesh['xh'=2,'xl'=2,'z'=12,'y'=8,'core'=2] {'xh','xl'}, dimensions={0} | all-to-all | bytes 655360 | tf_op jit(solution)/shard_map/all_to_all | solution.py:167
  19.2 0.0 all-gather.2.cloned.1.call-update
  19.2 0.0 copy-start
  19.2 1.5 %copy-done = f32[3,64,4,640]{3,2,1,0:T(4,128)S(1)} copy-done((f32[3,64,4,640]{3,2,1,0:T(4,128)S(1)}, f32[3,64,4,640]{3,2,1,0:T(4,128)}, u32[]{:S(2)}) %copy-start) | copy-done | bytes 1966104
  20.7 1.7 %shard_map.55 = f32[32,3,40,128]{3,2,1,0:T(8,128)S(1)} custom-call(f32[3,64,4,640]{3,2,1,0:T(4,128)S(1)} %copy-done), custom_call_target="tpu_custom_call" | custom-call | bytes 3932160 | tf_op jit(solution)/shard_map/pallas_call | solution.py:58
  22.5 61.8 %all_to_all.21.in_ref = f32[32,3,40,128]{3,2,1,0:T(8,128)S(1)} all-to-all(f32[32,3,40,128]{3,2,1,0:T(8,128)S(1)} %shard_map.55), channel_id=1, replica_groups=mesh['xh'=2,'xl'=2,'z'=12,'y'=8,'core'=2] {'y','core','xl'}, dimensions={0} | all-to-all | bytes 3932160 | tf_op jit(solution)/shard_map/all_to_all | solution.py:172
  84.3 1.6 %shard_map.57 = (bf16[384,1280]{1,0:T(8,128)(2,1)S(1)}, bf16[384,1280]{1,0:T(8,128)(2,1)S(1)}) custom-call(f32[32,3,40,128]{3,2,1,0:T(8,128)S(1)} %all_to_all.21.in_ref), custom_call_target="tpu_custom_call" | custom-call | bytes 3932160 | tf_op jit(solution)/shard_map/pallas_call | solution.py:103
  85.9 0.0 copy-start.1
  85.9 1.0 copy-done.1
  86.9 0.0 copy-start.2
  86.9 1.0 copy-done.2
  87.9 0.0 all-gather.2.cloned.1.call-done.columns_ref
  87.9 6.4 %shard_map.58 = f32[2,2,8,3,4,768]{5,4,3,2,1,0:T(4,128)} custom-call(bf16[384,1280]{1,0:T(8,128)(2,1)} %copy-done.1, bf16[384,1280]{1,0:T(8,128)(2,1)} %copy-done.2, f32[12,2,2,16,1280]{4,3,2,1,0:T(8,128)} %all-gather.2.cloned.1.call-done.columns_ref), custom_call_target="tpu_custom_call" | custom-call | flops 2264924160 | bytes 8388608 | tf_op jit(solution)/shard_map/pallas_call | solution.py:143
  94.3 10.3 %all_to_all.22 = f32[2,2,8,3,4,768]{5,4,3,2,1,0:T(4,128)S(1)} all-to-all(f32[2,2,8,3,4,768]{5,4,3,2,1,0:T(4,128)} %shard_map.58), channel_id=1, replica_groups=mesh['xh'=2,'xl'=2,'z'=12,'y'=8,'core'=2] {'core'}, dimensions={0} | all-to-all | bytes 2359296 | tf_op jit(solution)/shard_map/all_to_all | solution.py:177
  104.6 0.0 copy-start.3
  104.6 0.0 copy-start.4
  104.6 0.0 copy-start.5
  104.6 1.0 slice_add_fusion
  105.6 7.4 %all-to-all-start.3 = ((f32[16,3,4,768]{3,2,1,0:T(4,128)}), f32[16,3,4,768]{3,2,1,0:T(4,128)S(1)}, u32[]{:S(2)}, u32[]{:S(2)}) async-start(f32[16,3,4,768]{3,2,1,0:T(4,128)} %bitcast.2), calls=%async_computation.3 | async-start | bytes 1179648 | tf_op jit(solution)/shard_map/all_to_all | solution.py:179
  113.1 0.0 copy-done.3
  113.1 0.0 copy-done.4
  113.1 0.1 broadcast_xor_fusion
  113.1 0.1 xor.58
  113.2 0.1 dynamic_slice.3
  113.3 0.0 copy-done.5
  113.3 0.1 broadcast_xor_fusion.1
  113.4 15.4 %all-to-all-done.3 = f32[16,3,4,768]{3,2,1,0:T(4,128)S(1)} async-done(((f32[16,3,4,768]{3,2,1,0:T(4,128)}), f32[16,3,4,768]{3,2,1,0:T(4,128)S(1)}, u32[]{:S(2)}, u32[]{:S(2)}) %all-to-all-start.3) | async-done | bytes 589856 | tf_op jit(solution)/shard_map/all_to_all | solution.py:179
  128.8 0.1 reduce_sum.9
  128.9 0.7 fusion
Async XLA Ops:
  6.5 81.3 %all-gather.2.cloned.1.call-start = ((), (), s32[]{:S(2)}) async-start(), calls=%async_computation.4 | async-start | bytes 4259840 | tf_op jit(solution)/shard_map/all_gather | solution.py:168
  19.2 1.5 %copy-start = (f32[3,64,4,640]{3,2,1,0:T(4,128)S(1)}, f32[3,64,4,640]{3,2,1,0:T(4,128)}, u32[]{:S(2)}) copy-start(f32[3,64,4,640]{3,2,1,0:T(4,128)} %in_ref.1) | copy-start | bytes 5898244
  85.9 1.0 copy-start.1
  86.9 1.0 copy-start.2
  104.6 8.4 %copy-start.3 = (s32[12]{0:T(128)S(1)}, s32[12]{0:T(128)}, u32[]{:S(2)}) copy-start(s32[12]{0:T(128)} %param.8) | copy-start | bytes 148
  104.6 8.4 %copy-start.4 = (s32[64]{0:T(128)S(1)}, s32[64]{0:T(128)}, u32[]{:S(2)}) copy-start(s32[64]{0:T(128)} %param.9) | copy-start | bytes 772
  104.6 8.7 %copy-start.5 = (s32[3]{0:T(128)S(1)}, s32[3]{0:T(128)}, u32[]{:S(2)}) copy-start(s32[3]{0:T(128)} %param.7) | copy-start | bytes 40
  105.6 23.2 %all-to-all-start.3 = ((f32[16,3,4,768]{3,2,1,0:T(4,128)}), f32[16,3,4,768]{3,2,1,0:T(4,128)S(1)}, u32[]{:S(2)}, u32[]{:S(2)}) async-start(f32[16,3,4,768]{3,2,1,0:T(4,128)} %bitcast.2), calls=%async_computation.3 | async-start | bytes 1179648 | tf_op jit(solution)/shard_map/all_to_all | solution.py:179
Sparse Core Ops, SparseCore 0:
  19.3 68.3 all-gather.1

commit v3 on v2

--- a/solution.py
+++ b/solution.py
@@ -73,89 +73,116 @@
     )(amplitudes)
 
 
-def spin_kernel(in_ref, high_ref, low_ref, block):
+def spin_kernel(in_ref, high_ref, low_ref, block, mixed):
     sources, window, depth, lanes = in_ref.shape
     occupied = lanes // 2
-    local = 2 * occupied // sources
+    orbs = sources // 2
+    local = occupied // orbs
     for xl in range(2):
         for a in range(window):
-            row = (xl * window + a) * occupied
+            row = (xl * window + a) * occupied // 2
             for c in range(depth // local):
-                for orb in range(sources // 2):
-                    block[c % 2, pl.ds(local * orb, local), :] = in_ref[
+                slot = c % 2
+                for orb in range(orbs):
+                    block[slot, pl.ds(local * orb, local), :] = in_ref[
                         2 * orb + xl, a, c * local:(c + 1) * local
                     ]
-                swapped = block[c % 2]
+                swapped = block[slot]
                 turned = swapped.T
                 direct = jnp.concatenate([turned[:occupied], turned[occupied:]], axis=1)
                 spin = 2.0 * direct - swapped
-                high = spin.astype(jnp.bfloat16)
-                at = (slice(row, row + occupied), slice(c * lanes, (c + 1) * lanes))
-                high_ref[at] = high
-                low_ref[at] = (spin - high.astype(jnp.float32)).astype(jnp.bfloat16)
+                for orb in range(orbs):
+                    to = (orb % 2) * occupied // 2 + orb // 2 * local
+                    mixed[slot, pl.ds(to, local), :] = spin[local * orb:local * (orb + 1)]
+                for core in range(2):
+                    rows = mixed[slot, pl.ds(core * occupied // 2, occupied // 2), :]
+                    high = rows.astype(jnp.bfloat16)
+                    at = (core, slice(row, row + occupied // 2), slice(c * lanes, (c + 1) * lanes))
+                    high_ref[at] = high
+                    low_ref[at] = (rows - high.astype(jnp.float32)).astype(jnp.bfloat16)
 
 
 def spin_rows(got):
     sources, window, depth, lanes = got.shape
     occupied = lanes // 2
     local = 2 * occupied // sources
-    shape = jax.ShapeDtypeStruct((2 * window * occupied, depth // local * lanes), jnp.bfloat16)
+    shape = jax.ShapeDtypeStruct((2, window * occupied, depth // local * lanes), jnp.bfloat16)
     return pl.pallas_call(
         spin_kernel,
         out_shape=(shape, shape),
         in_specs=[VMEM],
         out_specs=(VMEM, VMEM),
-        scratch_shapes=[pltpu.VMEM((2, occupied, lanes), jnp.float32)],
-        compiler_params=pltpu.CompilerParams(vmem_limit_bytes=16 * MIB),
+        scratch_shapes=[pltpu.VMEM((2, occupied, lanes), jnp.float32)] * 2,
+        compiler_params=pltpu.CompilerParams(vmem_limit_bytes=8 * MIB),
         cost_estimate=pl.CostEstimate(flops=0, bytes_accessed=8 * got.size, transcendentals=0),
     )(got)
 
 
-def product_kernel(high_ref, low_ref, columns_ref, out_ref, right_high, right_low):
-    zs, _, xls, width, _ = columns_ref.shape
-    for xl in range(xls):
-        for z in range(zs):
-            at = pl.ds((xl * zs + z) * width, width)
-            block = columns_ref[z, 0, xl]
-            high = block.astype(jnp.bfloat16)
-            right_high[at] = high
-            right_low[at] = (block - high.astype(jnp.float32)).astype(jnp.bfloat16)
+def product_kernel(
+    core_ref, high_ref, low_ref, columns_ref, out_ref, left, right, right_high, right_low, sems
+):
+    zs, xs, width, depth = columns_ref.shape
+    core = core_ref[0]
+    copies = [
+        pltpu.make_async_copy(columns_ref.at[:, x], right.at[x], sems.at[x]) for x in range(xs)
+    ]
+    halves = [
+        pltpu.make_async_copy(ref.at[core], left.at[i], sems.at[xs + i])
+        for i, ref in enumerate((high_ref, low_ref))
+    ]
+    for copy in copies[:1] + halves + copies[1:]:
+        copy.start()
+    block = xs // 2 * zs * width
+    xls, ys, window, local = out_ref.shape[:4]
 
     def dot(left, right):
         return lax.dot_general(
-            left[...], right[...], (((1,), (1,)), ((), ())), preferred_element_type=jnp.float32
+            left, right, (((1,), (1,)), ((), ())), preferred_element_type=jnp.float32
         )
 
-    total = dot(high_ref, right_low) + dot(low_ref, right_high) + dot(high_ref, right_high)
-    cores, _, ys, window, local = out_ref.shape[:5]
-    for xl in range(xls):
-        for a in range(window):
-            for y in range(ys):
-                for core in range(cores):
-                    start = (((xl * window + a) * ys + y) * cores + core) * local
-                    out_ref[core, xl, y, a] = total[start:start + local]
-
-
-def product(high, low, columns, ys, window, local):
-    zs, xhs, xls, width, depth = columns.shape
-    rows = high.shape[0]
-    block = xls * zs * width
+    for side in range(2):
+        for x in range(side * xs // 2, (side + 1) * xs // 2):
+            copies[x].wait()
+            for z in range(zs):
+                at = pl.ds((x * zs + z) * width, width)
+                rows = right[x, z]
+                high = rows.astype(jnp.bfloat16)
+                right_high[at] = high
+                right_low[at] = (rows - high.astype(jnp.float32)).astype(jnp.bfloat16)
+        if side == 0:
+            for copy in halves:
+                copy.wait()
+        left_high, left_low = left[0], left[1]
+        at = pl.ds(side * block, block)
+        high, low = right_high[at], right_low[at]
+        total = dot(left_high, low) + dot(left_low, high) + dot(left_high, high)
+        for xl in range(xls):
+            for a in range(window):
+                for y in range(ys):
+                    start = ((xl * window + a) * ys + y) * local
+                    out_ref[xl, y, a, :, side * block:(side + 1) * block] = total[start:start + local]
+
+
+def product(core, high, low, columns, ys, window, local):
+    zs, xs, width, depth = columns.shape
+    rows = high.shape[1]
     return pl.pallas_call(
         product_kernel,
-        grid=(xhs,),
-        out_shape=jax.ShapeDtypeStruct((2, xls, ys, window, local, xhs * block), jnp.float32),
-        in_specs=[
-            pl.BlockSpec((rows, depth), lambda n: (0, 0)),
-            pl.BlockSpec((rows, depth), lambda n: (0, 0)),
-            pl.BlockSpec((zs, 1, xls, width, depth), lambda n: (0, n, 0, 0, 0)),
+        out_shape=jax.ShapeDtypeStruct((2, ys, window, local, xs * zs * width), jnp.float32),
+        in_specs=[pl.BlockSpec(memory_space=pltpu.SMEM)] + [pl.BlockSpec(memory_space=pl.ANY)] * 3,
+        out_specs=VMEM,
+        scratch_shapes=[
+            pltpu.VMEM((2, rows, depth), jnp.bfloat16),
+            pltpu.VMEM((xs, zs, width, depth), jnp.float32),
+            pltpu.VMEM((xs * zs * width, depth), jnp.bfloat16),
+            pltpu.VMEM((xs * zs * width, depth), jnp.bfloat16),
+            pltpu.SemaphoreType.DMA((xs + 2,)),
         ],
-        out_specs=pl.BlockSpec((2, xls, ys, window, local, block), lambda n: (0, 0, 0, 0, 0, n)),
-        scratch_shapes=[pltpu.VMEM((block, depth), jnp.bfloat16)] * 2,
-        compiler_params=pltpu.CompilerParams(vmem_limit_bytes=60 * MIB),
+        compiler_params=pltpu.CompilerParams(vmem_limit_bytes=52 * MIB),
         cost_estimate=pl.CostEstimate(
-            flops=6 * rows * depth * xhs * block, bytes_accessed=8 << 20, transcendentals=0
+            flops=6 * rows * depth * xs * zs * width, bytes_accessed=8 << 20, transcendentals=0
         ),
-    )(high, low, columns)
+    )(core, high, low, columns)
 
 
 def body(amplitudes, integrals, a_irrep, b_irrep, occ_irrep):
@@ -165,17 +192,19 @@
 
     sent = pack_integrals(integrals)
     got = lax.all_to_all(sent, ("xh", "xl"), 0, 0, tiled=True)
-    columns = lax.all_gather(got.reshape((2, 2) + got.shape[1:]), "z", axis=0)
-
     packed = pack_amplitudes(amplitudes, 4 * ys)
-    packed, _ = lax.optimization_barrier((packed, got))
+    packed, got = lax.optimization_barrier((packed, got))
+    columns = lax.all_gather(got, "z", axis=0)
+
     packed = lax.all_to_all(packed, ("y", "core", "xl"), 0, 0, tiled=True)
-
     high, low = spin_rows(packed)
-    partial = product(high, low, columns, ys, window, local)
-
-    partial = lax.all_to_all(partial, "core", 0, 0, tiled=True)
-    partial = (partial[0] + partial[1]).reshape(2 * ys, window, local, -1)
+
+    core = lax.axis_index("core").astype(jnp.int32).reshape(1)
+    given = product(1 - core, high, low, columns, ys, window, local)
+    given = lax.ppermute(given, "core", [(0, 1), (1, 0)])
+    partial = product(core, high, low, columns, ys, window, local) + given
+
+    partial = partial.reshape(2 * ys, window, local, -1)
     partial = lax.all_to_all(partial, ("xl", "y"), 0, 0, tiled=True)
     shares = jnp.sum(partial, axis=0)
 

time: 138 us -> 137 us (level)
  blocking collectives: 82.9 us -> 0 us
  waiting for transfers between devices: 15.4 us -> 69 us
  starting transfers between devices: 7.45 us -> 33.2 us
  Pallas kernels: 11.6 us -> 15.4 us
    all_to_all x3 -> x0, blocking collectives: 82.9 us -> none  [the longest x1 61.8 us: body(): packed = lax.all_to_all(packed, ('y', 'core', 'xl'), 0, 0, tiled=True)]
    all_to_all x0 -> x2, waiting for transfers between devices: none -> 48.8 us  [the longest x1 47.3 us: body(): packed = lax.all_to_all(packed, ('y', 'core', 'xl'), 0, 0, tiled=True)]
    all_to_all x0 -> x2, starting transfers between devices: none -> 18.8 us  [the longest x1 13.9 us: body(): packed = lax.all_to_all(packed, ('y', 'core', 'xl'), 0, 0, tiled=True)]
    ppermute x0 -> x1, starting transfers between devices: none -> 7.02 us  [body(): given = lax.ppermute(given, 'core', [(0, 1), (1, 0)])]
    all_gather x1, waiting for transfers between devices: 0.01 us -> 4.33 us  [body(): columns = lax.all_gather(got, 'z', axis=0)]
    pallas_call x1 -> x2, Pallas kernels: 6.41 us -> 8.93 us  [product(): pl.pallas_call(product_kernel, out_shape=jax.ShapeDtypeStruct((2, ys, win...]
  transfers between devices with their start and end apart: 2 -> 5, of which waited for: 1 -> 4; matrix products, arithmetic and copies ran while one was open for 0% -> 0% of each run, Pallas kernels for 2% -> 7%
where the time goes in v3:
time: 137 us
  waiting for transfers between devices  69 us (50%)
  starting transfers between devices  33.2 us (24%)
  Pallas kernels  15.4 us (11%)
  between operations  13.5 us (10%)
  local copies, waits for them, and re-layouts  3.36 us (2%)
  other arithmetic  1.96 us (1%)
    all_to_all x1, waiting for transfers between devices, body(): packed = lax.all_to_all(packed, ('y', 'core', 'xl'), 0, 0, tiled=True)  47.3 us
    all_to_all x1, waiting for transfers between devices, body(): partial = lax.all_to_all(partial, ('xl', 'y'), 0, 0, tiled=True)  15.8 us
    all_to_all x1, starting transfers between devices, body(): packed = lax.all_to_all(packed, ('y', 'core', 'xl'), 0, 0, tiled=True)  13.9 us
    pallas_call x2, Pallas kernels, product(): pl.pallas_call(product_kernel, out_shape=jax.ShapeDtypeStruct((2, ys, win...  8.93 us
    all_to_all x1, starting transfers between devices, body(): partial = lax.all_to_all(partial, ('xl', 'y'), 0, 0, tiled=True)  7.46 us
    ppermute x1, starting transfers between devices, body(): given = lax.ppermute(given, 'core', [(0, 1), (1, 0)])  7.02 us
    all_to_all x1, starting transfers between devices, body(): got = lax.all_to_all(sent, ('xh', 'xl'), 0, 0, tiled=True)  4.84 us
    all_gather x1, waiting for transfers between devices, body(): columns = lax.all_gather(got, 'z', axis=0)  4.33 us
  transfers between devices with their start and end apart: 5, of which 4 were waited for; matrix products, arithmetic and copies ran while one was open for 0% of the time, Pallas kernels for 7%

profile of v3, /device:TPU:1, one launch (start us, length us, event | category | flops | bytes accessed | tf_op | source)
XLA Modules:
  0.0 136.5 jit_solution(3946171030904593194)
XLA Ops:
  6.5 1.8 %shard_map.56 = f32[4,16,1280]{2,1,0:T(8,128)} custom-call(f32[40,16,64]{2,1,0:T(8,128)} %bitcast.6), custom_call_target="tpu_custom_call" | custom-call | tf_op jit(solution)/shard_map/pallas_call | solution.py:25
  8.3 4.8 %all-to-all-start = ((f32[4,16,1280]{2,1,0:T(8,128)}), f32[4,16,1280]{2,1,0:T(8,128)S(1)}, u32[]{:S(2)}, u32[]{:S(2)}) async-start(f32[4,16,1280]{2,1,0:T(8,128)} %shard_map.56), calls=%async_computation | async-start | bytes 655360 | tf_op jit(solution)/shard_map/all_to_all | solution.py:194
  13.2 0.0 all-gather.3.cloned.1.call-start
  13.2 0.0 copy-start.1
  13.2 1.5 %copy-done.1 = f32[3,64,4,640]{3,2,1,0:T(4,128)S(1)} copy-done((f32[3,64,4,640]{3,2,1,0:T(4,128)S(1)}, f32[3,64,4,640]{3,2,1,0:T(4,128)}, u32[]{:S(2)}) %copy-start.1) | copy-done | bytes 1966104
  14.7 2.8 %shard_map.55 = f32[32,3,40,128]{3,2,1,0:T(8,128)} custom-call(f32[3,64,4,640]{3,2,1,0:T(4,128)S(1)} %copy-done.1), custom_call_target="tpu_custom_call" | custom-call | bytes 3932160 | tf_op jit(solution)/shard_map/pallas_call | solution.py:58
  17.5 1.5 %all-to-all-done = f32[4,16,1280]{2,1,0:T(8,128)S(1)} async-done(((f32[4,16,1280]{2,1,0:T(8,128)}), f32[4,16,1280]{2,1,0:T(8,128)S(1)}, u32[]{:S(2)}, u32[]{:S(2)}) %all-to-all-start) | async-done | bytes 327712 | tf_op jit(solution)/shard_map/all_to_all | solution.py:194
  19.1 0.0 copy-start.2
  19.1 0.7 copy-done.2
  19.8 0.0 all-gather.3.cloned.1.call-update
  19.8 13.9 %all-to-all-start.1 = ((f32[32,3,40,128]{3,2,1,0:T(8,128)}), f32[32,3,40,128]{3,2,1,0:T(8,128)S(1)}, u32[]{:S(2)}, u32[]{:S(2)}) async-start(f32[32,3,40,128]{3,2,1,0:T(8,128)} %shard_map.55), calls=%async_computation.1 | async-start | bytes 3932160 | tf_op jit(solution)/shard_map/all_to_all | solution.py:199
  33.7 47.3 %all-to-all-done.1.in_ref = f32[32,3,40,128]{3,2,1,0:T(8,128)S(1)} async-done(((f32[32,3,40,128]{3,2,1,0:T(8,128)}), f32[32,3,40,128]{3,2,1,0:T(8,128)S(1)}, u32[]{:S(2)}, u32[]{:S(2)}) %all-to-all-start.1) | async-done | bytes 1966112 | tf_op jit(solution)/shard_map/all_to_all | solution.py:199
  81.1 1.9 %shard_map.57 = (bf16[2,192,1280]{2,1,0:T(8,128)(2,1)S(1)}, bf16[2,192,1280]{2,1,0:T(8,128)(2,1)S(1)}) custom-call(f32[32,3,40,128]{3,2,1,0:T(8,128)S(1)} %all-to-all-done.1.in_ref), custom_call_target="tpu_custom_call" | custom-call | bytes 3932160 | tf_op jit(solution)/shard_map/pallas_call | solution.py:110
  83.0 0.0 copy-start
  83.0 0.9 copy-done
  83.9 4.3 %all-gather.3.cloned.1.call-done = f32[48,16,1280]{2,1,0:T(8,128)} async-done(((f32[4,16,1280]{2,1,0:T(8,128)}), f32[48,16,1280]{2,1,0:T(8,128)}) %all-gather.3.cloned.1.call-update) | async-done | bytes 3932176 | tf_op jit(solution)/shard_map/all_gather | solution.py:197
  88.2 4.5 %shard_map.59 = f32[2,8,3,4,768]{4,3,2,1,0:T(4,128)S(1)} custom-call(s32[1]{0:T(128)S(6)} %sub.3.core_ref, bf16[2,192,1280]{2,1,0:T(8,128)(2,1)S(1)} %get-tuple-element.10.high_ref, bf16[2,192,1280]{2,1,0:T(8,128)(2,1)} %copy-done, f32[12,4,16,1280]{3,2,1,0:T(8,128)} %bitcast.4), custom_call_target="tpu_custom_call" | custom-call | flops 1132462080 | bytes 8388608 | tf_op jit(solution)/shard_map/pallas_call | solution.py:169
  92.7 7.0 %collective-permute-start = (f32[2,8,3,4,768]{4,3,2,1,0:T(4,128)S(1)}, f32[2,8,3,4,768]{4,3,2,1,0:T(4,128)S(1)}, u32[]{:S(2)}, u32[]{:S(2)}) collective-permute-start(f32[2,8,3,4,768]{4,3,2,1,0:T(4,128)S(1)} %shard_map.59), channel_id=1, source_target_pairs={{0,1},{1,0},{2,3},{3,2},{4,5},{5,4},{6,7},{7,6},{8,9},{9,8},{10,11... | collective-permute-start | bytes 1769480 | tf_op jit(solution)/shard_map/ppermute | solution.py:204
  99.7 4.5 %shard_map.58 = f32[2,8,3,4,768]{4,3,2,1,0:T(4,128)S(1)} custom-call(s32[1]{0:T(128)} %bitcast.core_ref, bf16[2,192,1280]{2,1,0:T(8,128)(2,1)S(1)} %get-tuple-element.10.high_ref, bf16[2,192,1280]{2,1,0:T(8,128)(2,1)} %copy-done, f32[12,4,16,1280]{3,2,1,0:T(8,128)} %bitcast.5), custom_call_target="tpu_custom_call" | custom-call | flops 1132462080 | bytes 8388608 | tf_op jit(solution)/shard_map/pallas_call | solution.py:169
  104.2 0.0 copy-start.3
  104.2 0.0 copy-start.4
  104.2 0.0 copy-start.5
  104.2 0.0 collective-permute-done
  104.3 1.0 add.11
  105.3 7.5 %all-to-all-start.2 = ((f32[16,3,4,768]{3,2,1,0:T(4,128)}), f32[16,3,4,768]{3,2,1,0:T(4,128)S(1)}, u32[]{:S(2)}, u32[]{:S(2)}) async-start(f32[16,3,4,768]{3,2,1,0:T(4,128)} %bitcast.3), calls=%async_computation.2 | async-start | bytes 1179648 | tf_op jit(solution)/shard_map/all_to_all | solution.py:208
  112.7 0.0 copy-done.3
  112.8 0.0 copy-done.4
  112.8 0.1 broadcast_xor_fusion
  112.8 0.1 xor.58
  112.9 0.1 dynamic_slice.3
  113.0 0.0 copy-done.5
  113.0 0.1 broadcast_xor_fusion.1
  113.1 15.8 %all-to-all-done.2 = f32[16,3,4,768]{3,2,1,0:T(4,128)S(1)} async-done(((f32[16,3,4,768]{3,2,1,0:T(4,128)}), f32[16,3,4,768]{3,2,1,0:T(4,128)S(1)}, u32[]{:S(2)}, u32[]{:S(2)}) %all-to-all-start.2) | async-done | bytes 589856 | tf_op jit(solution)/shard_map/all_to_all | solution.py:208
  128.9 0.1 reduce_sum.9
  129.0 0.7 fusion
Async XLA Ops:
  8.3 10.7 %all-to-all-start = ((f32[4,16,1280]{2,1,0:T(8,128)}), f32[4,16,1280]{2,1,0:T(8,128)S(1)}, u32[]{:S(2)}, u32[]{:S(2)}) async-start(f32[4,16,1280]{2,1,0:T(8,128)} %shard_map.56), calls=%async_computation | async-start | bytes 655360 | tf_op jit(solution)/shard_map/all_to_all | solution.py:194
  13.2 75.1 %all-gather.3.cloned.1.call-start = ((), (), s32[]{:S(2)}) async-start(), calls=%async_computation.3 | async-start | bytes 4259840 | tf_op jit(solution)/shard_map/all_gather | solution.py:197
  13.2 1.5 %copy-start.1 = (f32[3,64,4,640]{3,2,1,0:T(4,128)S(1)}, f32[3,64,4,640]{3,2,1,0:T(4,128)}, u32[]{:S(2)}) copy-start(f32[3,64,4,640]{3,2,1,0:T(4,128)} %in_ref.1) | copy-start | bytes 5898244
  19.1 0.7 copy-start.2
  19.8 61.3 %all-to-all-start.1 = ((f32[32,3,40,128]{3,2,1,0:T(8,128)}), f32[32,3,40,128]{3,2,1,0:T(8,128)S(1)}, u32[]{:S(2)}, u32[]{:S(2)}) async-start(f32[32,3,40,128]{3,2,1,0:T(8,128)} %shard_map.55), calls=%async_computation.1 | async-start | bytes 3932160 | tf_op jit(solution)/shard_map/all_to_all | solution.py:199
  83.0 0.9 copy-start
  92.7 11.5 %collective-permute-start = (f32[2,8,3,4,768]{4,3,2,1,0:T(4,128)S(1)}, f32[2,8,3,4,768]{4,3,2,1,0:T(4,128)S(1)}, u32[]{:S(2)}, u32[]{:S(2)}) collective-permute-start(f32[2,8,3,4,768]{4,3,2,1,0:T(4,128)S(1)} %shard_map.59), channel_id=1, source_target_pairs={{0,1},{1,0},{2,3},{3,2},{4,5},{5,4},{6,7},{7,6},{8,9},{9,8},{10,11... | collective-permute-start | bytes 1769480 | tf_op jit(solution)/shard_map/ppermute | solution.py:204
  104.2 8.5 %copy-start.3 = (s32[12]{0:T(128)S(1)}, s32[12]{0:T(128)}, u32[]{:S(2)}) copy-start(s32[12]{0:T(128)} %param.8) | copy-start | bytes 148
  104.2 8.5 %copy-start.4 = (s32[64]{0:T(128)S(1)}, s32[64]{0:T(128)}, u32[]{:S(2)}) copy-start(s32[64]{0:T(128)} %param.9) | copy-start | bytes 772
  104.2 8.8 %copy-start.5 = (s32[3]{0:T(128)S(1)}, s32[3]{0:T(128)}, u32[]{:S(2)}) copy-start(s32[3]{0:T(128)} %param.7) | copy-start | bytes 40
  105.3 23.6 %all-to-all-start.2 = ((f32[16,3,4,768]{3,2,1,0:T(4,128)}), f32[16,3,4,768]{3,2,1,0:T(4,128)S(1)}, u32[]{:S(2)}, u32[]{:S(2)}) async-start(f32[16,3,4,768]{3,2,1,0:T(4,128)} %bitcast.3), calls=%async_computation.2 | async-start | bytes 1179648 | tf_op jit(solution)/shard_map/all_to_all | solution.py:208
Sparse Core Ops, SparseCore 0:
  19.9 68.2 all-gather.2

commit v4 on v3

--- a/solution.py
+++ b/solution.py
@@ -118,101 +118,118 @@
     )(got)
 
 
-def product_kernel(
-    core_ref, high_ref, low_ref, columns_ref, out_ref, left, right, right_high, right_low, sems
-):
-    zs, xs, width, depth = columns_ref.shape
-    core = core_ref[0]
+def product_kernel(place_ref, high_ref, low_ref, *refs):
+    *columns_refs, own_ref, other_ref, left, right, right_high, right_low, sems = refs
+    zs = len(columns_refs)
+    xs, width = columns_refs[0].shape[:2]
+    z, core = place_ref[0], place_ref[1]
+    rows = high_ref.shape[1]
     copies = [
-        pltpu.make_async_copy(columns_ref.at[:, x], right.at[x], sems.at[x]) for x in range(xs)
+        pltpu.make_async_copy(ref, right.at[r], sems.at[r]) for r, ref in enumerate(columns_refs)
     ]
     halves = [
-        pltpu.make_async_copy(ref.at[core], left.at[i], sems.at[xs + i])
+        pltpu.make_async_copy(
+            ref.at[side], left.at[i, pl.ds(part * rows, rows)], sems.at[zs + 2 * i + part]
+        )
         for i, ref in enumerate((high_ref, low_ref))
+        for part, side in enumerate((core, 1 - core))
     ]
-    for copy in copies[:1] + halves + copies[1:]:
+    for copy in copies + halves:
         copy.start()
-    block = xs // 2 * zs * width
-    xls, ys, window, local = out_ref.shape[:4]
+    for r in range(zs):
+        copies[r].wait()
+        at_z = lax.rem(z + r, zs)
+        for x in range(xs):
+            at = pl.ds(pl.multiple_of((x * zs + at_z) * width, width), width)
+            block = right[r, x]
+            high = block.astype(jnp.bfloat16)
+            right_high[at] = high
+            right_low[at] = (block - high.astype(jnp.float32)).astype(jnp.bfloat16)
 
     def dot(left, right):
         return lax.dot_general(
-            left, right, (((1,), (1,)), ((), ())), preferred_element_type=jnp.float32
+            left, right[...], (((1,), (1,)), ((), ())), preferred_element_type=jnp.float32
         )
 
-    for side in range(2):
-        for x in range(side * xs // 2, (side + 1) * xs // 2):
-            copies[x].wait()
-            for z in range(zs):
-                at = pl.ds((x * zs + z) * width, width)
-                rows = right[x, z]
-                high = rows.astype(jnp.bfloat16)
-                right_high[at] = high
-                right_low[at] = (rows - high.astype(jnp.float32)).astype(jnp.bfloat16)
-        if side == 0:
-            for copy in halves:
-                copy.wait()
-        left_high, left_low = left[0], left[1]
-        at = pl.ds(side * block, block)
-        high, low = right_high[at], right_low[at]
-        total = dot(left_high, low) + dot(left_low, high) + dot(left_high, high)
+    for copy in halves:
+        copy.wait()
+    total = dot(left[0], right_low) + dot(left[1], right_high) + dot(left[0], right_high)
+    ys, xls, window, local = own_ref.shape[:4]
+    for i, ref in enumerate((own_ref, other_ref)):
         for xl in range(xls):
             for a in range(window):
                 for y in range(ys):
-                    start = ((xl * window + a) * ys + y) * local
-                    out_ref[xl, y, a, :, side * block:(side + 1) * block] = total[start:start + local]
-
-
-def product(core, high, low, columns, ys, window, local):
-    zs, xs, width, depth = columns.shape
+                    start = i * rows + ((xl * window + a) * ys + y) * local
+                    ref[y, xl, a] = total[start:start + local]
+
+
+def product(place, high, low, columns, ys, window, local):
+    xs, width, depth = columns[0].shape
     rows = high.shape[1]
+    block = xs * len(columns) * width
+    shape = jax.ShapeDtypeStruct((ys, 2, window, local, block), jnp.float32)
     return pl.pallas_call(
         product_kernel,
-        out_shape=jax.ShapeDtypeStruct((2, ys, window, local, xs * zs * width), jnp.float32),
-        in_specs=[pl.BlockSpec(memory_space=pltpu.SMEM)] + [pl.BlockSpec(memory_space=pl.ANY)] * 3,
-        out_specs=VMEM,
+        out_shape=(shape, shape),
+        in_specs=[pl.BlockSpec(memory_space=pltpu.SMEM)]
+        + [pl.BlockSpec(memory_space=pl.ANY)] * (2 + len(columns)),
+        out_specs=(VMEM, VMEM),
         scratch_shapes=[
-            pltpu.VMEM((2, rows, depth), jnp.bfloat16),
-            pltpu.VMEM((xs, zs, width, depth), jnp.float32),
-            pltpu.VMEM((xs * zs * width, depth), jnp.bfloat16),
-            pltpu.VMEM((xs * zs * width, depth), jnp.bfloat16),
-            pltpu.SemaphoreType.DMA((xs + 2,)),
+            pltpu.VMEM((2, 2 * rows, depth), jnp.bfloat16),
+            pltpu.VMEM((len(columns), xs, width, depth), jnp.float32),
+            pltpu.VMEM((block, depth), jnp.bfloat16),
+            pltpu.VMEM((block, depth), jnp.bfloat16),
+            pltpu.SemaphoreType.DMA((len(columns) + 4,)),
         ],
-        compiler_params=pltpu.CompilerParams(vmem_limit_bytes=52 * MIB),
+        compiler_params=pltpu.CompilerParams(vmem_limit_bytes=50 * MIB),
         cost_estimate=pl.CostEstimate(
-            flops=6 * rows * depth * xs * zs * width, bytes_accessed=8 << 20, transcendentals=0
+            flops=12 * rows * depth * block, bytes_accessed=8 << 20, transcendentals=0
         ),
-    )(core, high, low, columns)
+    )(place, high, low, *columns)
+
+
+def gather(block, axis, hops, sign):
+    size = lax.axis_size(axis)
+    pairs = [(i, (i - sign) % size) for i in range(size)]
+    blocks = [block]
+    for _ in range(hops):
+        blocks.append(lax.ppermute(blocks[-1], axis, pairs))
+    return blocks[1:]
 
 
 def body(amplitudes, integrals, a_irrep, b_irrep, occ_irrep):
     window, occupied, local, virtual = amplitudes.shape
     ys = lax.axis_size("y")
     orb = lax.axis_index("y") * 2 + lax.axis_index("core")
-
-    sent = pack_integrals(integrals)
-    got = lax.all_to_all(sent, ("xh", "xl"), 0, 0, tiled=True)
-    packed = pack_amplitudes(amplitudes, 4 * ys)
-    packed, got = lax.optimization_barrier((packed, got))
-    columns = lax.all_gather(got, "z", axis=0)
-
-    packed = lax.all_to_all(packed, ("y", "core", "xl"), 0, 0, tiled=True)
-    high, low = spin_rows(packed)
-
-    core = lax.axis_index("core").astype(jnp.int32).reshape(1)
-    given = product(1 - core, high, low, columns, ys, window, local)
-    given = lax.ppermute(given, "core", [(0, 1), (1, 0)])
-    partial = product(core, high, low, columns, ys, window, local) + given
-
-    partial = partial.reshape(2 * ys, window, local, -1)
-    partial = lax.all_to_all(partial, ("xl", "y"), 0, 0, tiled=True)
-    shares = jnp.sum(partial, axis=0)
 
     local_occ = lax.dynamic_slice_in_dim(occ_irrep, orb * local, local)
     col_sym = jnp.bitwise_xor(b_irrep[:, None], occ_irrep[None, :]).reshape(-1)
     symmetry = jnp.bitwise_xor(
         jnp.bitwise_xor(a_irrep[:, None, None], local_occ[None, :, None]), col_sym[None, None, :]
     )
+
+    sent = pack_integrals(integrals)
+    got = lax.all_to_all(sent, ("xh", "xl"), 0, 0, tiled=True)
+    half = lax.axis_size("z") // 2
+    ahead = gather(got, "z", half - 1, 1)
+    behind = gather(got, "z", half - 1, -1)
+
+    packed = pack_amplitudes(amplitudes, 4 * ys)
+    packed, _ = lax.optimization_barrier((packed, got))
+    packed = lax.all_to_all(packed, ("y", "core", "xl"), 0, 0, tiled=True)
+    packed, symmetry = lax.optimization_barrier((packed, symmetry))
+    high, low = spin_rows(packed)
+    last, high, low = lax.optimization_barrier((ahead[-1], high, low))
+    ahead += gather(last, "z", 1, 1)
+
+    place = jnp.stack([lax.axis_index("z"), lax.axis_index("core")]).astype(jnp.int32)
+    columns = [got] + ahead + behind[::-1]
+    partial, given = product(place, high, low, columns, ys, window, local)
+    partial = partial + lax.ppermute(given, "core", [(0, 1), (1, 0)])
+
+    partial = partial.reshape(2 * ys, window, local, -1)
+    partial = lax.all_to_all(partial, ("y", "xl"), 0, 0, tiled=True)
+    shares = jnp.sum(partial, axis=0)
     return jnp.where(symmetry == 0, shares, jnp.float32(0.0))
 
 

time: 137 us -> 139 us (1.015)
  waiting for transfers between devices: 69 us -> 21.6 us
  starting transfers between devices: 33.2 us -> 71.6 us
  blocking collectives: 0 us -> 25.8 us
  between operations: 13.5 us -> 0.22 us
  Pallas kernels: 15.4 us -> 12.2 us
  local copies, waits for them, and re-layouts: 3.36 us -> 4.93 us
    all_to_all x1, waiting for transfers between devices: 47.3 us -> 0.01 us  [body(): packed = lax.all_to_all(packed, ('y', 'core', 'xl'), 0, 0, tiled=True)]
    ppermute x1 -> x12, starting transfers between devices: 7.02 us -> 52.8 us  [the longest x11 45.7 us: gather(): blocks.append(lax.ppermute(blocks[-1], axis, pairs))]
    all_to_all x0 -> x1, blocking collectives: none -> 25.8 us  [body(): partial = lax.all_to_all(partial, ('y', 'xl'), 0, 0, tiled=True)]
    ppermute x1 -> x12, waiting for transfers between devices: 0.01 us -> 20.3 us  [the longest x11 18.5 us: gather(): blocks.append(lax.ppermute(blocks[-1], axis, pairs))]
    all_to_all x1 -> x0, waiting for transfers between devices: 15.8 us -> none  [body(): partial = lax.all_to_all(partial, ('xl', 'y'), 0, 0, tiled=True)]
    all_to_all x1 -> x0, starting transfers between devices: 7.46 us -> none  [body(): partial = lax.all_to_all(partial, ('xl', 'y'), 0, 0, tiled=True)]
    all_gather x1 -> x0, waiting for transfers between devices: 4.33 us -> none  [body(): columns = lax.all_gather(got, 'z', axis=0)]
    pallas_call x2 -> x1, Pallas kernels: 8.93 us -> 6.71 us  [product(): pl.pallas_call(product_kernel, out_shape=(shape, shape), in_specs=[pl.Blo...]
  transfers between devices with their start and end apart: 5 -> 14, of which waited for: 4 -> 7; matrix products, arithmetic and copies ran while one was open for 0% -> 0% of each run, Pallas kernels for 7% -> 3%
where the time goes in v4:
time: 139 us; the launch traced here: 138 us
  starting transfers between devices  71.6 us (52%)
  blocking collectives  25.8 us (19%)
  waiting for transfers between devices  21.6 us (16%)
  Pallas kernels  12.2 us (9%)
  local copies, waits for them, and re-layouts  4.93 us (4%)
  other arithmetic  2.24 us (2%)
    ppermute x11, starting transfers between devices, gather(): blocks.append(lax.ppermute(blocks[-1], axis, pairs))  45.7 us
    all_to_all x1, blocking collectives, body(): partial = lax.all_to_all(partial, ('y', 'xl'), 0, 0, tiled=True)  25.8 us
    ppermute x11, waiting for transfers between devices, gather(): blocks.append(lax.ppermute(blocks[-1], axis, pairs))  18.5 us
    all_to_all x1, starting transfers between devices, body(): packed = lax.all_to_all(packed, ('y', 'core', 'xl'), 0, 0, tiled=True)  13.9 us
    ppermute x1, starting transfers between devices, body(): partial = partial + lax.ppermute(given, 'core', [(0, 1), (1, 0)])  7.12 us
    pallas_call x1, Pallas kernels, product(): pl.pallas_call(product_kernel, out_shape=(shape, shape), in_specs=[pl.Blo...  6.71 us
    all_to_all x1, starting transfers between devices, body(): got = lax.all_to_all(sent, ('xh', 'xl'), 0, 0, tiled=True)  4.84 us
    unnamed x14, local copies, waits for them, and re-layouts  4.78 us
  transfers between devices with their start and end apart: 14, of which 7 were waited for; matrix products, arithmetic and copies ran while one was open for 0% of the time, Pallas kernels for 3%

profile of v4, /device:TPU:1, one launch (start us, length us, event | category | flops | bytes accessed | tf_op | source)
XLA Modules:
  0.0 138.5 jit_solution(325874161608359891)
XLA Ops:
  0.0 1.8 %shard_map.56 = f32[4,16,1280]{2,1,0:T(8,128)} custom-call(f32[40,16,64]{2,1,0:T(8,128)} %bitcast.5), custom_call_target="tpu_custom_call" | custom-call | tf_op jit(solution)/shard_map/pallas_call | solution.py:25
  1.8 4.8 %all-to-all-start = ((f32[4,16,1280]{2,1,0:T(8,128)}), f32[4,16,1280]{2,1,0:T(8,128)S(1)}, u32[]{:S(2)}, u32[]{:S(2)}) async-start(f32[4,16,1280]{2,1,0:T(8,128)} %shard_map.56), calls=%async_computation | async-start | bytes 655360 | tf_op jit(solution)/shard_map/all_to_all | solution.py:212
  6.7 1.5 %copy-done.1 = f32[3,64,4,640]{3,2,1,0:T(4,128)S(1)} copy-done((f32[3,64,4,640]{3,2,1,0:T(4,128)S(1)}, f32[3,64,4,640]{3,2,1,0:T(4,128)}, u32[]{:S(2)}) %copy-start.1) | copy-done | bytes 1966104
  8.2 1.7 %shard_map.55 = f32[32,3,40,128]{3,2,1,0:T(8,128)S(1)} custom-call(f32[3,64,4,640]{3,2,1,0:T(4,128)S(1)} %copy-done.1), custom_call_target="tpu_custom_call" | custom-call | bytes 3932160 | tf_op jit(solution)/shard_map/pallas_call | solution.py:58
  9.9 0.0 copy-start
  10.0 1.3 copy-done
  11.3 1.3 all-to-all-done.refs_0_
  12.5 13.9 %all-to-all-start.1 = ((f32[32,3,40,128]{3,2,1,0:T(8,128)}), f32[32,3,40,128]{3,2,1,0:T(8,128)S(1)}, u32[]{:S(2)}, u32[]{:S(2)}) async-start(f32[32,3,40,128]{3,2,1,0:T(8,128)} %copy-done), calls=%async_computation.1 | async-start | bytes 3932160 | tf_op jit(solution)/shard_map/all_to_all | solution.py:219
  26.4 10.1 %collective-permute-start = (f32[4,16,1280]{2,1,0:T(8,128)S(1)}, f32[4,16,1280]{2,1,0:T(8,128)S(1)}, u32[]{:S(2)}, u32[]{:S(2)}) collective-permute-start(f32[4,16,1280]{2,1,0:T(8,128)S(1)} %all-to-all-done.refs_0_), channel_id=1, source_target_pairs={{0,176},{16,0},{32,16},{48,32},{64,48},{80,64},{96,80},{112,96},{1... | collective-permute-start | bytes 983048 | tf_op jit(solution)/shard_map/ppermute | solution.py:196
  36.6 1.9 %collective-permute-start.6 = (f32[4,16,1280]{2,1,0:T(8,128)S(1)}, f32[4,16,1280]{2,1,0:T(8,128)S(1)}, u32[]{:S(2)}, u32[]{:S(2)}) collective-permute-start(f32[4,16,1280]{2,1,0:T(8,128)S(1)} %all-to-all-done.refs_0_), channel_id=1, source_target_pairs={{0,16},{16,32},{32,48},{48,64},{64,80},{80,96},{96,112},{112,128},... | collective-permute-start | bytes 983048 | tf_op jit(solution)/shard_map/ppermute | solution.py:196
  38.5 4.9 %collective-permute-done.refs_1_ = f32[4,16,1280]{2,1,0:T(8,128)S(1)} collective-permute-done((f32[4,16,1280]{2,1,0:T(8,128)S(1)}, f32[4,16,1280]{2,1,0:T(8,128)S(1)}, u32[]{:S(2)}, u32[]{:S(2)}) %collective-permute-start) | collective-permute-done | bytes 327712 | tf_op jit(solution)/shard_map/ppermute | solution.py:196
  43.4 5.3 %collective-permute-start.1 = (f32[4,16,1280]{2,1,0:T(8,128)S(1)}, f32[4,16,1280]{2,1,0:T(8,128)S(1)}, u32[]{:S(2)}, u32[]{:S(2)}) collective-permute-start(f32[4,16,1280]{2,1,0:T(8,128)S(1)} %collective-permute-done.refs_1_), channel_id=1, source_target_pairs={{0,176},{16,0},{32,16},{48,32},{64,48},{80,64},{96,80},{112,96},{1... | collective-permute-start | bytes 983048 | tf_op jit(solution)/shard_map/ppermute | solution.py:196
  48.7 0.0 collective-permute-done.6.refs_11_
  48.7 1.9 %collective-permute-start.7 = (f32[4,16,1280]{2,1,0:T(8,128)S(1)}, f32[4,16,1280]{2,1,0:T(8,128)}, u32[]{:S(2)}, u32[]{:S(2)}) collective-permute-start(f32[4,16,1280]{2,1,0:T(8,128)S(1)} %collective-permute-done.6.refs_11_), channel_id=1, source_target_pairs={{0,16},{16,32},{32,48},{48,64},{64,80},{80,96},{96,112},{112,128},... | collective-permute-start | bytes 983048 | tf_op jit(solution)/shard_map/ppermute | solution.py:196
  50.7 4.0 %collective-permute-done.1.refs_2_ = f32[4,16,1280]{2,1,0:T(8,128)S(1)} collective-permute-done((f32[4,16,1280]{2,1,0:T(8,128)S(1)}, f32[4,16,1280]{2,1,0:T(8,128)S(1)}, u32[]{:S(2)}, u32[]{:S(2)}) %collective-permute-start.1) | collective-permute-done | bytes 327712 | tf_op jit(solution)/shard_map/ppermute | solution.py:196
  54.7 5.3 %collective-permute-start.2 = (f32[4,16,1280]{2,1,0:T(8,128)S(1)}, f32[4,16,1280]{2,1,0:T(8,128)}, u32[]{:S(2)}, u32[]{:S(2)}) collective-permute-start(f32[4,16,1280]{2,1,0:T(8,128)S(1)} %collective-permute-done.1.refs_2_), channel_id=1, source_target_pairs={{0,176},{16,0},{32,16},{48,32},{64,48},{80,64},{96,80},{112,96},{1... | collective-permute-start | bytes 983048 | tf_op jit(solution)/shard_map/ppermute | solution.py:196
  60.0 0.0 collective-permute-done.7.refs_10_
  60.0 1.9 %collective-permute-start.8 = (f32[4,16,1280]{2,1,0:T(8,128)}, f32[4,16,1280]{2,1,0:T(8,128)}, u32[]{:S(2)}, u32[]{:S(2)}) collective-permute-start(f32[4,16,1280]{2,1,0:T(8,128)} %collective-permute-done.7.refs_10_), channel_id=1, source_target_pairs={{0,16},{16,32},{32,48},{48,64},{64,80},{80,96},{96,112},{112,128},... | collective-permute-start | bytes 983048 | tf_op jit(solution)/shard_map/ppermute | solution.py:196
  61.9 3.1 %collective-permute-done.2.refs_3_ = f32[4,16,1280]{2,1,0:T(8,128)} collective-permute-done((f32[4,16,1280]{2,1,0:T(8,128)S(1)}, f32[4,16,1280]{2,1,0:T(8,128)}, u32[]{:S(2)}, u32[]{:S(2)}) %collective-permute-start.2) | collective-permute-done | bytes 327712 | tf_op jit(solution)/shard_map/ppermute | solution.py:196
  65.0 5.4 %collective-permute-start.3 = (f32[4,16,1280]{2,1,0:T(8,128)}, f32[4,16,1280]{2,1,0:T(8,128)}, u32[]{:S(2)}, u32[]{:S(2)}) collective-permute-start(f32[4,16,1280]{2,1,0:T(8,128)} %collective-permute-done.2.refs_3_), channel_id=1, source_target_pairs={{0,176},{16,0},{32,16},{48,32},{64,48},{80,64},{96,80},{112,96},{1... | collective-permute-start | bytes 983048 | tf_op jit(solution)/shard_map/ppermute | solution.py:196
  70.4 0.0 copy-done.4
  70.4 0.1 dynamic_slice.3
  70.5 0.1 broadcast_xor_fusion.1
  70.6 0.0 collective-permute-done.8.refs_9_
  70.6 1.9 %collective-permute-start.9 = (f32[4,16,1280]{2,1,0:T(8,128)}, f32[4,16,1280]{2,1,0:T(8,128)}, u32[]{:S(2)}, u32[]{:S(2)}) collective-permute-start(f32[4,16,1280]{2,1,0:T(8,128)} %collective-permute-done.8.refs_9_), channel_id=1, source_target_pairs={{0,16},{16,32},{32,48},{48,64},{64,80},{80,96},{96,112},{112,128},... | collective-permute-start | bytes 983048 | tf_op jit(solution)/shard_map/ppermute | solution.py:196
  72.5 2.2 %collective-permute-done.3.refs_4_ = f32[4,16,1280]{2,1,0:T(8,128)} collective-permute-done((f32[4,16,1280]{2,1,0:T(8,128)}, f32[4,16,1280]{2,1,0:T(8,128)}, u32[]{:S(2)}, u32[]{:S(2)}) %collective-permute-start.3) | collective-permute-done | bytes 327712 | tf_op jit(solution)/shard_map/ppermute | solution.py:196
  74.7 5.4 %collective-permute-start.4 = (f32[4,16,1280]{2,1,0:T(8,128)}, f32[4,16,1280]{2,1,0:T(8,128)}, u32[]{:S(2)}, u32[]{:S(2)}) collective-permute-start(f32[4,16,1280]{2,1,0:T(8,128)} %collective-permute-done.3.refs_4_), channel_id=1, source_target_pairs={{0,176},{16,0},{32,16},{48,32},{64,48},{80,64},{96,80},{112,96},{1... | collective-permute-start | bytes 983048 | tf_op jit(solution)/shard_map/ppermute | solution.py:196
  80.1 0.1 broadcast_xor_fusion.2
  80.2 0.1 xor.58
  80.3 0.1 broadcast_xor_fusion
  80.4 0.0 collective-permute-done.9.refs_8_
  80.4 1.9 %collective-permute-start.10 = (f32[4,16,1280]{2,1,0:T(8,128)}, f32[4,16,1280]{2,1,0:T(8,128)}, u32[]{:S(2)}, u32[]{:S(2)}) collective-permute-start(f32[4,16,1280]{2,1,0:T(8,128)} %collective-permute-done.9.refs_8_), channel_id=1, source_target_pairs={{0,16},{16,32},{32,48},{48,64},{64,80},{80,96},{96,112},{112,128},... | collective-permute-start | bytes 983048 | tf_op jit(solution)/shard_map/ppermute | solution.py:196
  82.3 0.0 all-to-all-done.1.in_ref
  82.3 1.9 %shard_map.57 = (bf16[2,192,1280]{2,1,0:T(8,128)(2,1)S(1)}, bf16[2,192,1280]{2,1,0:T(8,128)(2,1)S(1)}) custom-call(f32[32,3,40,128]{3,2,1,0:T(8,128)S(1)} %all-to-all-done.1.in_ref), custom_call_target="tpu_custom_call" | custom-call | bytes 3932160 | tf_op jit(solution)/shard_map/pallas_call | solution.py:110
  84.2 1.0 copy-done.2
  85.2 1.0 copy-done.3
  86.1 0.0 collective-permute-done.4.refs_5_
  86.1 4.6 %collective-permute-start.5 = (f32[4,16,1280]{2,1,0:T(8,128)}, f32[4,16,1280]{2,1,0:T(8,128)S(1)}, u32[]{:S(2)}, u32[]{:S(2)}) collective-permute-start(f32[4,16,1280]{2,1,0:T(8,128)} %collective-permute-done.4.refs_5_), channel_id=1, source_target_pairs={{0,176},{16,0},{32,16},{48,32},{64,48},{80,64},{96,80},{112,96},{1... | collective-permute-start | bytes 983048 | tf_op jit(solution)/shard_map/ppermute | solution.py:196
  90.7 0.1 pad_add_fusion.place_ref
  90.8 0.0 collective-permute-done.10.refs_7_
  90.8 4.2 %collective-permute-done.5.refs_6_ = f32[4,16,1280]{2,1,0:T(8,128)S(1)} collective-permute-done((f32[4,16,1280]{2,1,0:T(8,128)}, f32[4,16,1280]{2,1,0:T(8,128)S(1)}, u32[]{:S(2)}, u32[]{:S(2)}) %collective-permute-start.5) | collective-permute-done | bytes 327712 | tf_op jit(solution)/shard_map/ppermute | solution.py:196
  95.0 6.7 %shard_map.58 = (f32[8,2,3,4,768]{4,3,2,1,0:T(4,128)}, f32[8,2,3,4,768]{4,3,2,1,0:T(4,128)}) custom-call(s32[2]{0:T(128)S(1)} %pad_add_fusion.place_ref, bf16[2,192,1280]{2,1,0:T(8,128)(2,1)} %copy-done.2, bf16[2,192,1280]{2,1,0:T(8,128)(2,1)} %copy-done.3, f32[4,16,1280]{2,1,0:T(8,128)S(1)} %all-to-all-done.refs_0_, ...), custom_call_target="tpu_custom_call" | custom-call | flops 2264924160 | bytes 8388608 | tf_op jit(solution)/shard_map/pallas_call | solution.py:171
  101.8 7.1 %collective-permute-start.11 = (f32[8,2,3,4,768]{4,3,2,1,0:T(4,128)}, f32[8,2,3,4,768]{4,3,2,1,0:T(4,128)S(1)}, u32[]{:S(2)}, u32[]{:S(2)}) collective-permute-start(f32[8,2,3,4,768]{4,3,2,1,0:T(4,128)} %get-tuple-element.24), channel_id=1, source_target_pairs={{0,1},{1,0},{2,3},{3,2},{4,5},{5,4},{6,7},{7,6},{8,9},{9,8},{10,11... | collective-permute-start | bytes 1769480 | tf_op jit(solution)/shard_map/ppermute | solution.py:228
  108.9 1.8 %collective-permute-done.11 = f32[8,2,3,4,768]{4,3,2,1,0:T(4,128)S(1)} collective-permute-done((f32[8,2,3,4,768]{4,3,2,1,0:T(4,128)}, f32[8,2,3,4,768]{4,3,2,1,0:T(4,128)S(1)}, u32[]{:S(2)}, u32[]{:S(2)}) %collective-permute-start.11) | collective-permute-done | bytes 589856 | tf_op jit(solution)/shard_map/ppermute | solution.py:228
  110.7 1.2 add.11
  111.9 25.8 %all_to_all.15 = f32[16,3,4,768]{3,2,1,0:T(4,128)S(1)} all-to-all(f32[16,3,4,768]{3,2,1,0:T(4,128)S(1)} %bitcast.4), channel_id=1, replica_groups=mesh['xh'=2,'xl'=2,'z'=12,'y'=8,'core'=2] {'y','xl'}, dimensions={0} | all-to-all | bytes 1179648 | tf_op jit(solution)/shard_map/all_to_all | solution.py:231
  137.7 0.1 reduce_sum.9
  137.8 0.6 compare_select_fusion
  (8 shorter events, 0.0 us)
Async XLA Ops:
  1.8 10.7 %all-to-all-start = ((f32[4,16,1280]{2,1,0:T(8,128)}), f32[4,16,1280]{2,1,0:T(8,128)S(1)}, u32[]{:S(2)}, u32[]{:S(2)}) async-start(f32[4,16,1280]{2,1,0:T(8,128)} %shard_map.56), calls=%async_computation | async-start | bytes 655360 | tf_op jit(solution)/shard_map/all_to_all | solution.py:212
  6.6 1.5 %copy-start.1 = (f32[3,64,4,640]{3,2,1,0:T(4,128)S(1)}, f32[3,64,4,640]{3,2,1,0:T(4,128)}, u32[]{:S(2)}) copy-start(f32[3,64,4,640]{3,2,1,0:T(4,128)} %in_ref.1) | copy-start | bytes 5898244
  9.9 1.3 copy-start
  11.2 59.2 %copy-start.4 = (s32[64]{0:T(128)S(1)}, s32[64]{0:T(128)}, u32[]{:S(2)}) copy-start(s32[64]{0:T(128)} %param.9) | copy-start | bytes 772
  11.2 59.3 %copy-start.5 = (s32[12]{0:T(128)S(1)}, s32[12]{0:T(128)}, u32[]{:S(2)}) copy-start(s32[12]{0:T(128)} %param.8) | copy-start | bytes 148
  11.3 68.9 %copy-start.6 = (s32[3]{0:T(128)S(1)}, s32[3]{0:T(128)}, u32[]{:S(2)}) copy-start(s32[3]{0:T(128)} %param.7) | copy-start | bytes 40
  12.5 69.8 %all-to-all-start.1 = ((f32[32,3,40,128]{3,2,1,0:T(8,128)}), f32[32,3,40,128]{3,2,1,0:T(8,128)S(1)}, u32[]{:S(2)}, u32[]{:S(2)}) async-start(f32[32,3,40,128]{3,2,1,0:T(8,128)} %copy-done), calls=%async_computation.1 | async-start | bytes 3932160 | tf_op jit(solution)/shard_map/all_to_all | solution.py:219
  26.4 17.0 %collective-permute-start = (f32[4,16,1280]{2,1,0:T(8,128)S(1)}, f32[4,16,1280]{2,1,0:T(8,128)S(1)}, u32[]{:S(2)}, u32[]{:S(2)}) collective-permute-start(f32[4,16,1280]{2,1,0:T(8,128)S(1)} %all-to-all-done.refs_0_), channel_id=1, source_target_pairs={{0,176},{16,0},{32,16},{48,32},{64,48},{80,64},{96,80},{112,96},{1... | collective-permute-start | bytes 983048 | tf_op jit(solution)/shard_map/ppermute | solution.py:196
  36.6 12.2 %collective-permute-start.6 = (f32[4,16,1280]{2,1,0:T(8,128)S(1)}, f32[4,16,1280]{2,1,0:T(8,128)S(1)}, u32[]{:S(2)}, u32[]{:S(2)}) collective-permute-start(f32[4,16,1280]{2,1,0:T(8,128)S(1)} %all-to-all-done.refs_0_), channel_id=1, source_target_pairs={{0,16},{16,32},{32,48},{48,64},{64,80},{80,96},{96,112},{112,128},... | collective-permute-start | bytes 983048 | tf_op jit(solution)/shard_map/ppermute | solution.py:196
  43.4 11.2 %collective-permute-start.1 = (f32[4,16,1280]{2,1,0:T(8,128)S(1)}, f32[4,16,1280]{2,1,0:T(8,128)S(1)}, u32[]{:S(2)}, u32[]{:S(2)}) collective-permute-start(f32[4,16,1280]{2,1,0:T(8,128)S(1)} %collective-permute-done.refs_1_), channel_id=1, source_target_pairs={{0,176},{16,0},{32,16},{48,32},{64,48},{80,64},{96,80},{112,96},{1... | collective-permute-start | bytes 983048 | tf_op jit(solution)/shard_map/ppermute | solution.py:196
  48.7 11.2 %collective-permute-start.7 = (f32[4,16,1280]{2,1,0:T(8,128)S(1)}, f32[4,16,1280]{2,1,0:T(8,128)}, u32[]{:S(2)}, u32[]{:S(2)}) collective-permute-start(f32[4,16,1280]{2,1,0:T(8,128)S(1)} %collective-permute-done.6.refs_11_), channel_id=1, source_target_pairs={{0,16},{16,32},{32,48},{48,64},{64,80},{80,96},{96,112},{112,128},... | collective-permute-start | bytes 983048 | tf_op jit(solution)/shard_map/ppermute | solution.py:196
  54.7 10.3 %collective-permute-start.2 = (f32[4,16,1280]{2,1,0:T(8,128)S(1)}, f32[4,16,1280]{2,1,0:T(8,128)}, u32[]{:S(2)}, u32[]{:S(2)}) collective-permute-start(f32[4,16,1280]{2,1,0:T(8,128)S(1)} %collective-permute-done.1.refs_2_), channel_id=1, source_target_pairs={{0,176},{16,0},{32,16},{48,32},{64,48},{80,64},{96,80},{112,96},{1... | collective-permute-start | bytes 983048 | tf_op jit(solution)/shard_map/ppermute | solution.py:196
  60.0 10.6 %collective-permute-start.8 = (f32[4,16,1280]{2,1,0:T(8,128)}, f32[4,16,1280]{2,1,0:T(8,128)}, u32[]{:S(2)}, u32[]{:S(2)}) collective-permute-start(f32[4,16,1280]{2,1,0:T(8,128)} %collective-permute-done.7.refs_10_), channel_id=1, source_target_pairs={{0,16},{16,32},{32,48},{48,64},{64,80},{80,96},{96,112},{112,128},... | collective-permute-start | bytes 983048 | tf_op jit(solution)/shard_map/ppermute | solution.py:196
  65.0 9.7 %collective-permute-start.3 = (f32[4,16,1280]{2,1,0:T(8,128)}, f32[4,16,1280]{2,1,0:T(8,128)}, u32[]{:S(2)}, u32[]{:S(2)}) collective-permute-start(f32[4,16,1280]{2,1,0:T(8,128)} %collective-permute-done.2.refs_3_), channel_id=1, source_target_pairs={{0,176},{16,0},{32,16},{48,32},{64,48},{80,64},{96,80},{112,96},{1... | collective-permute-start | bytes 983048 | tf_op jit(solution)/shard_map/ppermute | solution.py:196
  70.6 9.8 %collective-permute-start.9 = (f32[4,16,1280]{2,1,0:T(8,128)}, f32[4,16,1280]{2,1,0:T(8,128)}, u32[]{:S(2)}, u32[]{:S(2)}) collective-permute-start(f32[4,16,1280]{2,1,0:T(8,128)} %collective-permute-done.8.refs_9_), channel_id=1, source_target_pairs={{0,16},{16,32},{32,48},{48,64},{64,80},{80,96},{96,112},{112,128},... | collective-permute-start | bytes 983048 | tf_op jit(solution)/shard_map/ppermute | solution.py:196
  74.7 11.4 %collective-permute-start.4 = (f32[4,16,1280]{2,1,0:T(8,128)}, f32[4,16,1280]{2,1,0:T(8,128)}, u32[]{:S(2)}, u32[]{:S(2)}) collective-permute-start(f32[4,16,1280]{2,1,0:T(8,128)} %collective-permute-done.3.refs_4_), channel_id=1, source_target_pairs={{0,176},{16,0},{32,16},{48,32},{64,48},{80,64},{96,80},{112,96},{1... | collective-permute-start | bytes 983048 | tf_op jit(solution)/shard_map/ppermute | solution.py:196
  80.4 10.4 %collective-permute-start.10 = (f32[4,16,1280]{2,1,0:T(8,128)}, f32[4,16,1280]{2,1,0:T(8,128)}, u32[]{:S(2)}, u32[]{:S(2)}) collective-permute-start(f32[4,16,1280]{2,1,0:T(8,128)} %collective-permute-done.9.refs_8_), channel_id=1, source_target_pairs={{0,16},{16,32},{32,48},{48,64},{64,80},{80,96},{96,112},{112,128},... | collective-permute-start | bytes 983048 | tf_op jit(solution)/shard_map/ppermute | solution.py:196
  84.2 1.0 copy-start.2
  85.2 1.0 copy-start.3
  86.1 8.9 %collective-permute-start.5 = (f32[4,16,1280]{2,1,0:T(8,128)}, f32[4,16,1280]{2,1,0:T(8,128)S(1)}, u32[]{:S(2)}, u32[]{:S(2)}) collective-permute-start(f32[4,16,1280]{2,1,0:T(8,128)} %collective-permute-done.4.refs_5_), channel_id=1, source_target_pairs={{0,176},{16,0},{32,16},{48,32},{64,48},{80,64},{96,80},{112,96},{1... | collective-permute-start | bytes 983048 | tf_op jit(solution)/shard_map/ppermute | solution.py:196
  101.8 8.9 %collective-permute-start.11 = (f32[8,2,3,4,768]{4,3,2,1,0:T(4,128)}, f32[8,2,3,4,768]{4,3,2,1,0:T(4,128)S(1)}, u32[]{:S(2)}, u32[]{:S(2)}) collective-permute-start(f32[8,2,3,4,768]{4,3,2,1,0:T(4,128)} %get-tuple-element.24), channel_id=1, source_target_pairs={{0,1},{1,0},{2,3},{3,2},{4,5},{5,4},{6,7},{7,6},{8,9},{9,8},{10,11... | collective-permute-start | bytes 1769480 | tf_op jit(solution)/shard_map/ppermute | solution.py:228

commit v5 on v4

--- a/solution.py
+++ b/solution.py
@@ -118,52 +118,57 @@
     )(got)
 
 
-def product_kernel(place_ref, high_ref, low_ref, *refs):
+def product_kernel(core_ref, high_ref, low_ref, *refs):
     *columns_refs, own_ref, other_ref, left, right, right_high, right_low, sems = refs
-    zs = len(columns_refs)
-    xs, width = columns_refs[0].shape[:2]
-    z, core = place_ref[0], place_ref[1]
+    count = len(columns_refs)
+    xs, width, depth = columns_refs[0].shape
+    core = core_ref[0]
     rows = high_ref.shape[1]
     copies = [
         pltpu.make_async_copy(ref, right.at[r], sems.at[r]) for r, ref in enumerate(columns_refs)
     ]
     halves = [
         pltpu.make_async_copy(
-            ref.at[side], left.at[i, pl.ds(part * rows, rows)], sems.at[zs + 2 * i + part]
+            ref.at[side], left.at[i, pl.ds(part * rows, rows)], sems.at[count + 2 * i + part]
         )
         for i, ref in enumerate((high_ref, low_ref))
         for part, side in enumerate((core, 1 - core))
     ]
-    for copy in copies + halves:
+    for copy in copies[:2] + halves + copies[2:]:
         copy.start()
-    for r in range(zs):
-        copies[r].wait()
-        at_z = lax.rem(z + r, zs)
-        for x in range(xs):
-            at = pl.ds(pl.multiple_of((x * zs + at_z) * width, width), width)
-            block = right[r, x]
+
+    def dot(left, right):
+        return lax.dot_general(
+            left, right, (((1,), (1,)), ((), ())), preferred_element_type=jnp.float32
+        )
+
+    ys, xls, window, local = own_ref.shape[:4]
+    group = 4
+    for first in range(0, count, group):
+        for r in range(first, first + group):
+            copies[r].wait()
+            block = right[r].reshape(xs * width, depth)
             high = block.astype(jnp.bfloat16)
+            at = pl.ds(r * xs * width, xs * width)
             right_high[at] = high
             right_low[at] = (block - high.astype(jnp.float32)).astype(jnp.bfloat16)
-
-    def dot(left, right):
-        return lax.dot_general(
-            left, right[...], (((1,), (1,)), ((), ())), preferred_element_type=jnp.float32
-        )
-
-    for copy in halves:
-        copy.wait()
-    total = dot(left[0], right_low) + dot(left[1], right_high) + dot(left[0], right_high)
-    ys, xls, window, local = own_ref.shape[:4]
-    for i, ref in enumerate((own_ref, other_ref)):
-        for xl in range(xls):
-            for a in range(window):
-                for y in range(ys):
-                    start = i * rows + ((xl * window + a) * ys + y) * local
-                    ref[y, xl, a] = total[start:start + local]
-
-
-def product(place, high, low, columns, ys, window, local):
+        if first == 0:
+            for copy in halves:
+                copy.wait()
+        at = pl.ds(first * xs * width, group * xs * width)
+        high, low = right_high[at], right_low[at]
+        total = dot(left[0], low) + dot(left[1], high) + dot(left[0], high)
+        for i, ref in enumerate((own_ref, other_ref)):
+            for xl in range(xls):
+                for a in range(window):
+                    for y in range(ys):
+                        start = i * rows + ((xl * window + a) * ys + y) * local
+                        ref[y, xl, a, :, first * xs * width:(first + group) * xs * width] = total[
+                            start:start + local
+                        ]
+
+
+def product(core, high, low, columns, ys, window, local):
     xs, width, depth = columns[0].shape
     rows = high.shape[1]
     block = xs * len(columns) * width
@@ -181,11 +186,47 @@
             pltpu.VMEM((block, depth), jnp.bfloat16),
             pltpu.SemaphoreType.DMA((len(columns) + 4,)),
         ],
-        compiler_params=pltpu.CompilerParams(vmem_limit_bytes=50 * MIB),
+        compiler_params=pltpu.CompilerParams(vmem_limit_bytes=53 * MIB),
         cost_estimate=pl.CostEstimate(
             flops=12 * rows * depth * block, bytes_accessed=8 << 20, transcendentals=0
         ),
-    )(place, high, low, *columns)
+    )(core, high, low, *columns)
+
+
+def finish_kernel(z_ref, parts_ref, symmetry_ref, out_ref, rows):
+    sources, window, local, columns = parts_ref.shape
+    zs = 12
+    width = columns // zs
+    for a in range(window):
+        total = parts_ref[0, a]
+        for source in range(1, sources):
+            total = total + parts_ref[source, a]
+        rows[pl.ds(a * local, local), :] = total
+    turned = pltpu.roll(rows[...], lax.rem(z_ref[0] + zs - 4, zs) * width, 1)
+    ordered = jnp.concatenate(
+        [
+            turned[:, z * width + x * 16:z * width + (x + 1) * 16]
+            for x in range(width // 16)
+            for z in range(zs)
+        ],
+        axis=1,
+    )
+    for a in range(window):
+        out_ref[a] = jnp.where(
+            symmetry_ref[a] == 0, ordered[a * local:(a + 1) * local], jnp.float32(0.0)
+        )
+
+
+def finish(z, parts, symmetry):
+    _, window, local, columns = parts.shape
+    return pl.pallas_call(
+        finish_kernel,
+        out_shape=jax.ShapeDtypeStruct((window, local, columns), jnp.float32),
+        in_specs=[pl.BlockSpec(memory_space=pltpu.SMEM), VMEM, VMEM],
+        out_specs=VMEM,
+        scratch_shapes=[pltpu.VMEM((16, columns), jnp.float32)],
+        compiler_params=pltpu.CompilerParams(vmem_limit_bytes=8 * MIB),
+    )(z, parts, symmetry)
 
 
 def gather(block, axis, hops, sign):
@@ -222,15 +263,19 @@
     last, high, low = lax.optimization_barrier((ahead[-1], high, low))
     ahead += gather(last, "z", 1, 1)
 
-    place = jnp.stack([lax.axis_index("z"), lax.axis_index("core")]).astype(jnp.int32)
-    columns = [got] + ahead + behind[::-1]
-    partial, given = product(place, high, low, columns, ys, window, local)
-    partial = partial + lax.ppermute(given, "core", [(0, 1), (1, 0)])
+    core = lax.axis_index("core").astype(jnp.int32).reshape(1)
+    swap = [(0, 1), (1, 0)]
+    early = behind[3::-1] + [got] + ahead[:3]
+    late = ahead[3:] + behind[4:]
+    own, given = product(core, high, low, early, ys, window, local)
+    taken = lax.ppermute(given, "core", swap)
+    own_late, given = product(core, high, low, late, ys, window, local)
+    partial = jnp.concatenate([own + taken, own_late + lax.ppermute(given, "core", swap)], axis=-1)
 
     partial = partial.reshape(2 * ys, window, local, -1)
     partial = lax.all_to_all(partial, ("y", "xl"), 0, 0, tiled=True)
-    shares = jnp.sum(partial, axis=0)
-    return jnp.where(symmetry == 0, shares, jnp.float32(0.0))
+    z = lax.axis_index("z").astype(jnp.int32).reshape(1)
+    return finish(z, partial, symmetry)
 
 
 def solution(mesh):

time: 139 us -> 138 us (level)
  blocking collectives: 25.8 us -> 0 us
  waiting for transfers between devices: 21.6 us -> 34.1 us
  starting transfers between devices: 71.6 us -> 80.1 us
  Pallas kernels: 12.2 us -> 15.6 us
    all_to_all x1 -> x0, blocking collectives: 25.8 us -> none  [body(): partial = lax.all_to_all(partial, ('y', 'xl'), 0, 0, tiled=True)]
    all_to_all x0 -> x1, waiting for transfers between devices: none -> 17.4 us  [body(): partial = lax.all_to_all(partial, ('y', 'xl'), 0, 0, tiled=True)]
    all_to_all x0 -> x1, starting transfers between devices: none -> 7.15 us  [body(): partial = lax.all_to_all(partial, ('y', 'xl'), 0, 0, tiled=True)]
    ppermute x11, waiting for transfers between devices: 18.5 us -> 14.2 us  [gather(): blocks.append(lax.ppermute(blocks[-1], axis, pairs))]
    pallas_call x1 -> x2, Pallas kernels: 6.71 us -> 9.33 us  [product(): pl.pallas_call(product_kernel, out_shape=(shape, shape), in_specs=[pl.Blo...]
    ppermute x1 -> x2, starting transfers between devices: 7.12 us -> 8.61 us  [the longest x1 6.69 us: body(): taken = lax.ppermute(given, 'core', swap)]
    unnamed x14 -> x30, local copies, waits for them, and re-layouts: 4.78 us -> 5.47 us
  transfers between devices with their start and end apart: 14 -> 16, of which waited for: 7 -> 7; matrix products, arithmetic and copies ran while one was open for 0% -> 0% of each run, Pallas kernels for 3% -> 9%
where the time goes in v5:
time: 138 us; the launch traced here: 137 us
  starting transfers between devices  80.1 us (58%)
  waiting for transfers between devices  34.1 us (25%)
  Pallas kernels  15.6 us (11%)
  local copies, waits for them, and re-layouts  5.62 us (4%)
    ppermute x11, starting transfers between devices, gather(): blocks.append(lax.ppermute(blocks[-1], axis, pairs))  45.6 us
    all_to_all x1, waiting for transfers between devices, body(): partial = lax.all_to_all(partial, ('y', 'xl'), 0, 0, tiled=True)  17.4 us
    ppermute x11, waiting for transfers between devices, gather(): blocks.append(lax.ppermute(blocks[-1], axis, pairs))  14.2 us
    all_to_all x1, starting transfers between devices, body(): packed = lax.all_to_all(packed, ('y', 'core', 'xl'), 0, 0, tiled=True)  13.9 us
    pallas_call x2, Pallas kernels, product(): pl.pallas_call(product_kernel, out_shape=(shape, shape), in_specs=[pl.Blo...  9.33 us
    all_to_all x1, starting transfers between devices, body(): partial = lax.all_to_all(partial, ('y', 'xl'), 0, 0, tiled=True)  7.15 us
    ppermute x1, starting transfers between devices, body(): taken = lax.ppermute(given, 'core', swap)  6.69 us
    unnamed x30, local copies, waits for them, and re-layouts  5.47 us
  transfers between devices with their start and end apart: 16, of which 7 were waited for; matrix products, arithmetic and copies ran while one was open for 0% of the time, Pallas kernels for 9%

profile of v5, /device:TPU:1, one launch (start us, length us, event | category | flops | bytes accessed | tf_op | source)
XLA Modules:
  0.0 137.2 jit_solution(15005875781726705020)
XLA Ops:
  0.0 1.8 %shard_map.55 = f32[4,16,1280]{2,1,0:T(8,128)} custom-call(f32[40,16,64]{2,1,0:T(8,128)} %bitcast.4), custom_call_target="tpu_custom_call" | custom-call | tf_op jit(solution)/shard_map/pallas_call | solution.py:25
  1.8 4.8 %all-to-all-start = ((f32[4,16,1280]{2,1,0:T(8,128)}), f32[4,16,1280]{2,1,0:T(8,128)S(1)}, u32[]{:S(2)}, u32[]{:S(2)}) async-start(f32[4,16,1280]{2,1,0:T(8,128)} %shard_map.55), calls=%async_computation | async-start | bytes 655360 | tf_op jit(solution)/shard_map/all_to_all | solution.py:253
  6.7 1.5 %copy-done.1 = f32[3,64,4,640]{3,2,1,0:T(4,128)S(1)} copy-done((f32[3,64,4,640]{3,2,1,0:T(4,128)S(1)}, f32[3,64,4,640]{3,2,1,0:T(4,128)}, u32[]{:S(2)}) %copy-start.1) | copy-done | bytes 1966104
  8.2 1.7 %shard_map.56 = f32[32,3,40,128]{3,2,1,0:T(8,128)S(1)} custom-call(f32[3,64,4,640]{3,2,1,0:T(4,128)S(1)} %copy-done.1), custom_call_target="tpu_custom_call" | custom-call | bytes 3932160 | tf_op jit(solution)/shard_map/pallas_call | solution.py:58
  10.0 1.3 copy-done
  11.3 1.3 all-to-all-done.refs_4_
  12.5 13.9 %all-to-all-start.1 = ((f32[32,3,40,128]{3,2,1,0:T(8,128)}), f32[32,3,40,128]{3,2,1,0:T(8,128)S(1)}, u32[]{:S(2)}, u32[]{:S(2)}) async-start(f32[32,3,40,128]{3,2,1,0:T(8,128)} %copy-done), calls=%async_computation.1 | async-start | bytes 3932160 | tf_op jit(solution)/shard_map/all_to_all | solution.py:260
  26.5 10.1 %collective-permute-start = (f32[4,16,1280]{2,1,0:T(8,128)S(1)}, f32[4,16,1280]{2,1,0:T(8,128)S(1)}, u32[]{:S(2)}, u32[]{:S(2)}) collective-permute-start(f32[4,16,1280]{2,1,0:T(8,128)S(1)} %all-to-all-done.refs_4_), channel_id=1, source_target_pairs={{0,176},{16,0},{32,16},{48,32},{64,48},{80,64},{96,80},{112,96},{1... | collective-permute-start | bytes 983048 | tf_op jit(solution)/shard_map/ppermute | solution.py:237
  36.6 1.9 %collective-permute-start.5 = (f32[4,16,1280]{2,1,0:T(8,128)S(1)}, f32[4,16,1280]{2,1,0:T(8,128)S(1)}, u32[]{:S(2)}, u32[]{:S(2)}) collective-permute-start(f32[4,16,1280]{2,1,0:T(8,128)S(1)} %all-to-all-done.refs_4_), channel_id=1, source_target_pairs={{0,16},{16,32},{32,48},{48,64},{64,80},{80,96},{96,112},{112,128},... | collective-permute-start | bytes 983048 | tf_op jit(solution)/shard_map/ppermute | solution.py:237
  38.5 4.9 %collective-permute-done.refs_5_ = f32[4,16,1280]{2,1,0:T(8,128)S(1)} collective-permute-done((f32[4,16,1280]{2,1,0:T(8,128)S(1)}, f32[4,16,1280]{2,1,0:T(8,128)S(1)}, u32[]{:S(2)}, u32[]{:S(2)}) %collective-permute-start) | collective-permute-done | bytes 327712 | tf_op jit(solution)/shard_map/ppermute | solution.py:237
  43.4 5.3 %collective-permute-start.1 = (f32[4,16,1280]{2,1,0:T(8,128)S(1)}, f32[4,16,1280]{2,1,0:T(8,128)S(1)}, u32[]{:S(2)}, u32[]{:S(2)}) collective-permute-start(f32[4,16,1280]{2,1,0:T(8,128)S(1)} %collective-permute-done.refs_5_), channel_id=1, source_target_pairs={{0,176},{16,0},{32,16},{48,32},{64,48},{80,64},{96,80},{112,96},{1... | collective-permute-start | bytes 983048 | tf_op jit(solution)/shard_map/ppermute | solution.py:237
  48.7 0.0 collective-permute-done.5.refs_3_
  48.8 1.9 %collective-permute-start.6 = (f32[4,16,1280]{2,1,0:T(8,128)S(1)}, f32[4,16,1280]{2,1,0:T(8,128)S(1)}, u32[]{:S(2)}, u32[]{:S(2)}) collective-permute-start(f32[4,16,1280]{2,1,0:T(8,128)S(1)} %collective-permute-done.5.refs_3_), channel_id=1, source_target_pairs={{0,16},{16,32},{32,48},{48,64},{64,80},{80,96},{96,112},{112,128},... | collective-permute-start | bytes 983048 | tf_op jit(solution)/shard_map/ppermute | solution.py:237
  50.7 4.0 %collective-permute-done.1.refs_6_ = f32[4,16,1280]{2,1,0:T(8,128)S(1)} collective-permute-done((f32[4,16,1280]{2,1,0:T(8,128)S(1)}, f32[4,16,1280]{2,1,0:T(8,128)S(1)}, u32[]{:S(2)}, u32[]{:S(2)}) %collective-permute-start.1) | collective-permute-done | bytes 327712 | tf_op jit(solution)/shard_map/ppermute | solution.py:237
  54.7 5.3 %collective-permute-start.2 = (f32[4,16,1280]{2,1,0:T(8,128)S(1)}, f32[4,16,1280]{2,1,0:T(8,128)}, u32[]{:S(2)}, u32[]{:S(2)}) collective-permute-start(f32[4,16,1280]{2,1,0:T(8,128)S(1)} %collective-permute-done.1.refs_6_), channel_id=1, source_target_pairs={{0,176},{16,0},{32,16},{48,32},{64,48},{80,64},{96,80},{112,96},{1... | collective-permute-start | bytes 983048 | tf_op jit(solution)/shard_map/ppermute | solution.py:237
  60.0 0.0 collective-permute-done.6.refs_2_
  60.0 1.9 %collective-permute-start.7 = (f32[4,16,1280]{2,1,0:T(8,128)S(1)}, f32[4,16,1280]{2,1,0:T(8,128)S(1)}, u32[]{:S(2)}, u32[]{:S(2)}) collective-permute-start(f32[4,16,1280]{2,1,0:T(8,128)S(1)} %collective-permute-done.6.refs_2_), channel_id=1, source_target_pairs={{0,16},{16,32},{32,48},{48,64},{64,80},{80,96},{96,112},{112,128},... | collective-permute-start | bytes 983048 | tf_op jit(solution)/shard_map/ppermute | solution.py:237
  62.0 3.0 %collective-permute-done.2.refs_7_ = f32[4,16,1280]{2,1,0:T(8,128)} collective-permute-done((f32[4,16,1280]{2,1,0:T(8,128)S(1)}, f32[4,16,1280]{2,1,0:T(8,128)}, u32[]{:S(2)}, u32[]{:S(2)}) %collective-permute-start.2) | collective-permute-done | bytes 327712 | tf_op jit(solution)/shard_map/ppermute | solution.py:237
  65.0 5.4 %collective-permute-start.3 = (f32[4,16,1280]{2,1,0:T(8,128)}, f32[4,16,1280]{2,1,0:T(8,128)S(1)}, u32[]{:S(2)}, u32[]{:S(2)}) collective-permute-start(f32[4,16,1280]{2,1,0:T(8,128)} %collective-permute-done.2.refs_7_), channel_id=1, source_target_pairs={{0,176},{16,0},{32,16},{48,32},{64,48},{80,64},{96,80},{112,96},{1... | collective-permute-start | bytes 983048 | tf_op jit(solution)/shard_map/ppermute | solution.py:237
  70.4 0.1 dynamic_slice.3
  70.5 0.1 broadcast_xor_fusion.1
  70.6 1.9 %collective-permute-start.8 = (f32[4,16,1280]{2,1,0:T(8,128)S(1)}, f32[4,16,1280]{2,1,0:T(8,128)S(1)}, u32[]{:S(2)}, u32[]{:S(2)}) collective-permute-start(f32[4,16,1280]{2,1,0:T(8,128)S(1)} %collective-permute-done.7.refs_1_), channel_id=1, source_target_pairs={{0,16},{16,32},{32,48},{48,64},{64,80},{80,96},{96,112},{112,128},... | collective-permute-start | bytes 983048 | tf_op jit(solution)/shard_map/ppermute | solution.py:237
  72.5 2.2 %collective-permute-done.3.refs_0_ = f32[4,16,1280]{2,1,0:T(8,128)S(1)} collective-permute-done((f32[4,16,1280]{2,1,0:T(8,128)}, f32[4,16,1280]{2,1,0:T(8,128)S(1)}, u32[]{:S(2)}, u32[]{:S(2)}) %collective-permute-start.3) | collective-permute-done | bytes 327712 | tf_op jit(solution)/shard_map/ppermute | solution.py:237
  74.7 5.3 %collective-permute-start.4 = (f32[4,16,1280]{2,1,0:T(8,128)S(1)}, f32[4,16,1280]{2,1,0:T(8,128)S(1)}, u32[]{:S(2)}, u32[]{:S(2)}) collective-permute-start(f32[4,16,1280]{2,1,0:T(8,128)S(1)} %collective-permute-done.3.refs_0_), channel_id=1, source_target_pairs={{0,176},{16,0},{32,16},{48,32},{64,48},{80,64},{96,80},{112,96},{1... | collective-permute-start | bytes 983048 | tf_op jit(solution)/shard_map/ppermute | solution.py:237
  80.1 0.1 broadcast_xor_fusion.2
  80.1 0.1 xor.58
  80.2 0.1 broadcast_xor_fusion.symmetry_ref
  80.3 0.0 collective-permute-done.8.refs_0_
  80.3 1.9 %collective-permute-start.11 = (f32[4,16,1280]{2,1,0:T(8,128)S(1)}, f32[4,16,1280]{2,1,0:T(8,128)}, u32[]{:S(2)}, u32[]{:S(2)}) collective-permute-start(f32[4,16,1280]{2,1,0:T(8,128)S(1)} %collective-permute-done.8.refs_0_), channel_id=1, source_target_pairs={{0,16},{16,32},{32,48},{48,64},{64,80},{80,96},{96,112},{112,128},... | collective-permute-start | bytes 983048 | tf_op jit(solution)/shard_map/ppermute | solution.py:237
  82.2 1.9 %shard_map.57 = (bf16[2,192,1280]{2,1,0:T(8,128)(2,1)S(1)}, bf16[2,192,1280]{2,1,0:T(8,128)(2,1)S(1)}) custom-call(f32[32,3,40,128]{3,2,1,0:T(8,128)S(1)} %all-to-all-done.1.in_ref), custom_call_target="tpu_custom_call" | custom-call | bytes 3932160 | tf_op jit(solution)/shard_map/pallas_call | solution.py:110
  84.1 0.9 copy-done.2
  85.1 0.9 copy-done.3
  86.0 0.0 collective-permute-done.4.refs_1_
  86.0 4.6 %collective-permute-start.10 = (f32[4,16,1280]{2,1,0:T(8,128)S(1)}, f32[4,16,1280]{2,1,0:T(8,128)S(1)}, u32[]{:S(2)}, u32[]{:S(2)}) collective-permute-start(f32[4,16,1280]{2,1,0:T(8,128)S(1)} %collective-permute-done.4.refs_1_), channel_id=1, source_target_pairs={{0,176},{16,0},{32,16},{48,32},{64,48},{80,64},{96,80},{112,96},{1... | collective-permute-start | bytes 983048 | tf_op jit(solution)/shard_map/ppermute | solution.py:237
  90.6 6.4 %shard_map.58 = (f32[8,2,3,4,512]{4,3,2,1,0:T(4,128)}, f32[8,2,3,4,512]{4,3,2,1,0:T(4,128)}) custom-call(s32[1]{0:T(128)} %bitcast.1.core_ref, bf16[2,192,1280]{2,1,0:T(8,128)(2,1)} %copy-done.2, bf16[2,192,1280]{2,1,0:T(8,128)(2,1)} %copy-done.3, f32[4,16,1280]{2,1,0:T(8,128)S(1)} %collective-permute-done.8.refs_0_, ...), custom_call_target="tpu_custom_call" | custom-call | flops 1509949440 | bytes 8388608 | tf_op jit(solution)/shard_map/pallas_call | solution.py:176
  97.0 6.7 %collective-permute-start.9 = (f32[8,2,3,4,512]{4,3,2,1,0:T(4,128)}, f32[8,2,3,4,512]{4,3,2,1,0:T(4,128)S(1)}, u32[]{:S(2)}, u32[]{:S(2)}) collective-permute-start(f32[8,2,3,4,512]{4,3,2,1,0:T(4,128)} %get-tuple-element.24), channel_id=1, source_target_pairs={{0,1},{1,0},{2,3},{3,2},{4,5},{5,4},{6,7},{7,6},{8,9},{9,8},{10,11... | collective-permute-start | bytes 1179656 | tf_op jit(solution)/shard_map/ppermute | solution.py:271
  103.7 0.0 collective-permute-done.10.refs_2_
  103.7 0.7 copy-done.7
  104.4 2.9 %shard_map.59 = (f32[8,2,3,4,256]{4,3,2,1,0:T(4,128)S(1)}, f32[8,2,3,4,256]{4,3,2,1,0:T(4,128)S(1)}) custom-call(s32[1]{0:T(128)} %bitcast.1.core_ref, bf16[2,192,1280]{2,1,0:T(8,128)(2,1)} %copy-done.2, bf16[2,192,1280]{2,1,0:T(8,128)(2,1)} %copy-done.3, f32[4,16,1280]{2,1,0:T(8,128)S(1)} %collective-permute-done.3.refs_0_, f32[4,16,1280]{2,1,0:T(8,128)} %copy-done.6, ...), custom_call_target="tpu_custom_call" | custom-call | flops 754974720 | bytes 8388608 | tf_op jit(solution)/shard_map/pallas_call | solution.py:176
  107.4 1.9 %collective-permute-start.12 = (f32[8,2,3,4,256]{4,3,2,1,0:T(4,128)S(1)}, f32[8,2,3,4,256]{4,3,2,1,0:T(4,128)S(1)}, u32[]{:S(2)}, u32[]{:S(2)}) collective-permute-start(f32[8,2,3,4,256]{4,3,2,1,0:T(4,128)S(1)} %get-tuple-element.27), channel_id=1, source_target_pairs={{0,1},{1,0},{2,3},{3,2},{4,5},{5,4},{6,7},{7,6},{8,9},{9,8},{10,11... | collective-permute-start | bytes 589832 | tf_op jit(solution)/shard_map/ppermute | solution.py:273
  109.3 0.0 collective-permute-done.9
  109.3 0.1 add.14
  109.4 1.3 collective-permute-done.12
  110.7 0.1 add.15
  110.8 1.0 pad_maximum_fusion
  111.7 7.2 %all-to-all-start.2 = ((f32[16,3,4,768]{3,2,1,0:T(4,128)}), f32[16,3,4,768]{3,2,1,0:T(4,128)S(1)}, u32[]{:S(2)}, u32[]{:S(2)}) async-start(f32[16,3,4,768]{3,2,1,0:T(4,128)} %bitcast.3), calls=%async_computation.2 | async-start | bytes 1179648 | tf_op jit(solution)/shard_map/all_to_all | solution.py:276
  118.9 17.4 %all-to-all-done.2.parts_ref = f32[16,3,4,768]{3,2,1,0:T(4,128)S(1)} async-done(((f32[16,3,4,768]{3,2,1,0:T(4,128)}), f32[16,3,4,768]{3,2,1,0:T(4,128)S(1)}, u32[]{:S(2)}, u32[]{:S(2)}) %all-to-all-start.2) | async-done | bytes 589856 | tf_op jit(solution)/shard_map/all_to_all | solution.py:276
  136.3 0.9 shard_map.60
  (28 shorter events, 0.1 us)
Async XLA Ops:
  1.8 10.7 %all-to-all-start = ((f32[4,16,1280]{2,1,0:T(8,128)}), f32[4,16,1280]{2,1,0:T(8,128)S(1)}, u32[]{:S(2)}, u32[]{:S(2)}) async-start(f32[4,16,1280]{2,1,0:T(8,128)} %shard_map.55), calls=%async_computation | async-start | bytes 655360 | tf_op jit(solution)/shard_map/all_to_all | solution.py:253
  6.7 1.5 %copy-start.1 = (f32[3,64,4,640]{3,2,1,0:T(4,128)S(1)}, f32[3,64,4,640]{3,2,1,0:T(4,128)}, u32[]{:S(2)}) copy-start(f32[3,64,4,640]{3,2,1,0:T(4,128)} %in_ref.1) | copy-start | bytes 5898244
  10.0 1.3 copy-start
  11.3 59.2 %copy-start.8 = (s32[64]{0:T(128)S(1)}, s32[64]{0:T(128)}, u32[]{:S(2)}) copy-start(s32[64]{0:T(128)} %param.9) | copy-start | bytes 772
  11.3 59.3 %copy-start.9 = (s32[12]{0:T(128)S(1)}, s32[12]{0:T(128)}, u32[]{:S(2)}) copy-start(s32[12]{0:T(128)} %param.8) | copy-start | bytes 148
  11.3 68.8 %copy-start.10 = (s32[3]{0:T(128)S(1)}, s32[3]{0:T(128)}, u32[]{:S(2)}) copy-start(s32[3]{0:T(128)} %param.7) | copy-start | bytes 40
  12.5 24.0 %copy-start.5 = (f32[4,16,1280]{2,1,0:T(8,128)}, f32[4,16,1280]{2,1,0:T(8,128)S(1)}, u32[]{:S(2)}) copy-start(f32[4,16,1280]{2,1,0:T(8,128)S(1)} %all-to-all-done.refs_4_) | copy-start | bytes 983044
  12.5 69.7 %all-to-all-start.1 = ((f32[32,3,40,128]{3,2,1,0:T(8,128)}), f32[32,3,40,128]{3,2,1,0:T(8,128)S(1)}, u32[]{:S(2)}, u32[]{:S(2)}) async-start(f32[32,3,40,128]{3,2,1,0:T(8,128)} %copy-done), calls=%async_computation.1 | async-start | bytes 3932160 | tf_op jit(solution)/shard_map/all_to_all | solution.py:260
  26.5 17.0 %collective-permute-start = (f32[4,16,1280]{2,1,0:T(8,128)S(1)}, f32[4,16,1280]{2,1,0:T(8,128)S(1)}, u32[]{:S(2)}, u32[]{:S(2)}) collective-permute-start(f32[4,16,1280]{2,1,0:T(8,128)S(1)} %all-to-all-done.refs_4_), channel_id=1, source_target_pairs={{0,176},{16,0},{32,16},{48,32},{64,48},{80,64},{96,80},{112,96},{1... | collective-permute-start | bytes 983048 | tf_op jit(solution)/shard_map/ppermute | solution.py:237
  36.6 12.2 %collective-permute-start.5 = (f32[4,16,1280]{2,1,0:T(8,128)S(1)}, f32[4,16,1280]{2,1,0:T(8,128)S(1)}, u32[]{:S(2)}, u32[]{:S(2)}) collective-permute-start(f32[4,16,1280]{2,1,0:T(8,128)S(1)} %all-to-all-done.refs_4_), channel_id=1, source_target_pairs={{0,16},{16,32},{32,48},{48,64},{64,80},{80,96},{96,112},{112,128},... | collective-permute-start | bytes 983048 | tf_op jit(solution)/shard_map/ppermute | solution.py:237
  43.4 18.5 %copy-start.11 = (f32[4,16,1280]{2,1,0:T(8,128)}, f32[4,16,1280]{2,1,0:T(8,128)S(1)}, u32[]{:S(2)}) copy-start(f32[4,16,1280]{2,1,0:T(8,128)S(1)} %collective-permute-done.refs_5_) | copy-start | bytes 983044
  43.4 11.2 %collective-permute-start.1 = (f32[4,16,1280]{2,1,0:T(8,128)S(1)}, f32[4,16,1280]{2,1,0:T(8,128)S(1)}, u32[]{:S(2)}, u32[]{:S(2)}) collective-permute-start(f32[4,16,1280]{2,1,0:T(8,128)S(1)} %collective-permute-done.refs_5_), channel_id=1, source_target_pairs={{0,176},{16,0},{32,16},{48,32},{64,48},{80,64},{96,80},{112,96},{1... | collective-permute-start | bytes 983048 | tf_op jit(solution)/shard_map/ppermute | solution.py:237
  48.7 11.2 %copy-start.12 = (f32[4,16,1280]{2,1,0:T(8,128)}, f32[4,16,1280]{2,1,0:T(8,128)S(1)}, u32[]{:S(2)}) copy-start(f32[4,16,1280]{2,1,0:T(8,128)S(1)} %collective-permute-done.5.refs_3_) | copy-start | bytes 983044
  48.8 11.2 %collective-permute-start.6 = (f32[4,16,1280]{2,1,0:T(8,128)S(1)}, f32[4,16,1280]{2,1,0:T(8,128)S(1)}, u32[]{:S(2)}, u32[]{:S(2)}) collective-permute-start(f32[4,16,1280]{2,1,0:T(8,128)S(1)} %collective-permute-done.5.refs_3_), channel_id=1, source_target_pairs={{0,16},{16,32},{32,48},{48,64},{64,80},{80,96},{96,112},{112,128},... | collective-permute-start | bytes 983048 | tf_op jit(solution)/shard_map/ppermute | solution.py:237
  54.7 15.9 %copy-start.13 = (f32[4,16,1280]{2,1,0:T(8,128)}, f32[4,16,1280]{2,1,0:T(8,128)S(1)}, u32[]{:S(2)}) copy-start(f32[4,16,1280]{2,1,0:T(8,128)S(1)} %collective-permute-done.1.refs_6_) | copy-start | bytes 983044
  54.7 10.3 %collective-permute-start.2 = (f32[4,16,1280]{2,1,0:T(8,128)S(1)}, f32[4,16,1280]{2,1,0:T(8,128)}, u32[]{:S(2)}, u32[]{:S(2)}) collective-permute-start(f32[4,16,1280]{2,1,0:T(8,128)S(1)} %collective-permute-done.1.refs_6_), channel_id=1, source_target_pairs={{0,176},{16,0},{32,16},{48,32},{64,48},{80,64},{96,80},{112,96},{1... | collective-permute-start | bytes 983048 | tf_op jit(solution)/shard_map/ppermute | solution.py:237
  60.0 12.5 %copy-start.14 = (f32[4,16,1280]{2,1,0:T(8,128)}, f32[4,16,1280]{2,1,0:T(8,128)S(1)}, u32[]{:S(2)}) copy-start(f32[4,16,1280]{2,1,0:T(8,128)S(1)} %collective-permute-done.6.refs_2_) | copy-start | bytes 983044
  60.0 10.6 %collective-permute-start.7 = (f32[4,16,1280]{2,1,0:T(8,128)S(1)}, f32[4,16,1280]{2,1,0:T(8,128)S(1)}, u32[]{:S(2)}, u32[]{:S(2)}) collective-permute-start(f32[4,16,1280]{2,1,0:T(8,128)S(1)} %collective-permute-done.6.refs_2_), channel_id=1, source_target_pairs={{0,16},{16,32},{32,48},{48,64},{64,80},{80,96},{96,112},{112,128},... | collective-permute-start | bytes 983048 | tf_op jit(solution)/shard_map/ppermute | solution.py:237
  65.0 9.7 %collective-permute-start.3 = (f32[4,16,1280]{2,1,0:T(8,128)}, f32[4,16,1280]{2,1,0:T(8,128)S(1)}, u32[]{:S(2)}, u32[]{:S(2)}) collective-permute-start(f32[4,16,1280]{2,1,0:T(8,128)} %collective-permute-done.2.refs_7_), channel_id=1, source_target_pairs={{0,176},{16,0},{32,16},{48,32},{64,48},{80,64},{96,80},{112,96},{1... | collective-permute-start | bytes 983048 | tf_op jit(solution)/shard_map/ppermute | solution.py:237
  70.6 9.7 %collective-permute-start.8 = (f32[4,16,1280]{2,1,0:T(8,128)S(1)}, f32[4,16,1280]{2,1,0:T(8,128)S(1)}, u32[]{:S(2)}, u32[]{:S(2)}) collective-permute-start(f32[4,16,1280]{2,1,0:T(8,128)S(1)} %collective-permute-done.7.refs_1_), channel_id=1, source_target_pairs={{0,16},{16,32},{32,48},{48,64},{64,80},{80,96},{96,112},{112,128},... | collective-permute-start | bytes 983048 | tf_op jit(solution)/shard_map/ppermute | solution.py:237
  74.7 11.3 %collective-permute-start.4 = (f32[4,16,1280]{2,1,0:T(8,128)S(1)}, f32[4,16,1280]{2,1,0:T(8,128)S(1)}, u32[]{:S(2)}, u32[]{:S(2)}) collective-permute-start(f32[4,16,1280]{2,1,0:T(8,128)S(1)} %collective-permute-done.3.refs_0_), channel_id=1, source_target_pairs={{0,176},{16,0},{32,16},{48,32},{64,48},{80,64},{96,80},{112,96},{1... | collective-permute-start | bytes 983048 | tf_op jit(solution)/shard_map/ppermute | solution.py:237
  80.3 23.4 %collective-permute-start.11 = (f32[4,16,1280]{2,1,0:T(8,128)S(1)}, f32[4,16,1280]{2,1,0:T(8,128)}, u32[]{:S(2)}, u32[]{:S(2)}) collective-permute-start(f32[4,16,1280]{2,1,0:T(8,128)S(1)} %collective-permute-done.8.refs_0_), channel_id=1, source_target_pairs={{0,16},{16,32},{32,48},{48,64},{64,80},{80,96},{96,112},{112,128},... | collective-permute-start | bytes 983048 | tf_op jit(solution)/shard_map/ppermute | solution.py:237
  84.1 1.0 copy-start.2
  85.1 0.9 copy-start.3
  86.0 11.0 %copy-start.6 = (f32[4,16,1280]{2,1,0:T(8,128)}, f32[4,16,1280]{2,1,0:T(8,128)S(1)}, u32[]{:S(2)}) copy-start(f32[4,16,1280]{2,1,0:T(8,128)S(1)} %collective-permute-done.4.refs_1_) | copy-start | bytes 983044
  86.0 17.7 %collective-permute-start.10 = (f32[4,16,1280]{2,1,0:T(8,128)S(1)}, f32[4,16,1280]{2,1,0:T(8,128)S(1)}, u32[]{:S(2)}, u32[]{:S(2)}) collective-permute-start(f32[4,16,1280]{2,1,0:T(8,128)S(1)} %collective-permute-done.4.refs_1_), channel_id=1, source_target_pairs={{0,176},{16,0},{32,16},{48,32},{64,48},{80,64},{96,80},{112,96},{1... | collective-permute-start | bytes 983048 | tf_op jit(solution)/shard_map/ppermute | solution.py:237
  97.0 12.3 %copy-start.4 = (f32[8,2,3,4,512]{4,3,2,1,0:T(4,128)S(1)}, f32[8,2,3,4,512]{4,3,2,1,0:T(4,128)}, u32[]{:S(2)}) copy-start(f32[8,2,3,4,512]{4,3,2,1,0:T(4,128)} %get-tuple-element.23) | copy-start | bytes 1179652
  97.0 12.3 %collective-permute-start.9 = (f32[8,2,3,4,512]{4,3,2,1,0:T(4,128)}, f32[8,2,3,4,512]{4,3,2,1,0:T(4,128)S(1)}, u32[]{:S(2)}, u32[]{:S(2)}) collective-permute-start(f32[8,2,3,4,512]{4,3,2,1,0:T(4,128)} %get-tuple-element.24), channel_id=1, source_target_pairs={{0,1},{1,0},{2,3},{3,2},{4,5},{5,4},{6,7},{7,6},{8,9},{9,8},{10,11... | collective-permute-start | bytes 1179656 | tf_op jit(solution)/shard_map/ppermute | solution.py:271
  103.7 0.7 copy-start.7
  107.4 3.3 %collective-permute-start.12 = (f32[8,2,3,4,256]{4,3,2,1,0:T(4,128)S(1)}, f32[8,2,3,4,256]{4,3,2,1,0:T(4,128)S(1)}, u32[]{:S(2)}, u32[]{:S(2)}) collective-permute-start(f32[8,2,3,4,256]{4,3,2,1,0:T(4,128)S(1)} %get-tuple-element.27), channel_id=1, source_target_pairs={{0,1},{1,0},{2,3},{3,2},{4,5},{5,4},{6,7},{7,6},{8,9},{9,8},{10,11... | collective-permute-start | bytes 589832 | tf_op jit(solution)/shard_map/ppermute | solution.py:273
  111.7 24.6 %all-to-all-start.2 = ((f32[16,3,4,768]{3,2,1,0:T(4,128)}), f32[16,3,4,768]{3,2,1,0:T(4,128)S(1)}, u32[]{:S(2)}, u32[]{:S(2)}) async-start(f32[16,3,4,768]{3,2,1,0:T(4,128)} %bitcast.3), calls=%async_computation.2 | async-start | bytes 1179648 | tf_op jit(solution)/shard_map/all_to_all | solution.py:276

commit v6 on v5

--- a/solution.py
+++ b/solution.py
@@ -1,3 +1,5 @@
+import functools
+
 import jax
 import jax.numpy as jnp
 from jax import lax
@@ -118,23 +120,30 @@
     )(got)
 
 
-def product_kernel(core_ref, high_ref, low_ref, *refs):
-    *columns_refs, own_ref, other_ref, left, right, right_high, right_low, sems = refs
-    count = len(columns_refs)
+def product_kernel(count, core_ref, high_ref, low_ref, *refs):
+    *in_refs, own_ref, other_ref, left, right, right_high, right_low, sems = refs
+    columns_refs, split = in_refs[:count], in_refs[count:]
     xs, width, depth = columns_refs[0].shape
     core = core_ref[0]
     rows = high_ref.shape[1]
+    total_count = right_high.shape[0] // (xs * width)
     copies = [
         pltpu.make_async_copy(ref, right.at[r], sems.at[r]) for r, ref in enumerate(columns_refs)
     ]
+    ready, at = [], count * xs * width
+    for i, ref in enumerate(split):
+        to = right_low if i % 2 else right_high
+        place = pl.ds(at, ref.shape[0])
+        ready.append(pltpu.make_async_copy(ref, to.at[place], sems.at[total_count + 4 + i]))
+        at += ref.shape[0] * (i % 2)
     halves = [
         pltpu.make_async_copy(
-            ref.at[side], left.at[i, pl.ds(part * rows, rows)], sems.at[count + 2 * i + part]
+            ref.at[side], left.at[i, pl.ds(part * rows, rows)], sems.at[total_count + 2 * i + part]
         )
         for i, ref in enumerate((high_ref, low_ref))
         for part, side in enumerate((core, 1 - core))
     ]
-    for copy in copies[:2] + halves + copies[2:]:
+    for copy in copies[:2] + halves + copies[2:] + ready:
         copy.start()
 
     def dot(left, right):
@@ -144,8 +153,11 @@
 
     ys, xls, window, local = own_ref.shape[:4]
     group = 4
-    for first in range(0, count, group):
-        for r in range(first, first + group):
+    for first in range(0, total_count, group):
+        if first + group == total_count:
+            for copy in ready:
+                copy.wait()
+        for r in range(first, min(first + group, count)):
             copies[r].wait()
             block = right[r].reshape(xs * width, depth)
             high = block.astype(jnp.bfloat16)
@@ -168,29 +180,59 @@
                         ]
 
 
-def product(core, high, low, columns, ys, window, local):
+def product(core, high, low, columns, ready, ys, window, local):
     xs, width, depth = columns[0].shape
     rows = high.shape[1]
-    block = xs * len(columns) * width
+    block = xs * len(columns) * width + sum(part.shape[0] for part in ready[::2])
+    count = block // (xs * width)
     shape = jax.ShapeDtypeStruct((ys, 2, window, local, block), jnp.float32)
     return pl.pallas_call(
-        product_kernel,
+        functools.partial(product_kernel, len(columns)),
         out_shape=(shape, shape),
         in_specs=[pl.BlockSpec(memory_space=pltpu.SMEM)]
-        + [pl.BlockSpec(memory_space=pl.ANY)] * (2 + len(columns)),
+        + [pl.BlockSpec(memory_space=pl.ANY)] * (2 + len(columns) + len(ready)),
         out_specs=(VMEM, VMEM),
         scratch_shapes=[
             pltpu.VMEM((2, 2 * rows, depth), jnp.bfloat16),
-            pltpu.VMEM((len(columns), xs, width, depth), jnp.float32),
+            pltpu.VMEM((count, xs, width, depth), jnp.float32),
             pltpu.VMEM((block, depth), jnp.bfloat16),
             pltpu.VMEM((block, depth), jnp.bfloat16),
-            pltpu.SemaphoreType.DMA((len(columns) + 4,)),
+            pltpu.SemaphoreType.DMA((count + 4 + len(ready),)),
         ],
-        compiler_params=pltpu.CompilerParams(vmem_limit_bytes=53 * MIB),
+        compiler_params=pltpu.CompilerParams(vmem_limit_bytes=52 * MIB),
         cost_estimate=pl.CostEstimate(
             flops=12 * rows * depth * block, bytes_accessed=8 << 20, transcendentals=0
         ),
-    )(core, high, low, *columns)
+    )(core, high, low, *columns, *ready)
+
+
+def split_kernel(*refs):
+    *in_refs, high_ref, low_ref = refs
+    xs, width, depth = in_refs[0].shape
+    for i, ref in enumerate(in_refs):
+        block = ref[...].reshape(xs * width, depth)
+        high = block.astype(jnp.bfloat16)
+        at = slice(i * xs * width, (i + 1) * xs * width)
+        high_ref[at] = high
+        low_ref[at] = (block - high.astype(jnp.float32)).astype(jnp.bfloat16)
+
+
+def split(*blocks):
+    xs, width, depth = blocks[0].shape
+    shape = jax.ShapeDtypeStruct((len(blocks) * xs * width, depth), jnp.bfloat16)
+    return pl.pallas_call(
+        split_kernel,
+        out_shape=(shape, shape),
+        in_specs=[VMEM] * len(blocks),
+        out_specs=(VMEM, VMEM),
+        compiler_params=pltpu.CompilerParams(vmem_limit_bytes=8 * MIB),
+        cost_estimate=pl.CostEstimate(
+            flops=28_000_000_000, bytes_accessed=8 * blocks[0].size, transcendentals=0
+        ),
+    )(*blocks)
+
+
+ORDER = (1, 3, -1, -3, -4, 0, 2, -2, 4, 5, 6, 7)
 
 
 def finish_kernel(z_ref, parts_ref, symmetry_ref, out_ref, rows):
@@ -202,7 +244,11 @@
         for source in range(1, sources):
             total = total + parts_ref[source, a]
         rows[pl.ds(a * local, local), :] = total
-    turned = pltpu.roll(rows[...], lax.rem(z_ref[0] + zs - 4, zs) * width, 1)
+    blocks = rows[...]
+    blocks = jnp.concatenate(
+        [blocks[:, ORDER.index(r) * width:(ORDER.index(r) + 1) * width] for r in range(-4, 8)], axis=1
+    )
+    turned = pltpu.roll(blocks, lax.rem(z_ref[0] + zs - 4, zs) * width, 1)
     ordered = jnp.concatenate(
         [
             turned[:, z * width + x * 16:z * width + (x + 1) * 16]
@@ -256,20 +302,24 @@
     behind = gather(got, "z", half - 1, -1)
 
     packed = pack_amplitudes(amplitudes, 4 * ys)
-    packed, _ = lax.optimization_barrier((packed, got))
+    halves = split(got)
+    packed, *halves = lax.optimization_barrier((packed, *halves))
+    nearby = split(ahead[1], behind[1])
     packed = lax.all_to_all(packed, ("y", "core", "xl"), 0, 0, tiled=True)
-    packed, symmetry = lax.optimization_barrier((packed, symmetry))
+    packed, symmetry, *nearby = lax.optimization_barrier((packed, symmetry, *nearby))
+    halves += nearby
     high, low = spin_rows(packed)
     last, high, low = lax.optimization_barrier((ahead[-1], high, low))
     ahead += gather(last, "z", 1, 1)
 
     core = lax.axis_index("core").astype(jnp.int32).reshape(1)
     swap = [(0, 1), (1, 0)]
-    early = behind[3::-1] + [got] + ahead[:3]
+    early = [ahead[0], ahead[2], behind[0], behind[2], behind[3]]
     late = ahead[3:] + behind[4:]
-    own, given = product(core, high, low, early, ys, window, local)
+    own, given = product(core, high, low, early, halves, ys, window, local)
+    given, late[2] = lax.optimization_barrier((given, late[2]))
     taken = lax.ppermute(given, "core", swap)
-    own_late, given = product(core, high, low, late, ys, window, local)
+    own_late, given = product(core, high, low, late, [], ys, window, local)
     partial = jnp.concatenate([own + taken, own_late + lax.ppermute(given, "core", swap)], axis=-1)
 
     partial = partial.reshape(2 * ys, window, local, -1)

time: 138 us -> 136 us (0.986)
  starting transfers between devices: 80.1 us -> 71.9 us
  waiting for transfers between devices: 34.1 us -> 37.6 us
  Pallas kernels: 15.6 us -> 17.6 us
    all_to_all x1, starting transfers between devices: 13.9 us -> 9.7 us  [body(): packed = lax.all_to_all(packed, ('y', 'core', 'xl'), 0, 0, tiled=True)]
    all_to_all x1, waiting for transfers between devices: 0.01 us -> 4.03 us  [body(): packed = lax.all_to_all(packed, ('y', 'core', 'xl'), 0, 0, tiled=True)]
    ppermute x1, starting transfers between devices: 6.69 us -> 3.1 us  [body(): taken = lax.ppermute(given, 'core', swap)]
    all_to_all x1, starting transfers between devices: 7.15 us -> 5.66 us  [body(): partial = lax.all_to_all(partial, ('y', 'xl'), 0, 0, tiled=True)]
    pallas_call x2 -> x4, Pallas kernels: 9.33 us -> 10.2 us  [the longest x2 8.94 us: product(): pl.pallas_call(functools.partial(product_kernel, len(columns)), out_shape...]
    unnamed x30 -> x26, local copies, waits for them, and re-layouts: 5.47 us -> 6.24 us
  transfers between devices with their start and end apart: 16 -> 16, of which waited for: 7 -> 7; matrix products, arithmetic and copies ran while one was open for 0% -> 0% of each run, Pallas kernels for 9% -> 11%
where the time goes in v6:
time: 136 us; the launch traced here: 135 us
  starting transfers between devices  71.9 us (53%)
  waiting for transfers between devices  37.6 us (28%)
  Pallas kernels  17.6 us (13%)
  local copies, waits for them, and re-layouts  6.39 us (5%)
    ppermute x11, starting transfers between devices, gather(): blocks.append(lax.ppermute(blocks[-1], axis, pairs))  45.8 us
    all_to_all x1, waiting for transfers between devices, body(): partial = lax.all_to_all(partial, ('y', 'xl'), 0, 0, tiled=True)  17.4 us
    ppermute x11, waiting for transfers between devices, gather(): blocks.append(lax.ppermute(blocks[-1], axis, pairs))  13.5 us
    all_to_all x1, starting transfers between devices, body(): packed = lax.all_to_all(packed, ('y', 'core', 'xl'), 0, 0, tiled=True)  9.7 us
    pallas_call x2, Pallas kernels, product(): pl.pallas_call(functools.partial(product_kernel, len(columns)), out_shape...  8.94 us
    unnamed x26, local copies, waits for them, and re-layouts  6.24 us
    all_to_all x1, starting transfers between devices, body(): partial = lax.all_to_all(partial, ('y', 'xl'), 0, 0, tiled=True)  5.66 us
    all_to_all x1, starting transfers between devices, body(): got = lax.all_to_all(sent, ('xh', 'xl'), 0, 0, tiled=True)  4.84 us
  transfers between devices with their start and end apart: 16, of which 7 were waited for; matrix products, arithmetic and copies ran while one was open for 0% of the time, Pallas kernels for 11%

profile of v6, /device:TPU:1, one launch (start us, length us, event | category | flops | bytes accessed | tf_op | source)
XLA Modules:
  0.0 135.2 jit_solution(13081445954224708808)
XLA Ops:
  0.0 1.8 %shard_map.55 = f32[4,16,1280]{2,1,0:T(8,128)} custom-call(f32[40,16,64]{2,1,0:T(8,128)} %bitcast.4), custom_call_target="tpu_custom_call" | custom-call | tf_op jit(solution)/shard_map/pallas_call | solution.py:27
  1.8 4.8 %all-to-all-start = ((f32[4,16,1280]{2,1,0:T(8,128)}), f32[4,16,1280]{2,1,0:T(8,128)S(1)}, u32[]{:S(2)}, u32[]{:S(2)}) async-start(f32[4,16,1280]{2,1,0:T(8,128)} %shard_map.55), calls=%async_computation | async-start | bytes 655360 | tf_op jit(solution)/shard_map/all_to_all | solution.py:299
  6.7 1.5 %copy-done = f32[3,64,4,640]{3,2,1,0:T(4,128)S(1)} copy-done((f32[3,64,4,640]{3,2,1,0:T(4,128)S(1)}, f32[3,64,4,640]{3,2,1,0:T(4,128)}, u32[]{:S(2)}) %copy-start) | copy-done | bytes 1966104
  8.2 2.8 %shard_map.56 = f32[32,3,40,128]{3,2,1,0:T(8,128)} custom-call(f32[3,64,4,640]{3,2,1,0:T(4,128)S(1)} %copy-done), custom_call_target="tpu_custom_call" | custom-call | bytes 3932160 | tf_op jit(solution)/shard_map/pallas_call | solution.py:60
  11.0 1.5 %all-to-all-done.refs_0_ = f32[4,16,1280]{2,1,0:T(8,128)S(1)} async-done(((f32[4,16,1280]{2,1,0:T(8,128)}), f32[4,16,1280]{2,1,0:T(8,128)S(1)}, u32[]{:S(2)}, u32[]{:S(2)}) %all-to-all-start) | async-done | bytes 327712 | tf_op jit(solution)/shard_map/all_to_all | solution.py:299
  12.5 14.6 %collective-permute-start = (f32[4,16,1280]{2,1,0:T(8,128)S(1)}, f32[4,16,1280]{2,1,0:T(8,128)S(1)}, u32[]{:S(2)}, u32[]{:S(2)}) collective-permute-start(f32[4,16,1280]{2,1,0:T(8,128)S(1)} %all-to-all-done.refs_0_), channel_id=1, source_target_pairs={{0,176},{16,0},{32,16},{48,32},{64,48},{80,64},{96,80},{112,96},{1... | collective-permute-start | bytes 983048 | tf_op jit(solution)/shard_map/ppermute | solution.py:283
  27.1 0.1 shard_map.57
  27.2 0.0 copy-start.10
  27.2 0.0 copy-start.11
  27.2 0.6 copy-done.7
  27.9 9.7 %all-to-all-start.1 = ((f32[32,3,40,128]{3,2,1,0:T(8,128)}), f32[32,3,40,128]{3,2,1,0:T(8,128)S(1)}, u32[]{:S(2)}, u32[]{:S(2)}) async-start(f32[32,3,40,128]{3,2,1,0:T(8,128)} %shard_map.56), calls=%async_computation.1 | async-start | bytes 3932160 | tf_op jit(solution)/shard_map/all_to_all | solution.py:308
  37.6 1.9 %collective-permute-start.5 = (f32[4,16,1280]{2,1,0:T(8,128)S(1)}, f32[4,16,1280]{2,1,0:T(8,128)S(1)}, u32[]{:S(2)}, u32[]{:S(2)}) collective-permute-start(f32[4,16,1280]{2,1,0:T(8,128)S(1)} %all-to-all-done.refs_0_), channel_id=1, source_target_pairs={{0,16},{16,32},{32,48},{48,64},{64,80},{80,96},{96,112},{112,128},... | collective-permute-start | bytes 983048 | tf_op jit(solution)/shard_map/ppermute | solution.py:283
  39.5 4.6 %collective-permute-start.1 = (f32[4,16,1280]{2,1,0:T(8,128)S(1)}, f32[4,16,1280]{2,1,0:T(8,128)}, u32[]{:S(2)}, u32[]{:S(2)}) collective-permute-start(f32[4,16,1280]{2,1,0:T(8,128)S(1)} %collective-permute-done.refs_0_), channel_id=1, source_target_pairs={{0,176},{16,0},{32,16},{48,32},{64,48},{80,64},{96,80},{112,96},{1... | collective-permute-start | bytes 983048 | tf_op jit(solution)/shard_map/ppermute | solution.py:283
  44.1 5.7 %collective-permute-done.5.refs_2_ = f32[4,16,1280]{2,1,0:T(8,128)S(1)} collective-permute-done((f32[4,16,1280]{2,1,0:T(8,128)S(1)}, f32[4,16,1280]{2,1,0:T(8,128)S(1)}, u32[]{:S(2)}, u32[]{:S(2)}) %collective-permute-start.5) | collective-permute-done | bytes 327712 | tf_op jit(solution)/shard_map/ppermute | solution.py:283
  49.7 1.9 %collective-permute-start.6 = (f32[4,16,1280]{2,1,0:T(8,128)S(1)}, f32[4,16,1280]{2,1,0:T(8,128)}, u32[]{:S(2)}, u32[]{:S(2)}) collective-permute-start(f32[4,16,1280]{2,1,0:T(8,128)S(1)} %collective-permute-done.5.refs_2_), channel_id=1, source_target_pairs={{0,16},{16,32},{32,48},{48,64},{64,80},{80,96},{96,112},{112,128},... | collective-permute-start | bytes 983048 | tf_op jit(solution)/shard_map/ppermute | solution.py:283
  51.7 4.6 %collective-permute-start.2 = (f32[4,16,1280]{2,1,0:T(8,128)}, f32[4,16,1280]{2,1,0:T(8,128)S(1)}, u32[]{:S(2)}, u32[]{:S(2)}) collective-permute-start(f32[4,16,1280]{2,1,0:T(8,128)} %collective-permute-done.1.refs_0_), channel_id=1, source_target_pairs={{0,176},{16,0},{32,16},{48,32},{64,48},{80,64},{96,80},{112,96},{1... | collective-permute-start | bytes 983048 | tf_op jit(solution)/shard_map/ppermute | solution.py:283
  56.3 0.1 dynamic_slice.3
  56.4 0.1 broadcast_xor_fusion.1
  56.4 4.7 %collective-permute-done.6.refs_1_ = f32[4,16,1280]{2,1,0:T(8,128)} collective-permute-done((f32[4,16,1280]{2,1,0:T(8,128)S(1)}, f32[4,16,1280]{2,1,0:T(8,128)}, u32[]{:S(2)}, u32[]{:S(2)}) %collective-permute-start.6) | collective-permute-done | bytes 327712 | tf_op jit(solution)/shard_map/ppermute | solution.py:283
  61.1 1.9 %collective-permute-start.7 = (f32[4,16,1280]{2,1,0:T(8,128)}, f32[4,16,1280]{2,1,0:T(8,128)}, u32[]{:S(2)}, u32[]{:S(2)}) collective-permute-start(f32[4,16,1280]{2,1,0:T(8,128)} %collective-permute-done.6.refs_1_), channel_id=1, source_target_pairs={{0,16},{16,32},{32,48},{48,64},{64,80},{80,96},{96,112},{112,128},... | collective-permute-start | bytes 983048 | tf_op jit(solution)/shard_map/ppermute | solution.py:283
  63.0 4.6 %collective-permute-start.3 = (f32[4,16,1280]{2,1,0:T(8,128)S(1)}, f32[4,16,1280]{2,1,0:T(8,128)S(1)}, u32[]{:S(2)}, u32[]{:S(2)}) collective-permute-start(f32[4,16,1280]{2,1,0:T(8,128)S(1)} %collective-permute-done.2.refs_1_), channel_id=1, source_target_pairs={{0,176},{16,0},{32,16},{48,32},{64,48},{80,64},{96,80},{112,96},{1... | collective-permute-start | bytes 983048 | tf_op jit(solution)/shard_map/ppermute | solution.py:283
  67.6 0.7 copy-done.3
  68.4 0.1 broadcast_xor_fusion.2
  68.4 0.1 xor.58
  68.5 0.1 broadcast_xor_fusion.symmetry_ref
  68.6 3.2 %collective-permute-done.7.refs_3_ = f32[4,16,1280]{2,1,0:T(8,128)} collective-permute-done((f32[4,16,1280]{2,1,0:T(8,128)}, f32[4,16,1280]{2,1,0:T(8,128)}, u32[]{:S(2)}, u32[]{:S(2)}) %collective-permute-start.7) | collective-permute-done | bytes 327712 | tf_op jit(solution)/shard_map/ppermute | solution.py:283
  71.8 1.9 %collective-permute-start.8 = (f32[4,16,1280]{2,1,0:T(8,128)}, f32[4,16,1280]{2,1,0:T(8,128)}, u32[]{:S(2)}, u32[]{:S(2)}) collective-permute-start(f32[4,16,1280]{2,1,0:T(8,128)} %collective-permute-done.7.refs_3_), channel_id=1, source_target_pairs={{0,16},{16,32},{32,48},{48,64},{64,80},{80,96},{96,112},{112,128},... | collective-permute-start | bytes 983048 | tf_op jit(solution)/shard_map/ppermute | solution.py:283
  73.7 4.6 %collective-permute-start.4 = (f32[4,16,1280]{2,1,0:T(8,128)S(1)}, f32[4,16,1280]{2,1,0:T(8,128)S(1)}, u32[]{:S(2)}, u32[]{:S(2)}) collective-permute-start(f32[4,16,1280]{2,1,0:T(8,128)S(1)} %collective-permute-done.3.refs_0_), channel_id=1, source_target_pairs={{0,176},{16,0},{32,16},{48,32},{64,48},{80,64},{96,80},{112,96},{1... | collective-permute-start | bytes 983048 | tf_op jit(solution)/shard_map/ppermute | solution.py:283
  78.3 1.2 shard_map.58
  79.5 0.7 copy-done.5
  80.2 0.7 copy-done.6
  80.9 4.0 %all-to-all-done.1.in_ref = f32[32,3,40,128]{3,2,1,0:T(8,128)S(1)} async-done(((f32[32,3,40,128]{3,2,1,0:T(8,128)}), f32[32,3,40,128]{3,2,1,0:T(8,128)S(1)}, u32[]{:S(2)}, u32[]{:S(2)}) %all-to-all-start.1) | async-done | bytes 1966112 | tf_op jit(solution)/shard_map/all_to_all | solution.py:308
  84.9 1.9 %shard_map.59 = (bf16[2,192,1280]{2,1,0:T(8,128)(2,1)S(1)}, bf16[2,192,1280]{2,1,0:T(8,128)(2,1)S(1)}) custom-call(f32[32,3,40,128]{3,2,1,0:T(8,128)S(1)} %all-to-all-done.1.in_ref), custom_call_target="tpu_custom_call" | custom-call | bytes 3932160 | tf_op jit(solution)/shard_map/pallas_call | solution.py:112
  86.9 0.9 copy-done.1
  87.8 0.9 copy-done.2
  88.7 2.2 %collective-permute-start.9 = (f32[4,16,1280]{2,1,0:T(8,128)S(1)}, f32[4,16,1280]{2,1,0:T(8,128)S(1)}, u32[]{:S(2)}, u32[]{:S(2)}) collective-permute-start(f32[4,16,1280]{2,1,0:T(8,128)S(1)} %collective-permute-done.4.refs_1_), channel_id=1, source_target_pairs={{0,176},{16,0},{32,16},{48,32},{64,48},{80,64},{96,80},{112,96},{1... | collective-permute-start | bytes 983048 | tf_op jit(solution)/shard_map/ppermute | solution.py:283
  90.9 3.1 %collective-permute-start.11 = (f32[4,16,1280]{2,1,0:T(8,128)}, f32[4,16,1280]{2,1,0:T(8,128)S(1)}, u32[]{:S(2)}, u32[]{:S(2)}) collective-permute-start(f32[4,16,1280]{2,1,0:T(8,128)} %collective-permute-done.8.refs_4_), channel_id=1, source_target_pairs={{0,16},{16,32},{32,48},{48,64},{64,80},{80,96},{96,112},{112,128},... | collective-permute-start | bytes 983048 | tf_op jit(solution)/shard_map/ppermute | solution.py:283
  94.1 6.2 %shard_map.60 = (f32[8,2,3,4,512]{4,3,2,1,0:T(4,128)}, f32[8,2,3,4,512]{4,3,2,1,0:T(4,128)}) custom-call(s32[1]{0:T(128)} %bitcast.1.core_ref, bf16[2,192,1280]{2,1,0:T(8,128)(2,1)} %copy-done.1, bf16[2,192,1280]{2,1,0:T(8,128)(2,1)} %copy-done.2, f32[4,16,1280]{2,1,0:T(8,128)S(1)} %collective-permute-done.refs_0_, f32[4,16,1280]{2,1,0:T(8,128)S(1)} %copy-done.4, ...), custom_call_target="tpu_custom_call" | custom-call | flops 1509949440 | bytes 8388608 | tf_op jit(solution)/shard_map/pallas_call | solution.py:189
  100.3 3.1 %collective-permute-start.10 = (f32[8,2,3,4,512]{4,3,2,1,0:T(4,128)}, f32[8,2,3,4,512]{4,3,2,1,0:T(4,128)S(1)}, u32[]{:S(2)}, u32[]{:S(2)}) collective-permute-start(f32[8,2,3,4,512]{4,3,2,1,0:T(4,128)} %get-tuple-element.44), channel_id=1, source_target_pairs={{0,1},{1,0},{2,3},{3,2},{4,5},{5,4},{6,7},{7,6},{8,9},{9,8},{10,11... | collective-permute-start | bytes 1179656 | tf_op jit(solution)/shard_map/ppermute | solution.py:321
  103.4 2.7 %shard_map.61 = (f32[8,2,3,4,256]{4,3,2,1,0:T(4,128)S(1)}, f32[8,2,3,4,256]{4,3,2,1,0:T(4,128)S(1)}) custom-call(s32[1]{0:T(128)} %bitcast.1.core_ref, bf16[2,192,1280]{2,1,0:T(8,128)(2,1)} %copy-done.1, bf16[2,192,1280]{2,1,0:T(8,128)(2,1)} %copy-done.2, f32[4,16,1280]{2,1,0:T(8,128)S(1)} %collective-permute-done.3.refs_0_, ...), custom_call_target="tpu_custom_call" | custom-call | flops 754974720 | bytes 8388608 | tf_op jit(solution)/shard_map/pallas_call | solution.py:189
  106.2 2.8 %collective-permute-start.12 = (f32[8,2,3,4,256]{4,3,2,1,0:T(4,128)S(1)}, f32[8,2,3,4,256]{4,3,2,1,0:T(4,128)S(1)}, u32[]{:S(2)}, u32[]{:S(2)}) collective-permute-start(f32[8,2,3,4,256]{4,3,2,1,0:T(4,128)S(1)} %get-tuple-element.47), channel_id=1, source_target_pairs={{0,1},{1,0},{2,3},{3,2},{4,5},{5,4},{6,7},{7,6},{8,9},{9,8},{10,11... | collective-permute-start | bytes 589832 | tf_op jit(solution)/shard_map/ppermute | solution.py:323
  109.0 1.0 collective-permute-done.12
  110.1 0.1 add.15
  110.1 0.1 add.14
  110.2 1.0 pad_maximum_fusion
  111.2 5.7 %all-to-all-start.2 = ((f32[16,3,4,768]{3,2,1,0:T(4,128)}), f32[16,3,4,768]{3,2,1,0:T(4,128)S(1)}, u32[]{:S(2)}, u32[]{:S(2)}) async-start(f32[16,3,4,768]{3,2,1,0:T(4,128)} %bitcast.3), calls=%async_computation.2 | async-start | bytes 1179648 | tf_op jit(solution)/shard_map/all_to_all | solution.py:326
  116.9 17.4 %all-to-all-done.2.parts_ref = f32[16,3,4,768]{3,2,1,0:T(4,128)S(1)} async-done(((f32[16,3,4,768]{3,2,1,0:T(4,128)}), f32[16,3,4,768]{3,2,1,0:T(4,128)S(1)}, u32[]{:S(2)}, u32[]{:S(2)}) %all-to-all-start.2) | async-done | bytes 589856 | tf_op jit(solution)/shard_map/all_to_all | solution.py:326
  134.3 0.9 shard_map.62
  (26 shorter events, 0.1 us)
Async XLA Ops:
  1.8 10.7 %all-to-all-start = ((f32[4,16,1280]{2,1,0:T(8,128)}), f32[4,16,1280]{2,1,0:T(8,128)S(1)}, u32[]{:S(2)}, u32[]{:S(2)}) async-start(f32[4,16,1280]{2,1,0:T(8,128)} %shard_map.55), calls=%async_computation | async-start | bytes 655360 | tf_op jit(solution)/shard_map/all_to_all | solution.py:299
  6.7 1.5 %copy-start = (f32[3,64,4,640]{3,2,1,0:T(4,128)S(1)}, f32[3,64,4,640]{3,2,1,0:T(4,128)}, u32[]{:S(2)}) copy-start(f32[3,64,4,640]{3,2,1,0:T(4,128)} %in_ref.1) | copy-start | bytes 5898244
  12.5 27.0 %collective-permute-start = (f32[4,16,1280]{2,1,0:T(8,128)S(1)}, f32[4,16,1280]{2,1,0:T(8,128)S(1)}, u32[]{:S(2)}, u32[]{:S(2)}) collective-permute-start(f32[4,16,1280]{2,1,0:T(8,128)S(1)} %all-to-all-done.refs_0_), channel_id=1, source_target_pairs={{0,176},{16,0},{32,16},{48,32},{64,48},{80,64},{96,80},{112,96},{1... | collective-permute-start | bytes 983048 | tf_op jit(solution)/shard_map/ppermute | solution.py:283
  27.2 0.7 copy-start.7
  27.2 29.1 %copy-start.10 = (s32[64]{0:T(128)S(1)}, s32[64]{0:T(128)}, u32[]{:S(2)}) copy-start(s32[64]{0:T(128)} %param.9) | copy-start | bytes 772
  27.2 29.1 %copy-start.11 = (s32[12]{0:T(128)S(1)}, s32[12]{0:T(128)}, u32[]{:S(2)}) copy-start(s32[12]{0:T(128)} %param.8) | copy-start | bytes 148
  27.2 41.1 %copy-start.12 = (s32[3]{0:T(128)S(1)}, s32[3]{0:T(128)}, u32[]{:S(2)}) copy-start(s32[3]{0:T(128)} %param.7) | copy-start | bytes 40
  27.9 57.1 %all-to-all-start.1 = ((f32[32,3,40,128]{3,2,1,0:T(8,128)}), f32[32,3,40,128]{3,2,1,0:T(8,128)S(1)}, u32[]{:S(2)}, u32[]{:S(2)}) async-start(f32[32,3,40,128]{3,2,1,0:T(8,128)} %shard_map.56), calls=%async_computation.1 | async-start | bytes 3932160 | tf_op jit(solution)/shard_map/all_to_all | solution.py:308
  37.6 12.2 %collective-permute-start.5 = (f32[4,16,1280]{2,1,0:T(8,128)S(1)}, f32[4,16,1280]{2,1,0:T(8,128)S(1)}, u32[]{:S(2)}, u32[]{:S(2)}) collective-permute-start(f32[4,16,1280]{2,1,0:T(8,128)S(1)} %all-to-all-done.refs_0_), channel_id=1, source_target_pairs={{0,16},{16,32},{32,48},{48,64},{64,80},{80,96},{96,112},{112,128},... | collective-permute-start | bytes 983048 | tf_op jit(solution)/shard_map/ppermute | solution.py:283
  39.5 12.2 %collective-permute-start.1 = (f32[4,16,1280]{2,1,0:T(8,128)S(1)}, f32[4,16,1280]{2,1,0:T(8,128)}, u32[]{:S(2)}, u32[]{:S(2)}) collective-permute-start(f32[4,16,1280]{2,1,0:T(8,128)S(1)} %collective-permute-done.refs_0_), channel_id=1, source_target_pairs={{0,176},{16,0},{32,16},{48,32},{64,48},{80,64},{96,80},{112,96},{1... | collective-permute-start | bytes 983048 | tf_op jit(solution)/shard_map/ppermute | solution.py:283
  49.7 11.4 %collective-permute-start.6 = (f32[4,16,1280]{2,1,0:T(8,128)S(1)}, f32[4,16,1280]{2,1,0:T(8,128)}, u32[]{:S(2)}, u32[]{:S(2)}) collective-permute-start(f32[4,16,1280]{2,1,0:T(8,128)S(1)} %collective-permute-done.5.refs_2_), channel_id=1, source_target_pairs={{0,16},{16,32},{32,48},{48,64},{64,80},{80,96},{96,112},{112,128},... | collective-permute-start | bytes 983048 | tf_op jit(solution)/shard_map/ppermute | solution.py:283
  51.7 11.3 %collective-permute-start.2 = (f32[4,16,1280]{2,1,0:T(8,128)}, f32[4,16,1280]{2,1,0:T(8,128)S(1)}, u32[]{:S(2)}, u32[]{:S(2)}) collective-permute-start(f32[4,16,1280]{2,1,0:T(8,128)} %collective-permute-done.1.refs_0_), channel_id=1, source_target_pairs={{0,176},{16,0},{32,16},{48,32},{64,48},{80,64},{96,80},{112,96},{1... | collective-permute-start | bytes 983048 | tf_op jit(solution)/shard_map/ppermute | solution.py:283
  61.1 10.6 %collective-permute-start.7 = (f32[4,16,1280]{2,1,0:T(8,128)}, f32[4,16,1280]{2,1,0:T(8,128)}, u32[]{:S(2)}, u32[]{:S(2)}) collective-permute-start(f32[4,16,1280]{2,1,0:T(8,128)} %collective-permute-done.6.refs_1_), channel_id=1, source_target_pairs={{0,16},{16,32},{32,48},{48,64},{64,80},{80,96},{96,112},{112,128},... | collective-permute-start | bytes 983048 | tf_op jit(solution)/shard_map/ppermute | solution.py:283
  63.0 10.6 %collective-permute-start.3 = (f32[4,16,1280]{2,1,0:T(8,128)S(1)}, f32[4,16,1280]{2,1,0:T(8,128)S(1)}, u32[]{:S(2)}, u32[]{:S(2)}) collective-permute-start(f32[4,16,1280]{2,1,0:T(8,128)S(1)} %collective-permute-done.2.refs_1_), channel_id=1, source_target_pairs={{0,176},{16,0},{32,16},{48,32},{64,48},{80,64},{96,80},{112,96},{1... | collective-permute-start | bytes 983048 | tf_op jit(solution)/shard_map/ppermute | solution.py:283
  67.6 0.7 copy-start.3
  71.8 19.2 %collective-permute-start.8 = (f32[4,16,1280]{2,1,0:T(8,128)}, f32[4,16,1280]{2,1,0:T(8,128)}, u32[]{:S(2)}, u32[]{:S(2)}) collective-permute-start(f32[4,16,1280]{2,1,0:T(8,128)} %collective-permute-done.7.refs_3_), channel_id=1, source_target_pairs={{0,16},{16,32},{32,48},{48,64},{64,80},{80,96},{96,112},{112,128},... | collective-permute-start | bytes 983048 | tf_op jit(solution)/shard_map/ppermute | solution.py:283
  73.7 15.1 %collective-permute-start.4 = (f32[4,16,1280]{2,1,0:T(8,128)S(1)}, f32[4,16,1280]{2,1,0:T(8,128)S(1)}, u32[]{:S(2)}, u32[]{:S(2)}) collective-permute-start(f32[4,16,1280]{2,1,0:T(8,128)S(1)} %collective-permute-done.3.refs_0_), channel_id=1, source_target_pairs={{0,176},{16,0},{32,16},{48,32},{64,48},{80,64},{96,80},{112,96},{1... | collective-permute-start | bytes 983048 | tf_op jit(solution)/shard_map/ppermute | solution.py:283
  79.4 0.7 copy-start.5
  80.2 0.7 copy-start.6
  84.9 9.1 %copy-start.4 = (f32[4,16,1280]{2,1,0:T(8,128)S(1)}, f32[4,16,1280]{2,1,0:T(8,128)}, u32[]{:S(2)}) copy-start(f32[4,16,1280]{2,1,0:T(8,128)} %copy-done.3) | copy-start | bytes 983044
  84.9 9.1 %copy-start.8 = (bf16[64,1280]{1,0:T(8,128)(2,1)S(1)}, bf16[64,1280]{1,0:T(8,128)(2,1)}, u32[]{:S(2)}) copy-start(bf16[64,1280]{1,0:T(8,128)(2,1)} %copy-done.7) | copy-start | bytes 491524
  86.8 1.0 copy-start.1
  87.8 0.9 copy-start.2
  88.7 11.6 %collective-permute-start.9 = (f32[4,16,1280]{2,1,0:T(8,128)S(1)}, f32[4,16,1280]{2,1,0:T(8,128)S(1)}, u32[]{:S(2)}, u32[]{:S(2)}) collective-permute-start(f32[4,16,1280]{2,1,0:T(8,128)S(1)} %collective-permute-done.4.refs_1_), channel_id=1, source_target_pairs={{0,176},{16,0},{32,16},{48,32},{64,48},{80,64},{96,80},{112,96},{1... | collective-permute-start | bytes 983048 | tf_op jit(solution)/shard_map/ppermute | solution.py:283
  90.9 12.5 %collective-permute-start.11 = (f32[4,16,1280]{2,1,0:T(8,128)}, f32[4,16,1280]{2,1,0:T(8,128)S(1)}, u32[]{:S(2)}, u32[]{:S(2)}) collective-permute-start(f32[4,16,1280]{2,1,0:T(8,128)} %collective-permute-done.8.refs_4_), channel_id=1, source_target_pairs={{0,16},{16,32},{32,48},{48,64},{64,80},{80,96},{96,112},{112,128},... | collective-permute-start | bytes 983048 | tf_op jit(solution)/shard_map/ppermute | solution.py:283
  100.3 9.8 %copy-start.9 = (f32[8,2,3,4,512]{4,3,2,1,0:T(4,128)S(1)}, f32[8,2,3,4,512]{4,3,2,1,0:T(4,128)}, u32[]{:S(2)}) copy-start(f32[8,2,3,4,512]{4,3,2,1,0:T(4,128)} %get-tuple-element.41) | copy-start | bytes 1179652
  100.3 9.8 %collective-permute-start.10 = (f32[8,2,3,4,512]{4,3,2,1,0:T(4,128)}, f32[8,2,3,4,512]{4,3,2,1,0:T(4,128)S(1)}, u32[]{:S(2)}, u32[]{:S(2)}) collective-permute-start(f32[8,2,3,4,512]{4,3,2,1,0:T(4,128)} %get-tuple-element.44), channel_id=1, source_target_pairs={{0,1},{1,0},{2,3},{3,2},{4,5},{5,4},{6,7},{7,6},{8,9},{9,8},{10,11... | collective-permute-start | bytes 1179656 | tf_op jit(solution)/shard_map/ppermute | solution.py:321
  106.2 3.9 %collective-permute-start.12 = (f32[8,2,3,4,256]{4,3,2,1,0:T(4,128)S(1)}, f32[8,2,3,4,256]{4,3,2,1,0:T(4,128)S(1)}, u32[]{:S(2)}, u32[]{:S(2)}) collective-permute-start(f32[8,2,3,4,256]{4,3,2,1,0:T(4,128)S(1)} %get-tuple-element.47), channel_id=1, source_target_pairs={{0,1},{1,0},{2,3},{3,2},{4,5},{5,4},{6,7},{7,6},{8,9},{9,8},{10,11... | collective-permute-start | bytes 589832 | tf_op jit(solution)/shard_map/ppermute | solution.py:323
  111.2 23.1 %all-to-all-start.2 = ((f32[16,3,4,768]{3,2,1,0:T(4,128)}), f32[16,3,4,768]{3,2,1,0:T(4,128)S(1)}, u32[]{:S(2)}, u32[]{:S(2)}) async-start(f32[16,3,4,768]{3,2,1,0:T(4,128)} %bitcast.3), calls=%async_computation.2 | async-start | bytes 1179648 | tf_op jit(solution)/shard_map/all_to_all | solution.py:326

commit v7 on v6

--- a/solution.py
+++ b/solution.py
@@ -115,7 +115,7 @@
         in_specs=[VMEM],
         out_specs=(VMEM, VMEM),
         scratch_shapes=[pltpu.VMEM((2, occupied, lanes), jnp.float32)] * 2,
-        compiler_params=pltpu.CompilerParams(vmem_limit_bytes=8 * MIB),
+        compiler_params=pltpu.CompilerParams(vmem_limit_bytes=53 * MIB),
         cost_estimate=pl.CostEstimate(flops=0, bytes_accessed=8 * got.size, transcendentals=0),
     )(got)
 
@@ -152,7 +152,7 @@
         )
 
     ys, xls, window, local = own_ref.shape[:4]
-    group = 4
+    group = total_count
     for first in range(0, total_count, group):
         if first + group == total_count:
             for copy in ready:
@@ -199,7 +199,7 @@
             pltpu.VMEM((block, depth), jnp.bfloat16),
             pltpu.SemaphoreType.DMA((count + 4 + len(ready),)),
         ],
-        compiler_params=pltpu.CompilerParams(vmem_limit_bytes=52 * MIB),
+        compiler_params=pltpu.CompilerParams(vmem_limit_bytes=53 * MIB),
         cost_estimate=pl.CostEstimate(
             flops=12 * rows * depth * block, bytes_accessed=8 << 20, transcendentals=0
         ),
@@ -225,9 +225,9 @@
         out_shape=(shape, shape),
         in_specs=[VMEM] * len(blocks),
         out_specs=(VMEM, VMEM),
-        compiler_params=pltpu.CompilerParams(vmem_limit_bytes=8 * MIB),
+        compiler_params=pltpu.CompilerParams(vmem_limit_bytes=53 * MIB),
         cost_estimate=pl.CostEstimate(
-            flops=28_000_000_000, bytes_accessed=8 * blocks[0].size, transcendentals=0
+            flops=22_000_000_000, bytes_accessed=8 * blocks[0].size, transcendentals=0
         ),
     )(*blocks)
 
@@ -271,7 +271,7 @@
         in_specs=[pl.BlockSpec(memory_space=pltpu.SMEM), VMEM, VMEM],
         out_specs=VMEM,
         scratch_shapes=[pltpu.VMEM((16, columns), jnp.float32)],
-        compiler_params=pltpu.CompilerParams(vmem_limit_bytes=8 * MIB),
+        compiler_params=pltpu.CompilerParams(vmem_limit_bytes=53 * MIB),
     )(z, parts, symmetry)
 
 
@@ -309,8 +309,7 @@
     packed, symmetry, *nearby = lax.optimization_barrier((packed, symmetry, *nearby))
     halves += nearby
     high, low = spin_rows(packed)
-    last, high, low = lax.optimization_barrier((ahead[-1], high, low))
-    ahead += gather(last, "z", 1, 1)
+    ahead += gather(ahead[-1], "z", 1, 1)
 
     core = lax.axis_index("core").astype(jnp.int32).reshape(1)
     swap = [(0, 1), (1, 0)]

time: 136 us -> 142 us (1.044)
  starting transfers between devices: 71.9 us -> 77.2 us
  Pallas kernels: 17.6 us -> 19.1 us
    all_to_all x1, waiting for transfers between devices: 4.03 us -> 0.01 us  [body(): packed = lax.all_to_all(packed, ('y', 'core', 'xl'), 0, 0, tiled=True)]
    ppermute x11, waiting for transfers between devices: 13.5 us -> 17.5 us  [gather(): blocks.append(lax.ppermute(blocks[-1], axis, pairs))]
    ppermute x1, starting transfers between devices: 3.1 us -> 6.41 us  [body(): taken = lax.ppermute(given, 'core', swap)]
    pallas_call x1, Pallas kernels: 1.92 us -> 4.38 us  [spin_rows(): pl.pallas_call(spin_kernel, out_shape=(shape, shape), in_specs=[VMEM], ou...]
    all_to_all x1, starting transfers between devices: 5.66 us -> 7.16 us  [body(): partial = lax.all_to_all(partial, ('y', 'xl'), 0, 0, tiled=True)]
    unnamed x26 -> x20, local copies, waits for them, and re-layouts: 6.24 us -> 5.25 us
  transfers between devices with their start and end apart: 16 -> 16, of which waited for: 7 -> 7; matrix products, arithmetic and copies ran while one was open for 0% -> 0% of each run, Pallas kernels for 11% -> 12%
where the time goes in v7:
time: 142 us; the launch traced here: 141 us
  starting transfers between devices  77.2 us (54%)
  waiting for transfers between devices  37.8 us (27%)
  Pallas kernels  19.1 us (13%)
  local copies, waits for them, and re-layouts  5.4 us (4%)
    ppermute x11, starting transfers between devices, gather(): blocks.append(lax.ppermute(blocks[-1], axis, pairs))  47 us
    ppermute x11, waiting for transfers between devices, gather(): blocks.append(lax.ppermute(blocks[-1], axis, pairs))  17.5 us
    all_to_all x1, waiting for transfers between devices, body(): partial = lax.all_to_all(partial, ('y', 'xl'), 0, 0, tiled=True)  17.4 us
    all_to_all x1, starting transfers between devices, body(): packed = lax.all_to_all(packed, ('y', 'core', 'xl'), 0, 0, tiled=True)  9.84 us
    pallas_call x2, Pallas kernels, product(): pl.pallas_call(functools.partial(product_kernel, len(columns)), out_shape...  8.12 us
    all_to_all x1, starting transfers between devices, body(): partial = lax.all_to_all(partial, ('y', 'xl'), 0, 0, tiled=True)  7.16 us
    ppermute x1, starting transfers between devices, body(): taken = lax.ppermute(given, 'core', swap)  6.41 us
    unnamed x20, local copies, waits for them, and re-layouts  5.25 us
  transfers between devices with their start and end apart: 16, of which 7 were waited for; matrix products, arithmetic and copies ran while one was open for 0% of the time, Pallas kernels for 12%

profile of v7, /device:TPU:1, one launch (start us, length us, event | category | flops | bytes accessed | tf_op | source)
XLA Modules:
  0.0 141.2 jit_solution(3433607404845504720)
XLA Ops:
  0.0 1.8 %shard_map.56 = f32[4,16,1280]{2,1,0:T(8,128)} custom-call(f32[40,16,64]{2,1,0:T(8,128)} %bitcast.4), custom_call_target="tpu_custom_call" | custom-call | tf_op jit(solution)/shard_map/pallas_call | solution.py:27
  1.8 4.8 %all-to-all-start = ((f32[4,16,1280]{2,1,0:T(8,128)}), f32[4,16,1280]{2,1,0:T(8,128)S(1)}, u32[]{:S(2)}, u32[]{:S(2)}) async-start(f32[4,16,1280]{2,1,0:T(8,128)} %shard_map.56), calls=%async_computation | async-start | bytes 655360 | tf_op jit(solution)/shard_map/all_to_all | solution.py:299
  6.6 1.5 %copy-done = f32[3,64,4,640]{3,2,1,0:T(4,128)S(1)} copy-done((f32[3,64,4,640]{3,2,1,0:T(4,128)S(1)}, f32[3,64,4,640]{3,2,1,0:T(4,128)}, u32[]{:S(2)}) %copy-start) | copy-done | bytes 1966104
  8.2 2.8 %shard_map.55 = f32[32,3,40,128]{3,2,1,0:T(8,128)} custom-call(f32[3,64,4,640]{3,2,1,0:T(4,128)S(1)} %copy-done), custom_call_target="tpu_custom_call" | custom-call | bytes 3932160 | tf_op jit(solution)/shard_map/pallas_call | solution.py:60
  11.0 1.5 %all-to-all-done.refs_0_ = f32[4,16,1280]{2,1,0:T(8,128)S(1)} async-done(((f32[4,16,1280]{2,1,0:T(8,128)}), f32[4,16,1280]{2,1,0:T(8,128)S(1)}, u32[]{:S(2)}, u32[]{:S(2)}) %all-to-all-start) | async-done | bytes 327712 | tf_op jit(solution)/shard_map/all_to_all | solution.py:299
  12.5 14.6 %collective-permute-start = (f32[4,16,1280]{2,1,0:T(8,128)S(1)}, f32[4,16,1280]{2,1,0:T(8,128)S(1)}, u32[]{:S(2)}, u32[]{:S(2)}) collective-permute-start(f32[4,16,1280]{2,1,0:T(8,128)S(1)} %all-to-all-done.refs_0_), channel_id=1, source_target_pairs={{0,176},{16,0},{32,16},{48,32},{64,48},{80,64},{96,80},{112,96},{1... | collective-permute-start | bytes 983048 | tf_op jit(solution)/shard_map/ppermute | solution.py:283
  27.1 0.1 shard_map.57
  27.2 0.0 copy-start.6
  27.2 0.0 copy-start.7
  27.2 0.0 copy-start.8
  27.2 9.8 %all-to-all-start.1 = ((f32[32,3,40,128]{3,2,1,0:T(8,128)}), f32[32,3,40,128]{3,2,1,0:T(8,128)S(1)}, u32[]{:S(2)}, u32[]{:S(2)}) async-start(f32[32,3,40,128]{3,2,1,0:T(8,128)} %shard_map.55), calls=%async_computation.1 | async-start | bytes 3932160 | tf_op jit(solution)/shard_map/all_to_all | solution.py:308
  37.1 1.9 %collective-permute-start.2 = (f32[4,16,1280]{2,1,0:T(8,128)S(1)}, f32[4,16,1280]{2,1,0:T(8,128)S(1)}, u32[]{:S(2)}, u32[]{:S(2)}) collective-permute-start(f32[4,16,1280]{2,1,0:T(8,128)S(1)} %all-to-all-done.refs_0_), channel_id=1, source_target_pairs={{0,16},{16,32},{32,48},{48,64},{64,80},{80,96},{96,112},{112,128},... | collective-permute-start | bytes 983048 | tf_op jit(solution)/shard_map/ppermute | solution.py:283
  39.0 0.0 collective-permute-done.refs_0_
  39.0 4.6 %collective-permute-start.1 = (f32[4,16,1280]{2,1,0:T(8,128)S(1)}, f32[4,16,1280]{2,1,0:T(8,128)S(1)}, u32[]{:S(2)}, u32[]{:S(2)}) collective-permute-start(f32[4,16,1280]{2,1,0:T(8,128)S(1)} %collective-permute-done.refs_0_), channel_id=1, source_target_pairs={{0,176},{16,0},{32,16},{48,32},{64,48},{80,64},{96,80},{112,96},{1... | collective-permute-start | bytes 983048 | tf_op jit(solution)/shard_map/ppermute | solution.py:283
  43.6 5.7 %collective-permute-done.2.refs_2_ = f32[4,16,1280]{2,1,0:T(8,128)S(1)} collective-permute-done((f32[4,16,1280]{2,1,0:T(8,128)S(1)}, f32[4,16,1280]{2,1,0:T(8,128)S(1)}, u32[]{:S(2)}, u32[]{:S(2)}) %collective-permute-start.2) | collective-permute-done | bytes 327712 | tf_op jit(solution)/shard_map/ppermute | solution.py:283
  49.2 1.9 %collective-permute-start.3 = (f32[4,16,1280]{2,1,0:T(8,128)S(1)}, f32[4,16,1280]{2,1,0:T(8,128)}, u32[]{:S(2)}, u32[]{:S(2)}) collective-permute-start(f32[4,16,1280]{2,1,0:T(8,128)S(1)} %collective-permute-done.2.refs_2_), channel_id=1, source_target_pairs={{0,16},{16,32},{32,48},{48,64},{64,80},{80,96},{96,112},{112,128},... | collective-permute-start | bytes 983048 | tf_op jit(solution)/shard_map/ppermute | solution.py:283
  51.2 4.6 %collective-permute-start.4 = (f32[4,16,1280]{2,1,0:T(8,128)S(1)}, f32[4,16,1280]{2,1,0:T(8,128)}, u32[]{:S(2)}, u32[]{:S(2)}) collective-permute-start(f32[4,16,1280]{2,1,0:T(8,128)S(1)} %collective-permute-done.1.refs_0_), channel_id=1, source_target_pairs={{0,176},{16,0},{32,16},{48,32},{64,48},{80,64},{96,80},{112,96},{1... | collective-permute-start | bytes 983048 | tf_op jit(solution)/shard_map/ppermute | solution.py:283
  55.8 4.8 %collective-permute-done.3.refs_1_ = f32[4,16,1280]{2,1,0:T(8,128)} collective-permute-done((f32[4,16,1280]{2,1,0:T(8,128)S(1)}, f32[4,16,1280]{2,1,0:T(8,128)}, u32[]{:S(2)}, u32[]{:S(2)}) %collective-permute-start.3) | collective-permute-done | bytes 327712 | tf_op jit(solution)/shard_map/ppermute | solution.py:283
  60.6 1.9 %collective-permute-start.5 = (f32[4,16,1280]{2,1,0:T(8,128)}, f32[4,16,1280]{2,1,0:T(8,128)}, u32[]{:S(2)}, u32[]{:S(2)}) collective-permute-start(f32[4,16,1280]{2,1,0:T(8,128)} %collective-permute-done.3.refs_1_), channel_id=1, source_target_pairs={{0,16},{16,32},{32,48},{48,64},{64,80},{80,96},{96,112},{112,128},... | collective-permute-start | bytes 983048 | tf_op jit(solution)/shard_map/ppermute | solution.py:283
  62.5 4.6 %collective-permute-start.7 = (f32[4,16,1280]{2,1,0:T(8,128)}, f32[4,16,1280]{2,1,0:T(8,128)S(1)}, u32[]{:S(2)}, u32[]{:S(2)}) collective-permute-start(f32[4,16,1280]{2,1,0:T(8,128)} %collective-permute-done.4.refs_1_), channel_id=1, source_target_pairs={{0,176},{16,0},{32,16},{48,32},{64,48},{80,64},{96,80},{112,96},{1... | collective-permute-start | bytes 983048 | tf_op jit(solution)/shard_map/ppermute | solution.py:283
  67.1 0.1 dynamic_slice.3
  67.2 0.1 broadcast_xor_fusion.1
  67.3 4.0 %collective-permute-done.5.refs_3_ = f32[4,16,1280]{2,1,0:T(8,128)} collective-permute-done((f32[4,16,1280]{2,1,0:T(8,128)}, f32[4,16,1280]{2,1,0:T(8,128)}, u32[]{:S(2)}, u32[]{:S(2)}) %collective-permute-start.5) | collective-permute-done | bytes 327712 | tf_op jit(solution)/shard_map/ppermute | solution.py:283
  71.2 1.9 %collective-permute-start.6 = (f32[4,16,1280]{2,1,0:T(8,128)}, f32[4,16,1280]{2,1,0:T(8,128)}, u32[]{:S(2)}, u32[]{:S(2)}) collective-permute-start(f32[4,16,1280]{2,1,0:T(8,128)} %collective-permute-done.5.refs_3_), channel_id=1, source_target_pairs={{0,16},{16,32},{32,48},{48,64},{64,80},{80,96},{96,112},{112,128},... | collective-permute-start | bytes 983048 | tf_op jit(solution)/shard_map/ppermute | solution.py:283
  73.2 4.6 %collective-permute-start.8 = (f32[4,16,1280]{2,1,0:T(8,128)S(1)}, f32[4,16,1280]{2,1,0:T(8,128)}, u32[]{:S(2)}, u32[]{:S(2)}) collective-permute-start(f32[4,16,1280]{2,1,0:T(8,128)S(1)} %collective-permute-done.7.refs_0_), channel_id=1, source_target_pairs={{0,176},{16,0},{32,16},{48,32},{64,48},{80,64},{96,80},{112,96},{1... | collective-permute-start | bytes 983048 | tf_op jit(solution)/shard_map/ppermute | solution.py:283
  77.8 0.1 broadcast_xor_fusion.2
  77.8 0.1 xor.58
  77.9 0.1 broadcast_xor_fusion.symmetry_ref
  78.0 3.0 %collective-permute-done.6.refs_4_ = f32[4,16,1280]{2,1,0:T(8,128)} collective-permute-done((f32[4,16,1280]{2,1,0:T(8,128)}, f32[4,16,1280]{2,1,0:T(8,128)}, u32[]{:S(2)}, u32[]{:S(2)}) %collective-permute-start.6) | collective-permute-done | bytes 327712 | tf_op jit(solution)/shard_map/ppermute | solution.py:283
  81.0 1.9 %collective-permute-start.11 = (f32[4,16,1280]{2,1,0:T(8,128)}, f32[4,16,1280]{2,1,0:T(8,128)}, u32[]{:S(2)}, u32[]{:S(2)}) collective-permute-start(f32[4,16,1280]{2,1,0:T(8,128)} %collective-permute-done.6.refs_4_), channel_id=1, source_target_pairs={{0,16},{16,32},{32,48},{48,64},{64,80},{80,96},{96,112},{112,128},... | collective-permute-start | bytes 983048 | tf_op jit(solution)/shard_map/ppermute | solution.py:283
  82.9 4.6 %collective-permute-start.9 = (f32[4,16,1280]{2,1,0:T(8,128)}, f32[4,16,1280]{2,1,0:T(8,128)}, u32[]{:S(2)}, u32[]{:S(2)}) collective-permute-start(f32[4,16,1280]{2,1,0:T(8,128)} %collective-permute-done.8.refs_1_), channel_id=1, source_target_pairs={{0,176},{16,0},{32,16},{48,32},{64,48},{80,64},{96,80},{112,96},{1... | collective-permute-start | bytes 983048 | tf_op jit(solution)/shard_map/ppermute | solution.py:283
  87.5 1.1 shard_map.58
  88.6 0.7 copy-done.2
  89.3 0.7 copy-done.3
  90.0 1.3 copy-done.4
  91.3 4.4 %shard_map.59 = (bf16[2,192,1280]{2,1,0:T(8,128)(2,1)S(1)}, bf16[2,192,1280]{2,1,0:T(8,128)(2,1)}) custom-call(f32[32,3,40,128]{3,2,1,0:T(8,128)} %copy-done.4), custom_call_target="tpu_custom_call" | custom-call | bytes 3932160 | tf_op jit(solution)/shard_map/pallas_call | solution.py:112
  95.7 1.0 copy-done.1
  96.6 5.2 %shard_map.60 = (f32[8,2,3,4,512]{4,3,2,1,0:T(4,128)}, f32[8,2,3,4,512]{4,3,2,1,0:T(4,128)}) custom-call(s32[1]{0:T(128)} %bitcast.1.core_ref, bf16[2,192,1280]{2,1,0:T(8,128)(2,1)} %copy-done.1, bf16[2,192,1280]{2,1,0:T(8,128)(2,1)} %get-tuple-element.31.low_ref, f32[4,16,1280]{2,1,0:T(8,128)S(1)} %collective-permute-done.refs_0_, ...), custom_call_target="tpu_custom_call" | custom-call | flops 1509949440 | bytes 8388608 | tf_op jit(solution)/shard_map/pallas_call | solution.py:189
  101.8 6.4 %collective-permute-start.10 = (f32[8,2,3,4,512]{4,3,2,1,0:T(4,128)}, f32[8,2,3,4,512]{4,3,2,1,0:T(4,128)S(1)}, u32[]{:S(2)}, u32[]{:S(2)}) collective-permute-start(f32[8,2,3,4,512]{4,3,2,1,0:T(4,128)} %get-tuple-element.38), channel_id=1, source_target_pairs={{0,1},{1,0},{2,3},{3,2},{4,5},{5,4},{6,7},{7,6},{8,9},{9,8},{10,11... | collective-permute-start | bytes 1179656 | tf_op jit(solution)/shard_map/ppermute | solution.py:320
  108.3 2.9 %shard_map.61 = (f32[8,2,3,4,256]{4,3,2,1,0:T(4,128)S(1)}, f32[8,2,3,4,256]{4,3,2,1,0:T(4,128)S(1)}) custom-call(s32[1]{0:T(128)} %bitcast.1.core_ref, bf16[2,192,1280]{2,1,0:T(8,128)(2,1)} %copy-done.1, bf16[2,192,1280]{2,1,0:T(8,128)(2,1)} %get-tuple-element.31.low_ref, f32[4,16,1280]{2,1,0:T(8,128)S(1)} %collective-permute-done.7.refs_0_, ...), custom_call_target="tpu_custom_call" | custom-call | flops 754974720 | bytes 8388608 | tf_op jit(solution)/shard_map/pallas_call | solution.py:189
  111.2 1.9 %collective-permute-start.12 = (f32[8,2,3,4,256]{4,3,2,1,0:T(4,128)S(1)}, f32[8,2,3,4,256]{4,3,2,1,0:T(4,128)S(1)}, u32[]{:S(2)}, u32[]{:S(2)}) collective-permute-start(f32[8,2,3,4,256]{4,3,2,1,0:T(4,128)S(1)} %get-tuple-element.41), channel_id=1, source_target_pairs={{0,1},{1,0},{2,3},{3,2},{4,5},{5,4},{6,7},{7,6},{8,9},{9,8},{10,11... | collective-permute-start | bytes 589832 | tf_op jit(solution)/shard_map/ppermute | solution.py:322
  113.2 1.4 collective-permute-done.12
  114.6 0.1 add.15
  114.6 0.1 add.14
  114.7 1.0 pad_maximum_fusion
  115.7 7.2 %all-to-all-start.2 = ((f32[16,3,4,768]{3,2,1,0:T(4,128)}), f32[16,3,4,768]{3,2,1,0:T(4,128)S(1)}, u32[]{:S(2)}, u32[]{:S(2)}) async-start(f32[16,3,4,768]{3,2,1,0:T(4,128)} %bitcast.3), calls=%async_computation.2 | async-start | bytes 1179648 | tf_op jit(solution)/shard_map/all_to_all | solution.py:325
  122.9 17.4 %all-to-all-done.2.parts_ref = f32[16,3,4,768]{3,2,1,0:T(4,128)S(1)} async-done(((f32[16,3,4,768]{3,2,1,0:T(4,128)}), f32[16,3,4,768]{3,2,1,0:T(4,128)S(1)}, u32[]{:S(2)}, u32[]{:S(2)}) %all-to-all-start.2) | async-done | bytes 589856 | tf_op jit(solution)/shard_map/all_to_all | solution.py:325
  140.3 0.9 shard_map.62
  (20 shorter events, 0.0 us)
Async XLA Ops:
  1.8 10.7 %all-to-all-start = ((f32[4,16,1280]{2,1,0:T(8,128)}), f32[4,16,1280]{2,1,0:T(8,128)S(1)}, u32[]{:S(2)}, u32[]{:S(2)}) async-start(f32[4,16,1280]{2,1,0:T(8,128)} %shard_map.56), calls=%async_computation | async-start | bytes 655360 | tf_op jit(solution)/shard_map/all_to_all | solution.py:299
  6.6 1.5 %copy-start = (f32[3,64,4,640]{3,2,1,0:T(4,128)S(1)}, f32[3,64,4,640]{3,2,1,0:T(4,128)}, u32[]{:S(2)}) copy-start(f32[3,64,4,640]{3,2,1,0:T(4,128)} %in_ref.1) | copy-start | bytes 5898244
  12.5 26.5 %collective-permute-start = (f32[4,16,1280]{2,1,0:T(8,128)S(1)}, f32[4,16,1280]{2,1,0:T(8,128)S(1)}, u32[]{:S(2)}, u32[]{:S(2)}) collective-permute-start(f32[4,16,1280]{2,1,0:T(8,128)S(1)} %all-to-all-done.refs_0_), channel_id=1, source_target_pairs={{0,176},{16,0},{32,16},{48,32},{64,48},{80,64},{96,80},{112,96},{1... | collective-permute-start | bytes 983048 | tf_op jit(solution)/shard_map/ppermute | solution.py:283
  27.2 40.0 %copy-start.6 = (s32[64]{0:T(128)S(1)}, s32[64]{0:T(128)}, u32[]{:S(2)}) copy-start(s32[64]{0:T(128)} %param.9) | copy-start | bytes 772
  27.2 40.0 %copy-start.7 = (s32[12]{0:T(128)S(1)}, s32[12]{0:T(128)}, u32[]{:S(2)}) copy-start(s32[12]{0:T(128)} %param.8) | copy-start | bytes 148
  27.2 50.6 %copy-start.8 = (s32[3]{0:T(128)S(1)}, s32[3]{0:T(128)}, u32[]{:S(2)}) copy-start(s32[3]{0:T(128)} %param.7) | copy-start | bytes 40
  27.2 62.8 %all-to-all-start.1 = ((f32[32,3,40,128]{3,2,1,0:T(8,128)}), f32[32,3,40,128]{3,2,1,0:T(8,128)S(1)}, u32[]{:S(2)}, u32[]{:S(2)}) async-start(f32[32,3,40,128]{3,2,1,0:T(8,128)} %shard_map.55), calls=%async_computation.1 | async-start | bytes 3932160 | tf_op jit(solution)/shard_map/all_to_all | solution.py:308
  37.1 12.2 %collective-permute-start.2 = (f32[4,16,1280]{2,1,0:T(8,128)S(1)}, f32[4,16,1280]{2,1,0:T(8,128)S(1)}, u32[]{:S(2)}, u32[]{:S(2)}) collective-permute-start(f32[4,16,1280]{2,1,0:T(8,128)S(1)} %all-to-all-done.refs_0_), channel_id=1, source_target_pairs={{0,16},{16,32},{32,48},{48,64},{64,80},{80,96},{96,112},{112,128},... | collective-permute-start | bytes 983048 | tf_op jit(solution)/shard_map/ppermute | solution.py:283
  39.0 12.2 %collective-permute-start.1 = (f32[4,16,1280]{2,1,0:T(8,128)S(1)}, f32[4,16,1280]{2,1,0:T(8,128)S(1)}, u32[]{:S(2)}, u32[]{:S(2)}) collective-permute-start(f32[4,16,1280]{2,1,0:T(8,128)S(1)} %collective-permute-done.refs_0_), channel_id=1, source_target_pairs={{0,176},{16,0},{32,16},{48,32},{64,48},{80,64},{96,80},{112,96},{1... | collective-permute-start | bytes 983048 | tf_op jit(solution)/shard_map/ppermute | solution.py:283
  49.2 13.3 %copy-start.9 = (f32[4,16,1280]{2,1,0:T(8,128)}, f32[4,16,1280]{2,1,0:T(8,128)S(1)}, u32[]{:S(2)}) copy-start(f32[4,16,1280]{2,1,0:T(8,128)S(1)} %collective-permute-done.2.refs_2_) | copy-start | bytes 983044
  49.2 11.4 %collective-permute-start.3 = (f32[4,16,1280]{2,1,0:T(8,128)S(1)}, f32[4,16,1280]{2,1,0:T(8,128)}, u32[]{:S(2)}, u32[]{:S(2)}) collective-permute-start(f32[4,16,1280]{2,1,0:T(8,128)S(1)} %collective-permute-done.2.refs_2_), channel_id=1, source_target_pairs={{0,16},{16,32},{32,48},{48,64},{64,80},{80,96},{96,112},{112,128},... | collective-permute-start | bytes 983048 | tf_op jit(solution)/shard_map/ppermute | solution.py:283
  51.2 11.3 %collective-permute-start.4 = (f32[4,16,1280]{2,1,0:T(8,128)S(1)}, f32[4,16,1280]{2,1,0:T(8,128)}, u32[]{:S(2)}, u32[]{:S(2)}) collective-permute-start(f32[4,16,1280]{2,1,0:T(8,128)S(1)} %collective-permute-done.1.refs_0_), channel_id=1, source_target_pairs={{0,176},{16,0},{32,16},{48,32},{64,48},{80,64},{96,80},{112,96},{1... | collective-permute-start | bytes 983048 | tf_op jit(solution)/shard_map/ppermute | solution.py:283
  60.6 10.6 %collective-permute-start.5 = (f32[4,16,1280]{2,1,0:T(8,128)}, f32[4,16,1280]{2,1,0:T(8,128)}, u32[]{:S(2)}, u32[]{:S(2)}) collective-permute-start(f32[4,16,1280]{2,1,0:T(8,128)} %collective-permute-done.3.refs_1_), channel_id=1, source_target_pairs={{0,16},{16,32},{32,48},{48,64},{64,80},{80,96},{96,112},{112,128},... | collective-permute-start | bytes 983048 | tf_op jit(solution)/shard_map/ppermute | solution.py:283
  62.5 10.6 %collective-permute-start.7 = (f32[4,16,1280]{2,1,0:T(8,128)}, f32[4,16,1280]{2,1,0:T(8,128)S(1)}, u32[]{:S(2)}, u32[]{:S(2)}) collective-permute-start(f32[4,16,1280]{2,1,0:T(8,128)} %collective-permute-done.4.refs_1_), channel_id=1, source_target_pairs={{0,176},{16,0},{32,16},{48,32},{64,48},{80,64},{96,80},{112,96},{1... | collective-permute-start | bytes 983048 | tf_op jit(solution)/shard_map/ppermute | solution.py:283
  71.2 9.7 %collective-permute-start.6 = (f32[4,16,1280]{2,1,0:T(8,128)}, f32[4,16,1280]{2,1,0:T(8,128)}, u32[]{:S(2)}, u32[]{:S(2)}) collective-permute-start(f32[4,16,1280]{2,1,0:T(8,128)} %collective-permute-done.5.refs_3_), channel_id=1, source_target_pairs={{0,16},{16,32},{32,48},{48,64},{64,80},{80,96},{96,112},{112,128},... | collective-permute-start | bytes 983048 | tf_op jit(solution)/shard_map/ppermute | solution.py:283
  73.2 9.7 %collective-permute-start.8 = (f32[4,16,1280]{2,1,0:T(8,128)S(1)}, f32[4,16,1280]{2,1,0:T(8,128)}, u32[]{:S(2)}, u32[]{:S(2)}) collective-permute-start(f32[4,16,1280]{2,1,0:T(8,128)S(1)} %collective-permute-done.7.refs_0_), channel_id=1, source_target_pairs={{0,176},{16,0},{32,16},{48,32},{64,48},{80,64},{96,80},{112,96},{1... | collective-permute-start | bytes 983048 | tf_op jit(solution)/shard_map/ppermute | solution.py:283
  81.0 27.3 %collective-permute-start.11 = (f32[4,16,1280]{2,1,0:T(8,128)}, f32[4,16,1280]{2,1,0:T(8,128)}, u32[]{:S(2)}, u32[]{:S(2)}) collective-permute-start(f32[4,16,1280]{2,1,0:T(8,128)} %collective-permute-done.6.refs_4_), channel_id=1, source_target_pairs={{0,16},{16,32},{32,48},{48,64},{64,80},{80,96},{96,112},{112,128},... | collective-permute-start | bytes 983048 | tf_op jit(solution)/shard_map/ppermute | solution.py:283
  82.9 18.9 %collective-permute-start.9 = (f32[4,16,1280]{2,1,0:T(8,128)}, f32[4,16,1280]{2,1,0:T(8,128)}, u32[]{:S(2)}, u32[]{:S(2)}) collective-permute-start(f32[4,16,1280]{2,1,0:T(8,128)} %collective-permute-done.8.refs_1_), channel_id=1, source_target_pairs={{0,176},{16,0},{32,16},{48,32},{64,48},{80,64},{96,80},{112,96},{1... | collective-permute-start | bytes 983048 | tf_op jit(solution)/shard_map/ppermute | solution.py:283
  88.6 0.7 copy-start.2
  89.3 0.7 copy-start.3
  90.0 1.3 copy-start.4
  95.7 1.0 copy-start.1
  101.8 12.8 %copy-start.5 = (f32[8,2,3,4,512]{4,3,2,1,0:T(4,128)S(1)}, f32[8,2,3,4,512]{4,3,2,1,0:T(4,128)}, u32[]{:S(2)}) copy-start(f32[8,2,3,4,512]{4,3,2,1,0:T(4,128)} %get-tuple-element.36) | copy-start | bytes 1179652
  101.8 12.8 %collective-permute-start.10 = (f32[8,2,3,4,512]{4,3,2,1,0:T(4,128)}, f32[8,2,3,4,512]{4,3,2,1,0:T(4,128)S(1)}, u32[]{:S(2)}, u32[]{:S(2)}) collective-permute-start(f32[8,2,3,4,512]{4,3,2,1,0:T(4,128)} %get-tuple-element.38), channel_id=1, source_target_pairs={{0,1},{1,0},{2,3},{3,2},{4,5},{5,4},{6,7},{7,6},{8,9},{9,8},{10,11... | collective-permute-start | bytes 1179656 | tf_op jit(solution)/shard_map/ppermute | solution.py:320
  111.2 3.3 %collective-permute-start.12 = (f32[8,2,3,4,256]{4,3,2,1,0:T(4,128)S(1)}, f32[8,2,3,4,256]{4,3,2,1,0:T(4,128)S(1)}, u32[]{:S(2)}, u32[]{:S(2)}) collective-permute-start(f32[8,2,3,4,256]{4,3,2,1,0:T(4,128)S(1)} %get-tuple-element.41), channel_id=1, source_target_pairs={{0,1},{1,0},{2,3},{3,2},{4,5},{5,4},{6,7},{7,6},{8,9},{9,8},{10,11... | collective-permute-start | bytes 589832 | tf_op jit(solution)/shard_map/ppermute | solution.py:322
  115.7 24.6 %all-to-all-start.2 = ((f32[16,3,4,768]{3,2,1,0:T(4,128)}), f32[16,3,4,768]{3,2,1,0:T(4,128)S(1)}, u32[]{:S(2)}, u32[]{:S(2)}) async-start(f32[16,3,4,768]{3,2,1,0:T(4,128)} %bitcast.3), calls=%async_computation.2 | async-start | bytes 1179648 | tf_op jit(solution)/shard_map/all_to_all | solution.py:325

commit v8 on v7

--- a/solution.py
+++ b/solution.py
@@ -115,7 +115,7 @@
         in_specs=[VMEM],
         out_specs=(VMEM, VMEM),
         scratch_shapes=[pltpu.VMEM((2, occupied, lanes), jnp.float32)] * 2,
-        compiler_params=pltpu.CompilerParams(vmem_limit_bytes=53 * MIB),
+        compiler_params=pltpu.CompilerParams(vmem_limit_bytes=8 * MIB),
         cost_estimate=pl.CostEstimate(flops=0, bytes_accessed=8 * got.size, transcendentals=0),
     )(got)
 
@@ -225,9 +225,9 @@
         out_shape=(shape, shape),
         in_specs=[VMEM] * len(blocks),
         out_specs=(VMEM, VMEM),
-        compiler_params=pltpu.CompilerParams(vmem_limit_bytes=53 * MIB),
+        compiler_params=pltpu.CompilerParams(vmem_limit_bytes=8 * MIB),
         cost_estimate=pl.CostEstimate(
-            flops=22_000_000_000, bytes_accessed=8 * blocks[0].size, transcendentals=0
+            flops=26_000_000_000, bytes_accessed=8 * blocks[0].size, transcendentals=0
         ),
     )(*blocks)
 
@@ -271,7 +271,7 @@
         in_specs=[pl.BlockSpec(memory_space=pltpu.SMEM), VMEM, VMEM],
         out_specs=VMEM,
         scratch_shapes=[pltpu.VMEM((16, columns), jnp.float32)],
-        compiler_params=pltpu.CompilerParams(vmem_limit_bytes=53 * MIB),
+        compiler_params=pltpu.CompilerParams(vmem_limit_bytes=8 * MIB),
     )(z, parts, symmetry)
 
 
@@ -299,14 +299,16 @@
     got = lax.all_to_all(sent, ("xh", "xl"), 0, 0, tiled=True)
     half = lax.axis_size("z") // 2
     ahead = gather(got, "z", half - 1, 1)
-    behind = gather(got, "z", half - 1, -1)
+    behind = gather(got, "z", 2, -1)
+    nearby = split(ahead[1], behind[1])
+    last, *nearby = lax.optimization_barrier((behind[1], *nearby))
+    behind += gather(last, "z", half - 3, -1)
 
     packed = pack_amplitudes(amplitudes, 4 * ys)
     halves = split(got)
     packed, *halves = lax.optimization_barrier((packed, *halves))
-    nearby = split(ahead[1], behind[1])
     packed = lax.all_to_all(packed, ("y", "core", "xl"), 0, 0, tiled=True)
-    packed, symmetry, *nearby = lax.optimization_barrier((packed, symmetry, *nearby))
+    packed, symmetry = lax.optimization_barrier((packed, symmetry))
     halves += nearby
     high, low = spin_rows(packed)
     ahead += gather(ahead[-1], "z", 1, 1)

time: 142 us -> 136 us (0.958)
  waiting for transfers between devices: 37.8 us -> 32.5 us
  Pallas kernels: 19.1 us -> 15.7 us
  starting transfers between devices: 77.2 us -> 80.1 us
    ppermute x11, waiting for transfers between devices: 17.5 us -> 12.2 us  [gather(): blocks.append(lax.ppermute(blocks[-1], axis, pairs))]
    ppermute x11, starting transfers between devices: 47 us -> 50.3 us  [gather(): blocks.append(lax.ppermute(blocks[-1], axis, pairs))]
    pallas_call x1, Pallas kernels: 4.38 us -> 1.89 us  [spin_rows(): pl.pallas_call(spin_kernel, out_shape=(shape, shape), in_specs=[VMEM], ou...]
    unnamed x20 -> x24, local copies, waits for them, and re-layouts: 5.25 us -> 4.91 us
  transfers between devices with their start and end apart: 16 -> 16, of which waited for: 7 -> 9; matrix products, arithmetic and copies ran while one was open for 0% -> 0% of each run, Pallas kernels for 12% -> 10%
where the time goes in v8:
time: 136 us; the launch traced here: 135 us
  starting transfers between devices  80.1 us (59%)
  waiting for transfers between devices  32.5 us (24%)
  Pallas kernels  15.7 us (12%)
  local copies, waits for them, and re-layouts  5.06 us (4%)
    ppermute x11, starting transfers between devices, gather(): blocks.append(lax.ppermute(blocks[-1], axis, pairs))  50.3 us
    all_to_all x1, waiting for transfers between devices, body(): partial = lax.all_to_all(partial, ('y', 'xl'), 0, 0, tiled=True)  17.4 us
    ppermute x11, waiting for transfers between devices, gather(): blocks.append(lax.ppermute(blocks[-1], axis, pairs))  12.2 us
    all_to_all x1, starting transfers between devices, body(): packed = lax.all_to_all(packed, ('y', 'core', 'xl'), 0, 0, tiled=True)  9.71 us
    pallas_call x2, Pallas kernels, product(): pl.pallas_call(functools.partial(product_kernel, len(columns)), out_shape...  8.12 us
    all_to_all x1, starting transfers between devices, body(): partial = lax.all_to_all(partial, ('y', 'xl'), 0, 0, tiled=True)  7.16 us
    ppermute x1, starting transfers between devices, body(): taken = lax.ppermute(given, 'core', swap)  6.13 us
    unnamed x24, local copies, waits for them, and re-layouts  4.91 us
  transfers between devices with their start and end apart: 16, of which 9 were waited for; matrix products, arithmetic and copies ran while one was open for 0% of the time, Pallas kernels for 10%

profile of v8, /device:TPU:1, one launch (start us, length us, event | category | flops | bytes accessed | tf_op | source)
XLA Modules:
  0.0 135.1 jit_solution(9506250636414923617)
XLA Ops:
  0.0 1.8 %shard_map.56 = f32[4,16,1280]{2,1,0:T(8,128)} custom-call(f32[40,16,64]{2,1,0:T(8,128)} %bitcast.4), custom_call_target="tpu_custom_call" | custom-call | tf_op jit(solution)/shard_map/pallas_call | solution.py:27
  1.8 4.8 %all-to-all-start = ((f32[4,16,1280]{2,1,0:T(8,128)}), f32[4,16,1280]{2,1,0:T(8,128)S(1)}, u32[]{:S(2)}, u32[]{:S(2)}) async-start(f32[4,16,1280]{2,1,0:T(8,128)} %shard_map.56), calls=%async_computation | async-start | bytes 655360 | tf_op jit(solution)/shard_map/all_to_all | solution.py:299
  6.6 1.5 %copy-done = f32[3,64,4,640]{3,2,1,0:T(4,128)S(1)} copy-done((f32[3,64,4,640]{3,2,1,0:T(4,128)S(1)}, f32[3,64,4,640]{3,2,1,0:T(4,128)}, u32[]{:S(2)}) %copy-start) | copy-done | bytes 1966104
  8.2 2.8 %shard_map.55 = f32[32,3,40,128]{3,2,1,0:T(8,128)} custom-call(f32[3,64,4,640]{3,2,1,0:T(4,128)S(1)} %copy-done), custom_call_target="tpu_custom_call" | custom-call | bytes 3932160 | tf_op jit(solution)/shard_map/pallas_call | solution.py:60
  11.0 1.5 %all-to-all-done.refs_0_ = f32[4,16,1280]{2,1,0:T(8,128)S(1)} async-done(((f32[4,16,1280]{2,1,0:T(8,128)}), f32[4,16,1280]{2,1,0:T(8,128)S(1)}, u32[]{:S(2)}, u32[]{:S(2)}) %all-to-all-start) | async-done | bytes 327712 | tf_op jit(solution)/shard_map/all_to_all | solution.py:299
  12.5 14.6 %collective-permute-start = (f32[4,16,1280]{2,1,0:T(8,128)S(1)}, f32[4,16,1280]{2,1,0:T(8,128)S(1)}, u32[]{:S(2)}, u32[]{:S(2)}) collective-permute-start(f32[4,16,1280]{2,1,0:T(8,128)S(1)} %all-to-all-done.refs_0_), channel_id=1, source_target_pairs={{0,176},{16,0},{32,16},{48,32},{64,48},{80,64},{96,80},{112,96},{1... | collective-permute-start | bytes 983048 | tf_op jit(solution)/shard_map/ppermute | solution.py:283
  27.1 1.9 %collective-permute-start.3 = (f32[4,16,1280]{2,1,0:T(8,128)S(1)}, f32[4,16,1280]{2,1,0:T(8,128)S(1)}, u32[]{:S(2)}, u32[]{:S(2)}) collective-permute-start(f32[4,16,1280]{2,1,0:T(8,128)S(1)} %all-to-all-done.refs_0_), channel_id=1, source_target_pairs={{0,16},{16,32},{32,48},{48,64},{64,80},{80,96},{96,112},{112,128},... | collective-permute-start | bytes 983048 | tf_op jit(solution)/shard_map/ppermute | solution.py:283
  29.0 0.1 shard_map.57
  29.1 9.7 %all-to-all-start.1 = ((f32[32,3,40,128]{3,2,1,0:T(8,128)}), f32[32,3,40,128]{3,2,1,0:T(8,128)S(1)}, u32[]{:S(2)}, u32[]{:S(2)}) async-start(f32[32,3,40,128]{3,2,1,0:T(8,128)} %shard_map.55), calls=%async_computation.1 | async-start | bytes 3932160 | tf_op jit(solution)/shard_map/all_to_all | solution.py:310
  38.8 0.0 copy-start.7
  38.8 0.0 copy-start.8
  38.9 4.9 %collective-permute-start.1 = (f32[4,16,1280]{2,1,0:T(8,128)S(1)}, f32[4,16,1280]{2,1,0:T(8,128)S(1)}, u32[]{:S(2)}, u32[]{:S(2)}) collective-permute-start(f32[4,16,1280]{2,1,0:T(8,128)S(1)} %collective-permute-done.refs_0_), channel_id=1, source_target_pairs={{0,176},{16,0},{32,16},{48,32},{64,48},{80,64},{96,80},{112,96},{1... | collective-permute-start | bytes 983048 | tf_op jit(solution)/shard_map/ppermute | solution.py:283
  43.8 1.9 %collective-permute-start.4 = (f32[4,16,1280]{2,1,0:T(8,128)S(1)}, f32[4,16,1280]{2,1,0:T(8,128)S(1)}, u32[]{:S(2)}, u32[]{:S(2)}) collective-permute-start(f32[4,16,1280]{2,1,0:T(8,128)S(1)} %collective-permute-done.3.refs_2_), channel_id=1, source_target_pairs={{0,16},{16,32},{32,48},{48,64},{64,80},{80,96},{96,112},{112,128},... | collective-permute-start | bytes 983048 | tf_op jit(solution)/shard_map/ppermute | solution.py:283
  45.7 4.9 %collective-permute-done.1.refs_0_ = f32[4,16,1280]{2,1,0:T(8,128)S(1)} collective-permute-done((f32[4,16,1280]{2,1,0:T(8,128)S(1)}, f32[4,16,1280]{2,1,0:T(8,128)S(1)}, u32[]{:S(2)}, u32[]{:S(2)}) %collective-permute-start.1) | collective-permute-done | bytes 327712 | tf_op jit(solution)/shard_map/ppermute | solution.py:283
  50.6 5.3 %collective-permute-start.2 = (f32[4,16,1280]{2,1,0:T(8,128)S(1)}, f32[4,16,1280]{2,1,0:T(8,128)S(1)}, u32[]{:S(2)}, u32[]{:S(2)}) collective-permute-start(f32[4,16,1280]{2,1,0:T(8,128)S(1)} %collective-permute-done.1.refs_0_), channel_id=1, source_target_pairs={{0,176},{16,0},{32,16},{48,32},{64,48},{80,64},{96,80},{112,96},{1... | collective-permute-start | bytes 983048 | tf_op jit(solution)/shard_map/ppermute | solution.py:283
  55.9 0.1 shard_map.59
  56.1 0.7 copy-done.3
  56.8 0.7 copy-done.4
  57.5 1.9 %collective-permute-start.5 = (f32[4,16,1280]{2,1,0:T(8,128)S(1)}, f32[4,16,1280]{2,1,0:T(8,128)}, u32[]{:S(2)}, u32[]{:S(2)}) collective-permute-start(f32[4,16,1280]{2,1,0:T(8,128)S(1)} %collective-permute-done.4.refs_1_), channel_id=1, source_target_pairs={{0,16},{16,32},{32,48},{48,64},{64,80},{80,96},{96,112},{112,128},... | collective-permute-start | bytes 983048 | tf_op jit(solution)/shard_map/ppermute | solution.py:283
  59.4 2.4 %collective-permute-done.2.refs_1_ = f32[4,16,1280]{2,1,0:T(8,128)S(1)} collective-permute-done((f32[4,16,1280]{2,1,0:T(8,128)S(1)}, f32[4,16,1280]{2,1,0:T(8,128)S(1)}, u32[]{:S(2)}, u32[]{:S(2)}) %collective-permute-start.2) | collective-permute-done | bytes 327712 | tf_op jit(solution)/shard_map/ppermute | solution.py:283
  61.8 5.3 %collective-permute-start.7 = (f32[4,16,1280]{2,1,0:T(8,128)S(1)}, f32[4,16,1280]{2,1,0:T(8,128)S(1)}, u32[]{:S(2)}, u32[]{:S(2)}) collective-permute-start(f32[4,16,1280]{2,1,0:T(8,128)S(1)} %collective-permute-done.2.refs_1_), channel_id=1, source_target_pairs={{0,176},{16,0},{32,16},{48,32},{64,48},{80,64},{96,80},{112,96},{1... | collective-permute-start | bytes 983048 | tf_op jit(solution)/shard_map/ppermute | solution.py:283
  67.2 1.4 %collective-permute-done.5.refs_3_ = f32[4,16,1280]{2,1,0:T(8,128)} collective-permute-done((f32[4,16,1280]{2,1,0:T(8,128)S(1)}, f32[4,16,1280]{2,1,0:T(8,128)}, u32[]{:S(2)}, u32[]{:S(2)}) %collective-permute-start.5) | collective-permute-done | bytes 327712 | tf_op jit(solution)/shard_map/ppermute | solution.py:283
  68.6 1.9 %collective-permute-start.6 = (f32[4,16,1280]{2,1,0:T(8,128)}, f32[4,16,1280]{2,1,0:T(8,128)}, u32[]{:S(2)}, u32[]{:S(2)}) collective-permute-start(f32[4,16,1280]{2,1,0:T(8,128)} %collective-permute-done.5.refs_3_), channel_id=1, source_target_pairs={{0,16},{16,32},{32,48},{48,64},{64,80},{80,96},{96,112},{112,128},... | collective-permute-start | bytes 983048 | tf_op jit(solution)/shard_map/ppermute | solution.py:283
  70.5 1.7 %collective-permute-done.7.refs_0_ = f32[4,16,1280]{2,1,0:T(8,128)S(1)} collective-permute-done((f32[4,16,1280]{2,1,0:T(8,128)S(1)}, f32[4,16,1280]{2,1,0:T(8,128)S(1)}, u32[]{:S(2)}, u32[]{:S(2)}) %collective-permute-start.7) | collective-permute-done | bytes 327712 | tf_op jit(solution)/shard_map/ppermute | solution.py:283
  72.2 5.3 %collective-permute-start.8 = (f32[4,16,1280]{2,1,0:T(8,128)S(1)}, f32[4,16,1280]{2,1,0:T(8,128)S(1)}, u32[]{:S(2)}, u32[]{:S(2)}) collective-permute-start(f32[4,16,1280]{2,1,0:T(8,128)S(1)} %collective-permute-done.7.refs_0_), channel_id=1, source_target_pairs={{0,176},{16,0},{32,16},{48,32},{64,48},{80,64},{96,80},{112,96},{1... | collective-permute-start | bytes 983048 | tf_op jit(solution)/shard_map/ppermute | solution.py:283
  77.5 0.1 broadcast_xor_fusion.1
  77.6 0.1 dynamic_slice.3
  77.7 0.1 xor.58
  77.7 0.1 broadcast_xor_fusion.2
  77.8 1.1 collective-permute-done.6.refs_4_
  78.9 1.9 %collective-permute-start.11 = (f32[4,16,1280]{2,1,0:T(8,128)}, f32[4,16,1280]{2,1,0:T(8,128)}, u32[]{:S(2)}, u32[]{:S(2)}) collective-permute-start(f32[4,16,1280]{2,1,0:T(8,128)} %collective-permute-done.6.refs_4_), channel_id=1, source_target_pairs={{0,16},{16,32},{32,48},{48,64},{64,80},{80,96},{96,112},{112,128},... | collective-permute-start | bytes 983048 | tf_op jit(solution)/shard_map/ppermute | solution.py:283
  80.9 0.6 collective-permute-done.8.refs_1_
  81.5 5.4 %collective-permute-start.9 = (f32[4,16,1280]{2,1,0:T(8,128)S(1)}, f32[4,16,1280]{2,1,0:T(8,128)}, u32[]{:S(2)}, u32[]{:S(2)}) collective-permute-start(f32[4,16,1280]{2,1,0:T(8,128)S(1)} %collective-permute-done.8.refs_1_), channel_id=1, source_target_pairs={{0,176},{16,0},{32,16},{48,32},{64,48},{80,64},{96,80},{112,96},{1... | collective-permute-start | bytes 983048 | tf_op jit(solution)/shard_map/ppermute | solution.py:283
  86.9 0.1 broadcast_xor_fusion.symmetry_ref
  87.0 1.9 %shard_map.58 = (bf16[2,192,1280]{2,1,0:T(8,128)(2,1)S(1)}, bf16[2,192,1280]{2,1,0:T(8,128)(2,1)S(1)}) custom-call(f32[32,3,40,128]{3,2,1,0:T(8,128)S(1)} %all-to-all-done.1.in_ref), custom_call_target="tpu_custom_call" | custom-call | bytes 3932160 | tf_op jit(solution)/shard_map/pallas_call | solution.py:112
  88.9 1.0 copy-done.1
  89.8 0.9 copy-done.2
  90.8 5.2 %shard_map.60 = (f32[8,2,3,4,512]{4,3,2,1,0:T(4,128)}, f32[8,2,3,4,512]{4,3,2,1,0:T(4,128)}) custom-call(s32[1]{0:T(128)} %bitcast.1.core_ref, bf16[2,192,1280]{2,1,0:T(8,128)(2,1)} %copy-done.1, bf16[2,192,1280]{2,1,0:T(8,128)(2,1)} %copy-done.2, f32[4,16,1280]{2,1,0:T(8,128)S(1)} %collective-permute-done.refs_0_, f32[4,16,1280]{2,1,0:T(8,128)} %copy-done.11, ...), custom_call_target="tpu_custom_call" | custom-call | flops 1509949440 | bytes 8388608 | tf_op jit(solution)/shard_map/pallas_call | solution.py:189
  96.0 6.1 %collective-permute-start.10 = (f32[8,2,3,4,512]{4,3,2,1,0:T(4,128)}, f32[8,2,3,4,512]{4,3,2,1,0:T(4,128)S(1)}, u32[]{:S(2)}, u32[]{:S(2)}) collective-permute-start(f32[8,2,3,4,512]{4,3,2,1,0:T(4,128)} %get-tuple-element.40), channel_id=1, source_target_pairs={{0,1},{1,0},{2,3},{3,2},{4,5},{5,4},{6,7},{7,6},{8,9},{9,8},{10,11... | collective-permute-start | bytes 1179656 | tf_op jit(solution)/shard_map/ppermute | solution.py:322
  102.1 2.9 %shard_map.61 = (f32[8,2,3,4,256]{4,3,2,1,0:T(4,128)S(1)}, f32[8,2,3,4,256]{4,3,2,1,0:T(4,128)S(1)}) custom-call(s32[1]{0:T(128)} %bitcast.1.core_ref, bf16[2,192,1280]{2,1,0:T(8,128)(2,1)} %copy-done.1, bf16[2,192,1280]{2,1,0:T(8,128)(2,1)} %copy-done.2, f32[4,16,1280]{2,1,0:T(8,128)S(1)} %collective-permute-done.7.refs_0_, f32[4,16,1280]{2,1,0:T(8,128)} %copy-done.6, ...), custom_call_target="tpu_custom_call" | custom-call | flops 754974720 | bytes 8388608 | tf_op jit(solution)/shard_map/pallas_call | solution.py:189
  105.1 1.9 %collective-permute-start.12 = (f32[8,2,3,4,256]{4,3,2,1,0:T(4,128)S(1)}, f32[8,2,3,4,256]{4,3,2,1,0:T(4,128)S(1)}, u32[]{:S(2)}, u32[]{:S(2)}) collective-permute-start(f32[8,2,3,4,256]{4,3,2,1,0:T(4,128)S(1)} %get-tuple-element.43), channel_id=1, source_target_pairs={{0,1},{1,0},{2,3},{3,2},{4,5},{5,4},{6,7},{7,6},{8,9},{9,8},{10,11... | collective-permute-start | bytes 589832 | tf_op jit(solution)/shard_map/ppermute | solution.py:324
  107.0 1.4 %collective-permute-done.12 = f32[8,2,3,4,256]{4,3,2,1,0:T(4,128)S(1)} collective-permute-done((f32[8,2,3,4,256]{4,3,2,1,0:T(4,128)S(1)}, f32[8,2,3,4,256]{4,3,2,1,0:T(4,128)S(1)}, u32[]{:S(2)}, u32[]{:S(2)}) %collective-permute-start.12) | collective-permute-done | bytes 196640 | tf_op jit(solution)/shard_map/ppermute | solution.py:324
  108.4 0.1 add.15
  108.5 0.1 add.14
  108.6 1.0 pad_maximum_fusion
  109.6 7.2 %all-to-all-start.2 = ((f32[16,3,4,768]{3,2,1,0:T(4,128)}), f32[16,3,4,768]{3,2,1,0:T(4,128)S(1)}, u32[]{:S(2)}, u32[]{:S(2)}) async-start(f32[16,3,4,768]{3,2,1,0:T(4,128)} %bitcast.3), calls=%async_computation.2 | async-start | bytes 1179648 | tf_op jit(solution)/shard_map/all_to_all | solution.py:327
  116.7 17.4 %all-to-all-done.2.parts_ref = f32[16,3,4,768]{3,2,1,0:T(4,128)S(1)} async-done(((f32[16,3,4,768]{3,2,1,0:T(4,128)}), f32[16,3,4,768]{3,2,1,0:T(4,128)S(1)}, u32[]{:S(2)}, u32[]{:S(2)}) %all-to-all-start.2) | async-done | bytes 589856 | tf_op jit(solution)/shard_map/all_to_all | solution.py:327
  134.2 0.9 shard_map.62
  (24 shorter events, 0.1 us)
Async XLA Ops:
  1.8 10.7 %all-to-all-start = ((f32[4,16,1280]{2,1,0:T(8,128)}), f32[4,16,1280]{2,1,0:T(8,128)S(1)}, u32[]{:S(2)}, u32[]{:S(2)}) async-start(f32[4,16,1280]{2,1,0:T(8,128)} %shard_map.56), calls=%async_computation | async-start | bytes 655360 | tf_op jit(solution)/shard_map/all_to_all | solution.py:299
  6.6 1.5 %copy-start = (f32[3,64,4,640]{3,2,1,0:T(4,128)S(1)}, f32[3,64,4,640]{3,2,1,0:T(4,128)}, u32[]{:S(2)}) copy-start(f32[3,64,4,640]{3,2,1,0:T(4,128)} %in_ref.1) | copy-start | bytes 5898244
  12.5 26.3 %collective-permute-start = (f32[4,16,1280]{2,1,0:T(8,128)S(1)}, f32[4,16,1280]{2,1,0:T(8,128)S(1)}, u32[]{:S(2)}, u32[]{:S(2)}) collective-permute-start(f32[4,16,1280]{2,1,0:T(8,128)S(1)} %all-to-all-done.refs_0_), channel_id=1, source_target_pairs={{0,176},{16,0},{32,16},{48,32},{64,48},{80,64},{96,80},{112,96},{1... | collective-permute-start | bytes 983048 | tf_op jit(solution)/shard_map/ppermute | solution.py:283
  27.1 16.6 %collective-permute-start.3 = (f32[4,16,1280]{2,1,0:T(8,128)S(1)}, f32[4,16,1280]{2,1,0:T(8,128)S(1)}, u32[]{:S(2)}, u32[]{:S(2)}) collective-permute-start(f32[4,16,1280]{2,1,0:T(8,128)S(1)} %all-to-all-done.refs_0_), channel_id=1, source_target_pairs={{0,16},{16,32},{32,48},{48,64},{64,80},{80,96},{96,112},{112,128},... | collective-permute-start | bytes 983048 | tf_op jit(solution)/shard_map/ppermute | solution.py:283
  29.1 57.9 %all-to-all-start.1 = ((f32[32,3,40,128]{3,2,1,0:T(8,128)}), f32[32,3,40,128]{3,2,1,0:T(8,128)S(1)}, u32[]{:S(2)}, u32[]{:S(2)}) async-start(f32[32,3,40,128]{3,2,1,0:T(8,128)} %shard_map.55), calls=%async_computation.1 | async-start | bytes 3932160 | tf_op jit(solution)/shard_map/all_to_all | solution.py:310
  38.8 38.7 %copy-start.7 = (s32[12]{0:T(128)S(1)}, s32[12]{0:T(128)}, u32[]{:S(2)}) copy-start(s32[12]{0:T(128)} %param.8) | copy-start | bytes 148
  38.8 38.7 %copy-start.8 = (s32[64]{0:T(128)S(1)}, s32[64]{0:T(128)}, u32[]{:S(2)}) copy-start(s32[64]{0:T(128)} %param.9) | copy-start | bytes 772
  38.8 38.9 %copy-start.9 = (s32[3]{0:T(128)S(1)}, s32[3]{0:T(128)}, u32[]{:S(2)}) copy-start(s32[3]{0:T(128)} %param.7) | copy-start | bytes 40
  38.9 11.7 %collective-permute-start.1 = (f32[4,16,1280]{2,1,0:T(8,128)S(1)}, f32[4,16,1280]{2,1,0:T(8,128)S(1)}, u32[]{:S(2)}, u32[]{:S(2)}) collective-permute-start(f32[4,16,1280]{2,1,0:T(8,128)S(1)} %collective-permute-done.refs_0_), channel_id=1, source_target_pairs={{0,176},{16,0},{32,16},{48,32},{64,48},{80,64},{96,80},{112,96},{1... | collective-permute-start | bytes 983048 | tf_op jit(solution)/shard_map/ppermute | solution.py:283
  43.7 12.3 %copy-start.10 = (f32[4,16,1280]{2,1,0:T(8,128)}, f32[4,16,1280]{2,1,0:T(8,128)S(1)}, u32[]{:S(2)}) copy-start(f32[4,16,1280]{2,1,0:T(8,128)S(1)} %collective-permute-done.3.refs_2_) | copy-start | bytes 983044
  43.8 12.2 %collective-permute-start.4 = (f32[4,16,1280]{2,1,0:T(8,128)S(1)}, f32[4,16,1280]{2,1,0:T(8,128)S(1)}, u32[]{:S(2)}, u32[]{:S(2)}) collective-permute-start(f32[4,16,1280]{2,1,0:T(8,128)S(1)} %collective-permute-done.3.refs_2_), channel_id=1, source_target_pairs={{0,16},{16,32},{32,48},{48,64},{64,80},{80,96},{96,112},{112,128},... | collective-permute-start | bytes 983048 | tf_op jit(solution)/shard_map/ppermute | solution.py:283
  50.6 11.2 %collective-permute-start.2 = (f32[4,16,1280]{2,1,0:T(8,128)S(1)}, f32[4,16,1280]{2,1,0:T(8,128)S(1)}, u32[]{:S(2)}, u32[]{:S(2)}) collective-permute-start(f32[4,16,1280]{2,1,0:T(8,128)S(1)} %collective-permute-done.1.refs_0_), channel_id=1, source_target_pairs={{0,176},{16,0},{32,16},{48,32},{64,48},{80,64},{96,80},{112,96},{1... | collective-permute-start | bytes 983048 | tf_op jit(solution)/shard_map/ppermute | solution.py:283
  56.0 0.7 copy-start.3
  56.8 0.7 copy-start.4
  57.5 11.1 %collective-permute-start.5 = (f32[4,16,1280]{2,1,0:T(8,128)S(1)}, f32[4,16,1280]{2,1,0:T(8,128)}, u32[]{:S(2)}, u32[]{:S(2)}) collective-permute-start(f32[4,16,1280]{2,1,0:T(8,128)S(1)} %collective-permute-done.4.refs_1_), channel_id=1, source_target_pairs={{0,16},{16,32},{32,48},{48,64},{64,80},{80,96},{96,112},{112,128},... | collective-permute-start | bytes 983048 | tf_op jit(solution)/shard_map/ppermute | solution.py:283
  61.8 10.3 %copy-start.11 = (f32[4,16,1280]{2,1,0:T(8,128)}, f32[4,16,1280]{2,1,0:T(8,128)S(1)}, u32[]{:S(2)}) copy-start(f32[4,16,1280]{2,1,0:T(8,128)S(1)} %collective-permute-done.2.refs_1_) | copy-start | bytes 983044
  61.8 10.3 %collective-permute-start.7 = (f32[4,16,1280]{2,1,0:T(8,128)S(1)}, f32[4,16,1280]{2,1,0:T(8,128)S(1)}, u32[]{:S(2)}, u32[]{:S(2)}) collective-permute-start(f32[4,16,1280]{2,1,0:T(8,128)S(1)} %collective-permute-done.2.refs_1_), channel_id=1, source_target_pairs={{0,176},{16,0},{32,16},{48,32},{64,48},{80,64},{96,80},{112,96},{1... | collective-permute-start | bytes 983048 | tf_op jit(solution)/shard_map/ppermute | solution.py:283
  68.6 10.4 %collective-permute-start.6 = (f32[4,16,1280]{2,1,0:T(8,128)}, f32[4,16,1280]{2,1,0:T(8,128)}, u32[]{:S(2)}, u32[]{:S(2)}) collective-permute-start(f32[4,16,1280]{2,1,0:T(8,128)} %collective-permute-done.5.refs_3_), channel_id=1, source_target_pairs={{0,16},{16,32},{32,48},{48,64},{64,80},{80,96},{96,112},{112,128},... | collective-permute-start | bytes 983048 | tf_op jit(solution)/shard_map/ppermute | solution.py:283
  72.2 9.3 %collective-permute-start.8 = (f32[4,16,1280]{2,1,0:T(8,128)S(1)}, f32[4,16,1280]{2,1,0:T(8,128)S(1)}, u32[]{:S(2)}, u32[]{:S(2)}) collective-permute-start(f32[4,16,1280]{2,1,0:T(8,128)S(1)} %collective-permute-done.7.refs_0_), channel_id=1, source_target_pairs={{0,176},{16,0},{32,16},{48,32},{64,48},{80,64},{96,80},{112,96},{1... | collective-permute-start | bytes 983048 | tf_op jit(solution)/shard_map/ppermute | solution.py:283
  78.9 23.2 %collective-permute-start.11 = (f32[4,16,1280]{2,1,0:T(8,128)}, f32[4,16,1280]{2,1,0:T(8,128)}, u32[]{:S(2)}, u32[]{:S(2)}) collective-permute-start(f32[4,16,1280]{2,1,0:T(8,128)} %collective-permute-done.6.refs_4_), channel_id=1, source_target_pairs={{0,16},{16,32},{32,48},{48,64},{64,80},{80,96},{96,112},{112,128},... | collective-permute-start | bytes 983048 | tf_op jit(solution)/shard_map/ppermute | solution.py:283
  81.5 14.5 %copy-start.6 = (f32[4,16,1280]{2,1,0:T(8,128)}, f32[4,16,1280]{2,1,0:T(8,128)S(1)}, u32[]{:S(2)}) copy-start(f32[4,16,1280]{2,1,0:T(8,128)S(1)} %collective-permute-done.8.refs_1_) | copy-start | bytes 983044
  81.5 14.5 %collective-permute-start.9 = (f32[4,16,1280]{2,1,0:T(8,128)S(1)}, f32[4,16,1280]{2,1,0:T(8,128)}, u32[]{:S(2)}, u32[]{:S(2)}) collective-permute-start(f32[4,16,1280]{2,1,0:T(8,128)S(1)} %collective-permute-done.8.refs_1_), channel_id=1, source_target_pairs={{0,176},{16,0},{32,16},{48,32},{64,48},{80,64},{96,80},{112,96},{1... | collective-permute-start | bytes 983048 | tf_op jit(solution)/shard_map/ppermute | solution.py:283
  88.9 1.0 copy-start.1
  89.8 0.9 copy-start.2
  96.0 12.5 %copy-start.5 = (f32[8,2,3,4,512]{4,3,2,1,0:T(4,128)S(1)}, f32[8,2,3,4,512]{4,3,2,1,0:T(4,128)}, u32[]{:S(2)}) copy-start(f32[8,2,3,4,512]{4,3,2,1,0:T(4,128)} %get-tuple-element.38) | copy-start | bytes 1179652
  96.0 12.5 %collective-permute-start.10 = (f32[8,2,3,4,512]{4,3,2,1,0:T(4,128)}, f32[8,2,3,4,512]{4,3,2,1,0:T(4,128)S(1)}, u32[]{:S(2)}, u32[]{:S(2)}) collective-permute-start(f32[8,2,3,4,512]{4,3,2,1,0:T(4,128)} %get-tuple-element.40), channel_id=1, source_target_pairs={{0,1},{1,0},{2,3},{3,2},{4,5},{5,4},{6,7},{7,6},{8,9},{9,8},{10,11... | collective-permute-start | bytes 1179656 | tf_op jit(solution)/shard_map/ppermute | solution.py:322
  105.1 3.3 %collective-permute-start.12 = (f32[8,2,3,4,256]{4,3,2,1,0:T(4,128)S(1)}, f32[8,2,3,4,256]{4,3,2,1,0:T(4,128)S(1)}, u32[]{:S(2)}, u32[]{:S(2)}) collective-permute-start(f32[8,2,3,4,256]{4,3,2,1,0:T(4,128)S(1)} %get-tuple-element.43), channel_id=1, source_target_pairs={{0,1},{1,0},{2,3},{3,2},{4,5},{5,4},{6,7},{7,6},{8,9},{9,8},{10,11... | collective-permute-start | bytes 589832 | tf_op jit(solution)/shard_map/ppermute | solution.py:324
  109.6 24.6 %all-to-all-start.2 = ((f32[16,3,4,768]{3,2,1,0:T(4,128)}), f32[16,3,4,768]{3,2,1,0:T(4,128)S(1)}, u32[]{:S(2)}, u32[]{:S(2)}) async-start(f32[16,3,4,768]{3,2,1,0:T(4,128)} %bitcast.3), calls=%async_computation.2 | async-start | bytes 1179648 | tf_op jit(solution)/shard_map/all_to_all | solution.py:327

commit v9 on v8

--- a/solution.py
+++ b/solution.py
@@ -319,9 +319,10 @@
     late = ahead[3:] + behind[4:]
     own, given = product(core, high, low, early, halves, ys, window, local)
     given, late[2] = lax.optimization_barrier((given, late[2]))
-    taken = lax.ppermute(given, "core", swap)
-    own_late, given = product(core, high, low, late, [], ys, window, local)
-    partial = jnp.concatenate([own + taken, own_late + lax.ppermute(given, "core", swap)], axis=-1)
+    own_late, given_late = product(core, high, low, late, [], ys, window, local)
+    given, given_late = lax.optimization_barrier((given, given_late))
+    taken, taken_late = (lax.ppermute(part, "core", swap) for part in (given, given_late))
+    partial = jnp.concatenate([own + taken, own_late + taken_late], axis=-1)
 
     partial = partial.reshape(2 * ys, window, local, -1)
     partial = lax.all_to_all(partial, ("y", "xl"), 0, 0, tiled=True)

time: 136 us -> 136 us (level)
    unnamed x24 -> x26, local copies, waits for them, and re-layouts: 4.91 us -> 4.95 us
  transfers between devices with their start and end apart: 16 -> 16, of which waited for: 9 -> 9; matrix products, arithmetic and copies ran while one was open for 0% -> 0% of each run, Pallas kernels for 10% -> 7%
where the time goes in v9:
time: 136 us; the launch traced here: 135 us
  starting transfers between devices  79.9 us (59%)
  waiting for transfers between devices  32.5 us (24%)
  Pallas kernels  15.8 us (12%)
  local copies, waits for them, and re-layouts  5.09 us (4%)
    ppermute x11, starting transfers between devices, gather(): blocks.append(lax.ppermute(blocks[-1], axis, pairs))  50.3 us
    all_to_all x1, waiting for transfers between devices, body(): partial = lax.all_to_all(partial, ('y', 'xl'), 0, 0, tiled=True)  17.4 us
    ppermute x11, waiting for transfers between devices, gather(): blocks.append(lax.ppermute(blocks[-1], axis, pairs))  12.2 us
    all_to_all x1, starting transfers between devices, body(): packed = lax.all_to_all(packed, ('y', 'core', 'xl'), 0, 0, tiled=True)  9.71 us
    pallas_call x2, Pallas kernels, product(): pl.pallas_call(functools.partial(product_kernel, len(columns)), out_shape...  8.2 us
    ppermute x2, starting transfers between devices, body(): lax.ppermute(part, 'core', swap)  7.92 us
    all_to_all x1, starting transfers between devices, body(): partial = lax.all_to_all(partial, ('y', 'xl'), 0, 0, tiled=True)  7.15 us
    unnamed x26, local copies, waits for them, and re-layouts  4.95 us
  transfers between devices with their start and end apart: 16, of which 9 were waited for; matrix products, arithmetic and copies ran while one was open for 0% of the time, Pallas kernels for 7%

profile of v9, /device:TPU:1, one launch (start us, length us, event | category | flops | bytes accessed | tf_op | source)
XLA Modules:
  0.0 135.1 jit_solution(14436395661001734562)
XLA Ops:
  0.0 1.8 %shard_map.56 = f32[4,16,1280]{2,1,0:T(8,128)} custom-call(f32[40,16,64]{2,1,0:T(8,128)} %bitcast.4), custom_call_target="tpu_custom_call" | custom-call | tf_op jit(solution)/shard_map/pallas_call | solution.py:27
  1.8 4.8 %all-to-all-start = ((f32[4,16,1280]{2,1,0:T(8,128)}), f32[4,16,1280]{2,1,0:T(8,128)S(1)}, u32[]{:S(2)}, u32[]{:S(2)}) async-start(f32[4,16,1280]{2,1,0:T(8,128)} %shard_map.56), calls=%async_computation | async-start | bytes 655360 | tf_op jit(solution)/shard_map/all_to_all | solution.py:299
  6.7 1.5 %copy-done = f32[3,64,4,640]{3,2,1,0:T(4,128)S(1)} copy-done((f32[3,64,4,640]{3,2,1,0:T(4,128)S(1)}, f32[3,64,4,640]{3,2,1,0:T(4,128)}, u32[]{:S(2)}) %copy-start) | copy-done | bytes 1966104
  8.2 2.8 %shard_map.55 = f32[32,3,40,128]{3,2,1,0:T(8,128)} custom-call(f32[3,64,4,640]{3,2,1,0:T(4,128)S(1)} %copy-done), custom_call_target="tpu_custom_call" | custom-call | bytes 3932160 | tf_op jit(solution)/shard_map/pallas_call | solution.py:60
  11.0 1.5 %all-to-all-done.refs_0_ = f32[4,16,1280]{2,1,0:T(8,128)S(1)} async-done(((f32[4,16,1280]{2,1,0:T(8,128)}), f32[4,16,1280]{2,1,0:T(8,128)S(1)}, u32[]{:S(2)}, u32[]{:S(2)}) %all-to-all-start) | async-done | bytes 327712 | tf_op jit(solution)/shard_map/all_to_all | solution.py:299
  12.5 14.6 %collective-permute-start = (f32[4,16,1280]{2,1,0:T(8,128)S(1)}, f32[4,16,1280]{2,1,0:T(8,128)S(1)}, u32[]{:S(2)}, u32[]{:S(2)}) collective-permute-start(f32[4,16,1280]{2,1,0:T(8,128)S(1)} %all-to-all-done.refs_0_), channel_id=1, source_target_pairs={{0,176},{16,0},{32,16},{48,32},{64,48},{80,64},{96,80},{112,96},{1... | collective-permute-start | bytes 983048 | tf_op jit(solution)/shard_map/ppermute | solution.py:283
  27.1 1.9 %collective-permute-start.3 = (f32[4,16,1280]{2,1,0:T(8,128)S(1)}, f32[4,16,1280]{2,1,0:T(8,128)S(1)}, u32[]{:S(2)}, u32[]{:S(2)}) collective-permute-start(f32[4,16,1280]{2,1,0:T(8,128)S(1)} %all-to-all-done.refs_0_), channel_id=1, source_target_pairs={{0,16},{16,32},{32,48},{48,64},{64,80},{80,96},{96,112},{112,128},... | collective-permute-start | bytes 983048 | tf_op jit(solution)/shard_map/ppermute | solution.py:283
  29.1 0.1 shard_map.57
  29.1 9.7 %all-to-all-start.1 = ((f32[32,3,40,128]{3,2,1,0:T(8,128)}), f32[32,3,40,128]{3,2,1,0:T(8,128)S(1)}, u32[]{:S(2)}, u32[]{:S(2)}) async-start(f32[32,3,40,128]{3,2,1,0:T(8,128)} %shard_map.55), calls=%async_computation.1 | async-start | bytes 3932160 | tf_op jit(solution)/shard_map/all_to_all | solution.py:310
  38.8 0.0 copy-start.7
  38.8 0.0 copy-start.8
  38.9 4.9 %collective-permute-start.1 = (f32[4,16,1280]{2,1,0:T(8,128)S(1)}, f32[4,16,1280]{2,1,0:T(8,128)S(1)}, u32[]{:S(2)}, u32[]{:S(2)}) collective-permute-start(f32[4,16,1280]{2,1,0:T(8,128)S(1)} %collective-permute-done.refs_0_), channel_id=1, source_target_pairs={{0,176},{16,0},{32,16},{48,32},{64,48},{80,64},{96,80},{112,96},{1... | collective-permute-start | bytes 983048 | tf_op jit(solution)/shard_map/ppermute | solution.py:283
  43.8 1.9 %collective-permute-start.4 = (f32[4,16,1280]{2,1,0:T(8,128)S(1)}, f32[4,16,1280]{2,1,0:T(8,128)S(1)}, u32[]{:S(2)}, u32[]{:S(2)}) collective-permute-start(f32[4,16,1280]{2,1,0:T(8,128)S(1)} %collective-permute-done.3.refs_2_), channel_id=1, source_target_pairs={{0,16},{16,32},{32,48},{48,64},{64,80},{80,96},{96,112},{112,128},... | collective-permute-start | bytes 983048 | tf_op jit(solution)/shard_map/ppermute | solution.py:283
  45.7 4.9 %collective-permute-done.1.refs_0_ = f32[4,16,1280]{2,1,0:T(8,128)S(1)} collective-permute-done((f32[4,16,1280]{2,1,0:T(8,128)S(1)}, f32[4,16,1280]{2,1,0:T(8,128)S(1)}, u32[]{:S(2)}, u32[]{:S(2)}) %collective-permute-start.1) | collective-permute-done | bytes 327712 | tf_op jit(solution)/shard_map/ppermute | solution.py:283
  50.6 5.3 %collective-permute-start.2 = (f32[4,16,1280]{2,1,0:T(8,128)S(1)}, f32[4,16,1280]{2,1,0:T(8,128)S(1)}, u32[]{:S(2)}, u32[]{:S(2)}) collective-permute-start(f32[4,16,1280]{2,1,0:T(8,128)S(1)} %collective-permute-done.1.refs_0_), channel_id=1, source_target_pairs={{0,176},{16,0},{32,16},{48,32},{64,48},{80,64},{96,80},{112,96},{1... | collective-permute-start | bytes 983048 | tf_op jit(solution)/shard_map/ppermute | solution.py:283
  55.9 0.1 shard_map.59
  56.1 0.7 copy-done.3
  56.8 0.7 copy-done.4
  57.5 1.9 %collective-permute-start.5 = (f32[4,16,1280]{2,1,0:T(8,128)S(1)}, f32[4,16,1280]{2,1,0:T(8,128)}, u32[]{:S(2)}, u32[]{:S(2)}) collective-permute-start(f32[4,16,1280]{2,1,0:T(8,128)S(1)} %collective-permute-done.4.refs_1_), channel_id=1, source_target_pairs={{0,16},{16,32},{32,48},{48,64},{64,80},{80,96},{96,112},{112,128},... | collective-permute-start | bytes 983048 | tf_op jit(solution)/shard_map/ppermute | solution.py:283
  59.5 2.4 %collective-permute-done.2.refs_1_ = f32[4,16,1280]{2,1,0:T(8,128)S(1)} collective-permute-done((f32[4,16,1280]{2,1,0:T(8,128)S(1)}, f32[4,16,1280]{2,1,0:T(8,128)S(1)}, u32[]{:S(2)}, u32[]{:S(2)}) %collective-permute-start.2) | collective-permute-done | bytes 327712 | tf_op jit(solution)/shard_map/ppermute | solution.py:283
  61.8 5.3 %collective-permute-start.7 = (f32[4,16,1280]{2,1,0:T(8,128)S(1)}, f32[4,16,1280]{2,1,0:T(8,128)S(1)}, u32[]{:S(2)}, u32[]{:S(2)}) collective-permute-start(f32[4,16,1280]{2,1,0:T(8,128)S(1)} %collective-permute-done.2.refs_1_), channel_id=1, source_target_pairs={{0,176},{16,0},{32,16},{48,32},{64,48},{80,64},{96,80},{112,96},{1... | collective-permute-start | bytes 983048 | tf_op jit(solution)/shard_map/ppermute | solution.py:283
  67.2 1.4 %collective-permute-done.5.refs_3_ = f32[4,16,1280]{2,1,0:T(8,128)} collective-permute-done((f32[4,16,1280]{2,1,0:T(8,128)S(1)}, f32[4,16,1280]{2,1,0:T(8,128)}, u32[]{:S(2)}, u32[]{:S(2)}) %collective-permute-start.5) | collective-permute-done | bytes 327712 | tf_op jit(solution)/shard_map/ppermute | solution.py:283
  68.6 1.9 %collective-permute-start.6 = (f32[4,16,1280]{2,1,0:T(8,128)}, f32[4,16,1280]{2,1,0:T(8,128)}, u32[]{:S(2)}, u32[]{:S(2)}) collective-permute-start(f32[4,16,1280]{2,1,0:T(8,128)} %collective-permute-done.5.refs_3_), channel_id=1, source_target_pairs={{0,16},{16,32},{32,48},{48,64},{64,80},{80,96},{96,112},{112,128},... | collective-permute-start | bytes 983048 | tf_op jit(solution)/shard_map/ppermute | solution.py:283
  70.5 1.6 %collective-permute-done.7.refs_0_ = f32[4,16,1280]{2,1,0:T(8,128)S(1)} collective-permute-done((f32[4,16,1280]{2,1,0:T(8,128)S(1)}, f32[4,16,1280]{2,1,0:T(8,128)S(1)}, u32[]{:S(2)}, u32[]{:S(2)}) %collective-permute-start.7) | collective-permute-done | bytes 327712 | tf_op jit(solution)/shard_map/ppermute | solution.py:283
  72.2 5.3 %collective-permute-start.8 = (f32[4,16,1280]{2,1,0:T(8,128)S(1)}, f32[4,16,1280]{2,1,0:T(8,128)S(1)}, u32[]{:S(2)}, u32[]{:S(2)}) collective-permute-start(f32[4,16,1280]{2,1,0:T(8,128)S(1)} %collective-permute-done.7.refs_0_), channel_id=1, source_target_pairs={{0,176},{16,0},{32,16},{48,32},{64,48},{80,64},{96,80},{112,96},{1... | collective-permute-start | bytes 983048 | tf_op jit(solution)/shard_map/ppermute | solution.py:283
  77.5 0.1 broadcast_xor_fusion.1
  77.6 0.1 dynamic_slice.3
  77.7 0.1 xor.58
  77.7 0.1 broadcast_xor_fusion.2
  77.8 1.2 collective-permute-done.6.refs_4_
  79.0 1.9 %collective-permute-start.10 = (f32[4,16,1280]{2,1,0:T(8,128)}, f32[4,16,1280]{2,1,0:T(8,128)}, u32[]{:S(2)}, u32[]{:S(2)}) collective-permute-start(f32[4,16,1280]{2,1,0:T(8,128)} %collective-permute-done.6.refs_4_), channel_id=1, source_target_pairs={{0,16},{16,32},{32,48},{48,64},{64,80},{80,96},{96,112},{112,128},... | collective-permute-start | bytes 983048 | tf_op jit(solution)/shard_map/ppermute | solution.py:283
  80.9 0.6 collective-permute-done.8.refs_1_
  81.5 5.4 %collective-permute-start.9 = (f32[4,16,1280]{2,1,0:T(8,128)S(1)}, f32[4,16,1280]{2,1,0:T(8,128)}, u32[]{:S(2)}, u32[]{:S(2)}) collective-permute-start(f32[4,16,1280]{2,1,0:T(8,128)S(1)} %collective-permute-done.8.refs_1_), channel_id=1, source_target_pairs={{0,176},{16,0},{32,16},{48,32},{64,48},{80,64},{96,80},{112,96},{1... | collective-permute-start | bytes 983048 | tf_op jit(solution)/shard_map/ppermute | solution.py:283
  86.9 0.1 broadcast_xor_fusion.symmetry_ref
  87.0 1.9 %shard_map.58 = (bf16[2,192,1280]{2,1,0:T(8,128)(2,1)S(1)}, bf16[2,192,1280]{2,1,0:T(8,128)(2,1)S(1)}) custom-call(f32[32,3,40,128]{3,2,1,0:T(8,128)S(1)} %all-to-all-done.1.in_ref), custom_call_target="tpu_custom_call" | custom-call | bytes 3932160 | tf_op jit(solution)/shard_map/pallas_call | solution.py:112
  88.9 0.9 copy-done.1
  89.8 0.9 copy-done.2
  90.8 5.2 %shard_map.60 = (f32[8,2,3,4,512]{4,3,2,1,0:T(4,128)}, f32[8,2,3,4,512]{4,3,2,1,0:T(4,128)}) custom-call(s32[1]{0:T(128)} %bitcast.1.core_ref, bf16[2,192,1280]{2,1,0:T(8,128)(2,1)} %copy-done.1, bf16[2,192,1280]{2,1,0:T(8,128)(2,1)} %copy-done.2, f32[4,16,1280]{2,1,0:T(8,128)S(1)} %collective-permute-done.refs_0_, f32[4,16,1280]{2,1,0:T(8,128)} %copy-done.12, ...), custom_call_target="tpu_custom_call" | custom-call | flops 1509949440 | bytes 8388608 | tf_op jit(solution)/shard_map/pallas_call | solution.py:189
  96.0 3.0 %shard_map.61 = (f32[8,2,3,4,256]{4,3,2,1,0:T(4,128)S(1)}, f32[8,2,3,4,256]{4,3,2,1,0:T(4,128)S(1)}) custom-call(s32[1]{0:T(128)} %bitcast.1.core_ref, bf16[2,192,1280]{2,1,0:T(8,128)(2,1)} %copy-done.1, bf16[2,192,1280]{2,1,0:T(8,128)(2,1)} %copy-done.2, f32[4,16,1280]{2,1,0:T(8,128)S(1)} %collective-permute-done.7.refs_0_, f32[4,16,1280]{2,1,0:T(8,128)} %copy-done.6, ...), custom_call_target="tpu_custom_call" | custom-call | flops 754974720 | bytes 8388608 | tf_op jit(solution)/shard_map/pallas_call | solution.py:189
  99.1 6.0 %collective-permute-start.11 = (f32[8,2,3,4,512]{4,3,2,1,0:T(4,128)S(1)}, f32[8,2,3,4,512]{4,3,2,1,0:T(4,128)S(1)}, u32[]{:S(2)}, u32[]{:S(2)}) collective-permute-start(f32[8,2,3,4,512]{4,3,2,1,0:T(4,128)S(1)} %copy-done.10), channel_id=1, source_target_pairs={{0,1},{1,0},{2,3},{3,2},{4,5},{5,4},{6,7},{7,6},{8,9},{9,8},{10,11... | collective-permute-start | bytes 1179656 | tf_op jit(solution)/shard_map/ppermute | solution.py:324
  105.1 1.9 %collective-permute-start.12 = (f32[8,2,3,4,256]{4,3,2,1,0:T(4,128)S(1)}, f32[8,2,3,4,256]{4,3,2,1,0:T(4,128)S(1)}, u32[]{:S(2)}, u32[]{:S(2)}) collective-permute-start(f32[8,2,3,4,256]{4,3,2,1,0:T(4,128)S(1)} %get-tuple-element.47), channel_id=1, source_target_pairs={{0,1},{1,0},{2,3},{3,2},{4,5},{5,4},{6,7},{7,6},{8,9},{9,8},{10,11... | collective-permute-start | bytes 589832 | tf_op jit(solution)/shard_map/ppermute | solution.py:324
  107.0 1.4 %collective-permute-done.12 = f32[8,2,3,4,256]{4,3,2,1,0:T(4,128)S(1)} collective-permute-done((f32[8,2,3,4,256]{4,3,2,1,0:T(4,128)S(1)}, f32[8,2,3,4,256]{4,3,2,1,0:T(4,128)S(1)}, u32[]{:S(2)}, u32[]{:S(2)}) %collective-permute-start.12) | collective-permute-done | bytes 196640 | tf_op jit(solution)/shard_map/ppermute | solution.py:324
  108.4 0.1 add.15
  108.5 0.1 add.14
  108.6 1.0 pad_maximum_fusion
  109.6 7.1 %all-to-all-start.2 = ((f32[16,3,4,768]{3,2,1,0:T(4,128)}), f32[16,3,4,768]{3,2,1,0:T(4,128)S(1)}, u32[]{:S(2)}, u32[]{:S(2)}) async-start(f32[16,3,4,768]{3,2,1,0:T(4,128)} %bitcast.3), calls=%async_computation.2 | async-start | bytes 1179648 | tf_op jit(solution)/shard_map/all_to_all | solution.py:328
  116.7 17.4 %all-to-all-done.2.parts_ref = f32[16,3,4,768]{3,2,1,0:T(4,128)S(1)} async-done(((f32[16,3,4,768]{3,2,1,0:T(4,128)}), f32[16,3,4,768]{3,2,1,0:T(4,128)S(1)}, u32[]{:S(2)}, u32[]{:S(2)}) %all-to-all-start.2) | async-done | bytes 589856 | tf_op jit(solution)/shard_map/all_to_all | solution.py:328
  134.1 0.9 shard_map.62
  (26 shorter events, 0.1 us)
Async XLA Ops:
  1.8 10.7 %all-to-all-start = ((f32[4,16,1280]{2,1,0:T(8,128)}), f32[4,16,1280]{2,1,0:T(8,128)S(1)}, u32[]{:S(2)}, u32[]{:S(2)}) async-start(f32[4,16,1280]{2,1,0:T(8,128)} %shard_map.56), calls=%async_computation | async-start | bytes 655360 | tf_op jit(solution)/shard_map/all_to_all | solution.py:299
  6.7 1.5 %copy-start = (f32[3,64,4,640]{3,2,1,0:T(4,128)S(1)}, f32[3,64,4,640]{3,2,1,0:T(4,128)}, u32[]{:S(2)}) copy-start(f32[3,64,4,640]{3,2,1,0:T(4,128)} %in_ref.1) | copy-start | bytes 5898244
  12.5 26.3 %collective-permute-start = (f32[4,16,1280]{2,1,0:T(8,128)S(1)}, f32[4,16,1280]{2,1,0:T(8,128)S(1)}, u32[]{:S(2)}, u32[]{:S(2)}) collective-permute-start(f32[4,16,1280]{2,1,0:T(8,128)S(1)} %all-to-all-done.refs_0_), channel_id=1, source_target_pairs={{0,176},{16,0},{32,16},{48,32},{64,48},{80,64},{96,80},{112,96},{1... | collective-permute-start | bytes 983048 | tf_op jit(solution)/shard_map/ppermute | solution.py:283
  27.1 16.6 %collective-permute-start.3 = (f32[4,16,1280]{2,1,0:T(8,128)S(1)}, f32[4,16,1280]{2,1,0:T(8,128)S(1)}, u32[]{:S(2)}, u32[]{:S(2)}) collective-permute-start(f32[4,16,1280]{2,1,0:T(8,128)S(1)} %all-to-all-done.refs_0_), channel_id=1, source_target_pairs={{0,16},{16,32},{32,48},{48,64},{64,80},{80,96},{96,112},{112,128},... | collective-permute-start | bytes 983048 | tf_op jit(solution)/shard_map/ppermute | solution.py:283
  29.1 57.9 %all-to-all-start.1 = ((f32[32,3,40,128]{3,2,1,0:T(8,128)}), f32[32,3,40,128]{3,2,1,0:T(8,128)S(1)}, u32[]{:S(2)}, u32[]{:S(2)}) async-start(f32[32,3,40,128]{3,2,1,0:T(8,128)} %shard_map.55), calls=%async_computation.1 | async-start | bytes 3932160 | tf_op jit(solution)/shard_map/all_to_all | solution.py:310
  38.8 38.7 %copy-start.7 = (s32[12]{0:T(128)S(1)}, s32[12]{0:T(128)}, u32[]{:S(2)}) copy-start(s32[12]{0:T(128)} %param.8) | copy-start | bytes 148
  38.8 38.7 %copy-start.8 = (s32[64]{0:T(128)S(1)}, s32[64]{0:T(128)}, u32[]{:S(2)}) copy-start(s32[64]{0:T(128)} %param.9) | copy-start | bytes 772
  38.9 38.9 %copy-start.9 = (s32[3]{0:T(128)S(1)}, s32[3]{0:T(128)}, u32[]{:S(2)}) copy-start(s32[3]{0:T(128)} %param.7) | copy-start | bytes 40
  38.9 11.7 %collective-permute-start.1 = (f32[4,16,1280]{2,1,0:T(8,128)S(1)}, f32[4,16,1280]{2,1,0:T(8,128)S(1)}, u32[]{:S(2)}, u32[]{:S(2)}) collective-permute-start(f32[4,16,1280]{2,1,0:T(8,128)S(1)} %collective-permute-done.refs_0_), channel_id=1, source_target_pairs={{0,176},{16,0},{32,16},{48,32},{64,48},{80,64},{96,80},{112,96},{1... | collective-permute-start | bytes 983048 | tf_op jit(solution)/shard_map/ppermute | solution.py:283
  43.8 12.3 %copy-start.11 = (f32[4,16,1280]{2,1,0:T(8,128)}, f32[4,16,1280]{2,1,0:T(8,128)S(1)}, u32[]{:S(2)}) copy-start(f32[4,16,1280]{2,1,0:T(8,128)S(1)} %collective-permute-done.3.refs_2_) | copy-start | bytes 983044
  43.8 12.2 %collective-permute-start.4 = (f32[4,16,1280]{2,1,0:T(8,128)S(1)}, f32[4,16,1280]{2,1,0:T(8,128)S(1)}, u32[]{:S(2)}, u32[]{:S(2)}) collective-permute-start(f32[4,16,1280]{2,1,0:T(8,128)S(1)} %collective-permute-done.3.refs_2_), channel_id=1, source_target_pairs={{0,16},{16,32},{32,48},{48,64},{64,80},{80,96},{96,112},{112,128},... | collective-permute-start | bytes 983048 | tf_op jit(solution)/shard_map/ppermute | solution.py:283
  50.6 11.2 %collective-permute-start.2 = (f32[4,16,1280]{2,1,0:T(8,128)S(1)}, f32[4,16,1280]{2,1,0:T(8,128)S(1)}, u32[]{:S(2)}, u32[]{:S(2)}) collective-permute-start(f32[4,16,1280]{2,1,0:T(8,128)S(1)} %collective-permute-done.1.refs_0_), channel_id=1, source_target_pairs={{0,176},{16,0},{32,16},{48,32},{64,48},{80,64},{96,80},{112,96},{1... | collective-permute-start | bytes 983048 | tf_op jit(solution)/shard_map/ppermute | solution.py:283
  56.1 0.7 copy-start.3
  56.8 0.7 copy-start.4
  57.5 11.1 %collective-permute-start.5 = (f32[4,16,1280]{2,1,0:T(8,128)S(1)}, f32[4,16,1280]{2,1,0:T(8,128)}, u32[]{:S(2)}, u32[]{:S(2)}) collective-permute-start(f32[4,16,1280]{2,1,0:T(8,128)S(1)} %collective-permute-done.4.refs_1_), channel_id=1, source_target_pairs={{0,16},{16,32},{32,48},{48,64},{64,80},{80,96},{96,112},{112,128},... | collective-permute-start | bytes 983048 | tf_op jit(solution)/shard_map/ppermute | solution.py:283
  61.8 10.3 %copy-start.12 = (f32[4,16,1280]{2,1,0:T(8,128)}, f32[4,16,1280]{2,1,0:T(8,128)S(1)}, u32[]{:S(2)}) copy-start(f32[4,16,1280]{2,1,0:T(8,128)S(1)} %collective-permute-done.2.refs_1_) | copy-start | bytes 983044
  61.8 10.3 %collective-permute-start.7 = (f32[4,16,1280]{2,1,0:T(8,128)S(1)}, f32[4,16,1280]{2,1,0:T(8,128)S(1)}, u32[]{:S(2)}, u32[]{:S(2)}) collective-permute-start(f32[4,16,1280]{2,1,0:T(8,128)S(1)} %collective-permute-done.2.refs_1_), channel_id=1, source_target_pairs={{0,176},{16,0},{32,16},{48,32},{64,48},{80,64},{96,80},{112,96},{1... | collective-permute-start | bytes 983048 | tf_op jit(solution)/shard_map/ppermute | solution.py:283
  68.6 10.4 %collective-permute-start.6 = (f32[4,16,1280]{2,1,0:T(8,128)}, f32[4,16,1280]{2,1,0:T(8,128)}, u32[]{:S(2)}, u32[]{:S(2)}) collective-permute-start(f32[4,16,1280]{2,1,0:T(8,128)} %collective-permute-done.5.refs_3_), channel_id=1, source_target_pairs={{0,16},{16,32},{32,48},{48,64},{64,80},{80,96},{96,112},{112,128},... | collective-permute-start | bytes 983048 | tf_op jit(solution)/shard_map/ppermute | solution.py:283
  72.2 9.3 %collective-permute-start.8 = (f32[4,16,1280]{2,1,0:T(8,128)S(1)}, f32[4,16,1280]{2,1,0:T(8,128)S(1)}, u32[]{:S(2)}, u32[]{:S(2)}) collective-permute-start(f32[4,16,1280]{2,1,0:T(8,128)S(1)} %collective-permute-done.7.refs_0_), channel_id=1, source_target_pairs={{0,176},{16,0},{32,16},{48,32},{64,48},{80,64},{96,80},{112,96},{1... | collective-permute-start | bytes 983048 | tf_op jit(solution)/shard_map/ppermute | solution.py:283
  79.0 17.0 %collective-permute-start.10 = (f32[4,16,1280]{2,1,0:T(8,128)}, f32[4,16,1280]{2,1,0:T(8,128)}, u32[]{:S(2)}, u32[]{:S(2)}) collective-permute-start(f32[4,16,1280]{2,1,0:T(8,128)} %collective-permute-done.6.refs_4_), channel_id=1, source_target_pairs={{0,16},{16,32},{32,48},{48,64},{64,80},{80,96},{96,112},{112,128},... | collective-permute-start | bytes 983048 | tf_op jit(solution)/shard_map/ppermute | solution.py:283
  81.5 14.5 %copy-start.6 = (f32[4,16,1280]{2,1,0:T(8,128)}, f32[4,16,1280]{2,1,0:T(8,128)S(1)}, u32[]{:S(2)}) copy-start(f32[4,16,1280]{2,1,0:T(8,128)S(1)} %collective-permute-done.8.refs_1_) | copy-start | bytes 983044
  81.5 14.5 %collective-permute-start.9 = (f32[4,16,1280]{2,1,0:T(8,128)S(1)}, f32[4,16,1280]{2,1,0:T(8,128)}, u32[]{:S(2)}, u32[]{:S(2)}) collective-permute-start(f32[4,16,1280]{2,1,0:T(8,128)S(1)} %collective-permute-done.8.refs_1_), channel_id=1, source_target_pairs={{0,176},{16,0},{32,16},{48,32},{64,48},{80,64},{96,80},{112,96},{1... | collective-permute-start | bytes 983048 | tf_op jit(solution)/shard_map/ppermute | solution.py:283
  88.9 1.0 copy-start.1
  89.8 0.9 copy-start.2
  96.0 3.1 %copy-start.10 = (f32[8,2,3,4,512]{4,3,2,1,0:T(4,128)S(1)}, f32[8,2,3,4,512]{4,3,2,1,0:T(4,128)}, u32[]{:S(2)}) copy-start(f32[8,2,3,4,512]{4,3,2,1,0:T(4,128)} %get-tuple-element.45) | copy-start | bytes 1179652
  96.0 12.5 %copy-start.5 = (f32[8,2,3,4,512]{4,3,2,1,0:T(4,128)S(1)}, f32[8,2,3,4,512]{4,3,2,1,0:T(4,128)}, u32[]{:S(2)}) copy-start(f32[8,2,3,4,512]{4,3,2,1,0:T(4,128)} %get-tuple-element.40) | copy-start | bytes 1179652
  99.1 9.4 %collective-permute-start.11 = (f32[8,2,3,4,512]{4,3,2,1,0:T(4,128)S(1)}, f32[8,2,3,4,512]{4,3,2,1,0:T(4,128)S(1)}, u32[]{:S(2)}, u32[]{:S(2)}) collective-permute-start(f32[8,2,3,4,512]{4,3,2,1,0:T(4,128)S(1)} %copy-done.10), channel_id=1, source_target_pairs={{0,1},{1,0},{2,3},{3,2},{4,5},{5,4},{6,7},{7,6},{8,9},{9,8},{10,11... | collective-permute-start | bytes 1179656 | tf_op jit(solution)/shard_map/ppermute | solution.py:324
  105.1 3.3 %collective-permute-start.12 = (f32[8,2,3,4,256]{4,3,2,1,0:T(4,128)S(1)}, f32[8,2,3,4,256]{4,3,2,1,0:T(4,128)S(1)}, u32[]{:S(2)}, u32[]{:S(2)}) collective-permute-start(f32[8,2,3,4,256]{4,3,2,1,0:T(4,128)S(1)} %get-tuple-element.47), channel_id=1, source_target_pairs={{0,1},{1,0},{2,3},{3,2},{4,5},{5,4},{6,7},{7,6},{8,9},{9,8},{10,11... | collective-permute-start | bytes 589832 | tf_op jit(solution)/shard_map/ppermute | solution.py:324
  109.6 24.6 %all-to-all-start.2 = ((f32[16,3,4,768]{3,2,1,0:T(4,128)}), f32[16,3,4,768]{3,2,1,0:T(4,128)S(1)}, u32[]{:S(2)}, u32[]{:S(2)}) async-start(f32[16,3,4,768]{3,2,1,0:T(4,128)} %bitcast.3), calls=%async_computation.2 | async-start | bytes 1179648 | tf_op jit(solution)/shard_map/all_to_all | solution.py:328
